TPU v7x, 32 devices: a whole 2x2x4 slice. The times are simulated.
32 devices in a mesh: head: 4 (over x, core), tok: 8 (over z, y).
Axes of the slice: x: 2, y: 2, z: 4, core: 2. Of those that a mesh axis runs over, the one named last changes fastest.
Arguments:
- query_rows: bfloat16 [2, 2048, 1280], P(None, 'tok', 'head'), may hold values from -6 to 6
- key_rows: bfloat16 [2, 2048, 1280], P(None, 'tok', 'head'), may hold values from -6 to 6
- value_rows: bfloat16 [2, 2048, 1280], P(None, 'tok', 'head'), may hold values from -8 to 8
- token_rates: float32 [2, 4, 2048], P(None, 'head', 'tok'), may hold values from 0.1 to 1
- gate_weight: bfloat16 [4, 320, 320], P('head'), may hold values from -0.3125 to 0.3125
- up_weight: bfloat16 [4, 320, 320], P('head'), may hold values from -0.3125 to 0.3125
- down_weight: bfloat16 [4, 320, 320], P('head'), may hold values from -0.3125 to 0.3125
- step_size: float32 [4], P('head'), may hold values from 0.3 to 1
- branch_gains: float32 [2, 1280], replicated, may hold values from 0.1 to 1.9
Outputs:
- block_output: float32 [2, 8, 256, 1280], P(None, 'tok', 'head')
All inputs are finite; a program needn't handle non-finite values.
Results may differ from a plain program's by a relative error of at most 0.018.
Values may be sent and summed in bfloat16 or wider, within the bound.
No kernel may reach another device: no remote copies, remote signals or barrier semaphores. Data moves between devices by JAX's collectives and lax.ppermute only.
A program may use at most 64 MiB of HBM per device.

v0:
```python
import math

import jax
import jax.numpy as jnp
from jax import lax
from jax.sharding import PartitionSpec as P

SEGMENTS = 2
WINDOW = 256
NS_STEPS = 3


NEWTON_A = 3.4445
NEWTON_B = -4.775
NEWTON_C = 2.0315
NORM_EPS = 1e-06
FROB_EPS = 1e-07


def passed_along(array, axis, by):
    peers = lax.axis_size(axis)
    return lax.ppermute(array, axis, [(i, (i + by) % peers) for i in range(peers)])


def product(left, right):
    return jnp.dot(left, right, preferred_element_type=jnp.float32)


def over_tokens(left, right):
    return lax.dot_general(
        left, right, (((0,), (0,)), ((), ())), preferred_element_type=jnp.float32
    )


def gradients(key_part, value_part, rate_part, weights):
    pre_gate = product(key_part, weights[0])
    pre_up = product(key_part, weights[1])
    sig_gate = jax.nn.sigmoid(pre_gate)
    swish = pre_gate * sig_gate
    hidden = (swish * pre_up).astype(jnp.bfloat16)
    target = (-(rate_part[:, None] * value_part.astype(jnp.float32))).astype(jnp.bfloat16)
    grad_down = over_tokens(hidden, target)
    backward = lax.dot_general(
        target, weights[2], (((1,), (1,)), ((), ())), preferred_element_type=jnp.float32
    )
    d_gate = (backward * pre_up * sig_gate * (1.0 + pre_gate * (1.0 - sig_gate))).astype(
        jnp.bfloat16
    )
    d_up = (backward * swish).astype(jnp.bfloat16)
    return jnp.stack([over_tokens(key_part, d_gate), over_tokens(key_part, d_up), grad_down])


def local_orthogonalize(stacked):
    norms = jnp.sqrt(jnp.sum(stacked * stacked, axis=(1, 2), keepdims=True))
    iterate = (stacked / (norms + FROB_EPS)).astype(jnp.bfloat16)
    for sweep_index in range(NS_STEPS):
        square = jnp.einsum(
            "mij,mkj->mik", iterate, iterate, preferred_element_type=jnp.float32
        ).astype(jnp.bfloat16)
        mixing = (
            NEWTON_B * square.astype(jnp.float32)
            + NEWTON_C
            * jnp.einsum("mij,mjk->mik", square, square, preferred_element_type=jnp.float32)
        ).astype(jnp.bfloat16)
        iterate = (
            NEWTON_A * iterate.astype(jnp.float32)
            + jnp.einsum("mij,mjk->mik", mixing, iterate, preferred_element_type=jnp.float32)
        ).astype(jnp.bfloat16)
    return iterate


def apply_fast(query_part, weights):
    gate = product(query_part, weights[0])
    up_part = product(query_part, weights[1])
    hidden = (jax.nn.silu(gate) * up_part).astype(jnp.bfloat16)
    return product(hidden, weights[2]).astype(jnp.bfloat16)


def window_attention(query_rows, key_rows, value_rows):
    segment_count, row_count, head_width = query_rows.shape
    rim_keys, rim_values = passed_along((key_rows, value_rows), "tok", 1)
    leading = lax.axis_index("tok") == 0

    def previous(array):
        return jnp.concatenate([jnp.zeros_like(array[:1]), array[:-1]], 0)

    rim_keys = jnp.where(leading, previous(rim_keys), rim_keys)
    rim_values = jnp.where(leading, previous(rim_values), rim_values)
    rim_live = jnp.logical_not(leading & (jnp.arange(segment_count) == 0))
    all_keys = jnp.concatenate([rim_keys, key_rows], 1)
    all_values = jnp.concatenate([rim_values, value_rows], 1)
    scores = jnp.einsum(
        "cqd,ckd->cqk", query_rows, all_keys, preferred_element_type=jnp.float32
    ) * (1.0 / math.sqrt(head_width))
    query_index = jnp.arange(row_count)[:, None]
    key_index = jnp.arange(row_count + WINDOW)[None, :]
    band = (key_index > query_index) & (key_index <= query_index + WINDOW)
    live = band[None] & ((key_index >= WINDOW)[None] | rim_live[:, None, None])
    scores = jnp.where(live, scores, -1e30)
    top = jnp.max(scores, axis=-1, keepdims=True)
    expo = jnp.exp(scores - top)
    probs = (expo / jnp.sum(expo, axis=-1, keepdims=True)).astype(jnp.bfloat16)
    return jnp.einsum("cqk,ckd->cqd", probs, all_values, preferred_element_type=jnp.float32).astype(
        jnp.bfloat16
    )


def scaled(branch, total, full_width, gain):
    widened = branch.astype(jnp.float32)
    return widened * lax.rsqrt(total[..., None] / full_width + NORM_EPS) * gain


def on_device(
    query_rows,
    key_rows,
    value_rows,
    token_rates,
    gate_weight,
    up_weight,
    down_weight,
    step_size,
    branch_gains,
):
    segment_count, row_count, head_width = query_rows.shape
    full_width = head_width * lax.axis_size("head")
    attended = window_attention(query_rows, key_rows, value_rows)
    weights = jnp.stack([gate_weight[0], up_weight[0], down_weight[0]])
    outputs = []
    for section_index in range(SEGMENTS):
        grads = gradients(
            key_rows[section_index],
            value_rows[section_index],
            token_rates[section_index, 0],
            weights,
        )
        update = local_orthogonalize(lax.psum(grads, "tok"))
        weights = (weights.astype(jnp.float32) - step_size[0] * update.astype(jnp.float32)).astype(
            jnp.bfloat16
        )
        outputs.append(apply_fast(query_rows[section_index], weights))
    fast = jnp.stack(outputs)
    fast_all = lax.all_to_all(fast, "head", split_axis=1, concat_axis=2, tiled=True)
    attended_all = lax.all_to_all(attended, "head", split_axis=1, concat_axis=2, tiled=True)
    fast_wide = fast_all.astype(jnp.float32)
    attended_wide = attended_all.astype(jnp.float32)
    first_part = scaled(
        fast_all, jnp.sum(fast_wide * fast_wide, axis=-1), full_width, branch_gains[0]
    )
    second_part = scaled(
        attended_all, jnp.sum(attended_wide * attended_wide, axis=-1), full_width, branch_gains[1]
    )
    mixed = first_part + second_part
    return mixed[:, None]


def solution(mesh):
    placed = (
        P(None, "tok", "head"),
        P(None, "tok", "head"),
        P(None, "tok", "head"),
        P(None, "head", "tok"),
        P("head", None, None),
        P("head", None, None),
        P("head", None, None),
        P("head"),
        P(),
    )
    return jax.shard_map(
        on_device,
        mesh=mesh,
        in_specs=placed,
        out_specs=P(None, "tok", "head", None),
        check_vma=False,
    )
```

profile of v0, /device:TPU:0, one launch (start us, length us, event | category | flops | bytes accessed | tf_op | source)
XLA Modules:
  0.0 246.0 jit_solution(1143017144728419544)
XLA Ops:
  7.3 1.3 fusion.53
  8.6 1.3 fusion.55
  11.5 1.2 pad_maximum_fusion
  12.8 3.0 %collective-permute-start.1 = (bf16[2,256,320]{1,2,0:T(8,128)(2,1)S(1)}, bf16[2,256,320]{1,2,0:T(8,128)(2,1)S(1)}, u32[]{:S(2)}, u32[]{:S(2)}) collective-permute-start(bf16[2,256,320]{1,2,0:T(8,128)(2,1)S(1)} %copy-done.12), channel_id=1, source_target_pairs={{0,1},{1,2},{2,3},{3,4},{4,5},{5,6},{6,7},{7,0},{8,9},{9,10},{10,1... | collective-permute-start | bytes 983048 | tf_op jit(solution)/shard_map/ppermute | solution.py:22
  15.8 1.5 collective-permute-start
  20.7 8.2 %collective-permute-done.1 = bf16[2,256,320]{1,2,0:T(8,128)(2,1)S(1)} collective-permute-done((bf16[2,256,320]{1,2,0:T(8,128)(2,1)S(1)}, bf16[2,256,320]{1,2,0:T(8,128)(2,1)S(1)}, u32[]{:S(2)}, u32[]{:S(2)}) %collective-permute-start.1) | collective-permute-done | bytes 327712 | tf_op jit(solution)/shard_map/ppermute | solution.py:22
  28.9 13.2 %collective-permute-done = bf16[2,256,320]{1,2,0:T(8,128)(2,1)S(1)} collective-permute-done((bf16[2,256,320]{1,2,0:T(8,128)(2,1)S(1)}, bf16[2,256,320]{1,2,0:T(8,128)(2,1)S(1)}, u32[]{:S(2)}, u32[]{:S(2)}) %collective-permute-start) | collective-permute-done | bytes 327712 | tf_op jit(solution)/shard_map/ppermute | solution.py:22
  43.1 67.8 %all-reduce.5.cloned.1.call-done = f32[3,320,320]{1,2,0:T(8,128)} async-done(((f32[3,320,320]{1,2,0:T(8,128)}), f32[3,320,320]{1,2,0:T(8,128)}) %all-reduce.5.cloned.1.call-update) | async-done | bytes 1228816 | tf_op jit(solution)/shard_map/psum | solution.py:136
  110.9 1.7 multiply_reduce_fusion.1
  113.6 1.1 add_convert_fusion.10
  115.4 1.1 add_convert_fusion.8
  117.7 1.2 subtract_convert_fusion.1
  121.0 1.2 pad_maximum_fusion.1
  122.3 0.9 copy-done.6
  123.3 1.7 fusion.142
  125.0 1.6 convolution_convert_fusion.6
  126.6 1.1 copy.179
  127.7 3.6 %all-to-all-start.1 = ((bf16[2,256,320]{2,0,1:T(2,128)(2,1)}), bf16[2,256,320]{2,0,1:T(2,128)(2,1)S(1)}, u32[]{:S(2)}, u32[]{:S(2)}) async-start(bf16[2,256,320]{2,0,1:T(2,128)(2,1)} %copy.179), calls=%async_computation.1 | async-start | bytes 786432 | tf_op jit(solution)/shard_map/all_to_all | solution.py:143
  132.0 6.6 %all-to-all-done.1 = bf16[2,256,320]{2,0,1:T(2,128)(2,1)S(1)} async-done(((bf16[2,256,320]{2,0,1:T(2,128)(2,1)}), bf16[2,256,320]{2,0,1:T(2,128)(2,1)S(1)}, u32[]{:S(2)}, u32[]{:S(2)}) %all-to-all-start.1) | async-done | bytes 327712 | tf_op jit(solution)/shard_map/all_to_all | solution.py:143
  139.5 69.0 %all-reduce.7.cloned.1.call-done = f32[3,320,320]{1,2,0:T(8,128)} async-done(((f32[3,320,320]{1,2,0:T(8,128)}), f32[3,320,320]{1,2,0:T(8,128)}) %all-reduce.7.cloned.1.call-update) | async-done | bytes 1228816 | tf_op jit(solution)/shard_map/psum | solution.py:136
  208.4 1.7 multiply_reduce_fusion
  210.4 1.5 convolution_convert_fusion.2
  212.0 2.8 %add_convert_fusion.4 = bf16[3,320,320]{1,2,0:T(8,128)(2,1)S(1)} fusion(bf16[3,320,320]{1,2,0:T(8,128)(2,1)S(1)} %divide_convert_fusion, bf16[3,320,320]{2,1,0:T(8,128)(2,1)} %convolution_convert_fusion.2), kind=kOutput, calls=%fused_computation.9 | convolution fusion | flops 395980800 | bytes 1843200 | tf_op jit(solution)/shard_map/mij,mjk->mik/dot_general | solution.py:67
  214.8 1.5 convolution_convert_fusion.1
  216.3 2.8 %add_convert_fusion.2 = bf16[3,320,320]{1,2,0:T(8,128)(2,1)S(1)} fusion(bf16[3,320,320]{1,2,0:T(8,128)(2,1)S(1)} %add_convert_fusion.4, bf16[3,320,320]{2,1,0:T(8,128)(2,1)} %convolution_convert_fusion.1), kind=kOutput, calls=%fused_computation.7 | convolution fusion | flops 395980800 | bytes 1843200 | tf_op jit(solution)/shard_map/mij,mjk->mik/dot_general | solution.py:67
  219.7 2.0 subtract_convert_fusion
  221.8 1.3 convolution_bitcast_fusion.7
  223.1 1.7 fusion.10
  224.8 1.1 copy.175
  225.9 3.5 %all-to-all-start = ((bf16[2,256,320]{2,0,1:T(2,128)(2,1)}), bf16[2,256,320]{2,0,1:T(2,128)(2,1)S(1)}, u32[]{:S(2)}, u32[]{:S(2)}) async-start(bf16[2,256,320]{2,0,1:T(2,128)(2,1)} %copy.175), calls=%async_computation | async-start | bytes 786432 | tf_op jit(solution)/shard_map/all_to_all | solution.py:142
  230.7 6.1 %all-to-all-done = bf16[2,256,320]{2,0,1:T(2,128)(2,1)S(1)} async-done(((bf16[2,256,320]{2,0,1:T(2,128)(2,1)}), bf16[2,256,320]{2,0,1:T(2,128)(2,1)S(1)}, u32[]{:S(2)}, u32[]{:S(2)}) %all-to-all-start) | async-done | bytes 327712 | tf_op jit(solution)/shard_map/all_to_all | solution.py:142
  238.2 1.0 add_bitcast_fusion
  (85 shorter events, 16.1 us)
Async XLA Ops:
  6.5 3.4 %copy-start.12 = (bf16[2,256,320]{1,2,0:T(8,128)(2,1)S(1)}, bf16[2,256,320]{1,2,0:T(8,128)(2,1)}, u32[]{:S(2)}) copy-start(bf16[2,256,320]{1,2,0:T(8,128)(2,1)} %param.11) | copy-start | bytes 983044
  6.5 3.4 %copy-start.5 = (bf16[1,320,320]{2,1,0:T(8,128)(2,1)S(1)}, bf16[1,320,320]{2,1,0:T(8,128)(2,1)}, u32[]{:S(2)}) copy-start(bf16[1,320,320]{2,1,0:T(8,128)(2,1)} %param.15) | copy-start | bytes 614404
  6.5 104.4 %all-reduce.5.cloned.1.call-start = ((), (), s32[]{:S(2)}) async-start(), calls=%async_computation.2 | async-start | bytes 2949120 | tf_op jit(solution)/shard_map/psum | solution.py:136
  9.9 1.0 copy-start.2
  12.7 4.6 %copy-start.3 = (bf16[1,320,320]{2,1,0:T(8,128)(2,1)S(1)}, bf16[1,320,320]{2,1,0:T(8,128)(2,1)}, u32[]{:S(2)}) copy-start(bf16[1,320,320]{2,1,0:T(8,128)(2,1)} %param.13) | copy-start | bytes 614404
  12.7 5.5 %copy-start.4 = (bf16[1,320,320]{2,1,0:T(8,128)(2,1)S(1)}, bf16[1,320,320]{2,1,0:T(8,128)(2,1)}, u32[]{:S(2)}) copy-start(bf16[1,320,320]{2,1,0:T(8,128)(2,1)} %param.14) | copy-start | bytes 614404
  12.7 195.7 %all-reduce.7.cloned.1.call-start = ((), (), s32[]{:S(2)}) async-start(), calls=%async_computation.3 | async-start | bytes 2949120 | tf_op jit(solution)/shard_map/psum | solution.py:136
  12.8 16.2 %collective-permute-start.1 = (bf16[2,256,320]{1,2,0:T(8,128)(2,1)S(1)}, bf16[2,256,320]{1,2,0:T(8,128)(2,1)S(1)}, u32[]{:S(2)}, u32[]{:S(2)}) collective-permute-start(bf16[2,256,320]{1,2,0:T(8,128)(2,1)S(1)} %copy-done.12), channel_id=1, source_target_pairs={{0,1},{1,2},{2,3},{3,4},{4,5},{5,6},{6,7},{7,0},{8,9},{9,10},{10,1... | collective-permute-start | bytes 983048 | tf_op jit(solution)/shard_map/ppermute | solution.py:22
  15.8 26.3 %collective-permute-start = (bf16[2,256,320]{1,2,0:T(8,128)(2,1)S(1)}, bf16[2,256,320]{1,2,0:T(8,128)(2,1)S(1)}, u32[]{:S(2)}, u32[]{:S(2)}) collective-permute-start(bf16[2,256,320]{1,2,0:T(8,128)(2,1)S(1)} %copy-done.2), channel_id=1, source_target_pairs={{0,1},{1,2},{2,3},{3,4},{4,5},{5,6},{6,7},{7,0},{8,9},{9,10},{10,1... | collective-permute-start | bytes 983048 | tf_op jit(solution)/shard_map/ppermute | solution.py:22
  110.9 1.8 copy-start
  116.5 0.9 copy-start.9
  116.5 1.1 copy-start.10
  116.5 1.2 copy-start.11
  118.9 1.0 copy-start.13
  122.3 1.0 copy-start.6
  122.3 1.1 copy-start.8
  123.3 1.7 copy-start.7
  126.6 4.8 %copy-start.16 = (f32[2,1280]{1,0:T(2,128)S(1)}, f32[2,1280]{1,0:T(2,128)}, u32[]{:S(2)}) copy-start(f32[2,1280]{1,0:T(2,128)} %param.17) | copy-start | bytes 30724
  127.7 10.9 %all-to-all-start.1 = ((bf16[2,256,320]{2,0,1:T(2,128)(2,1)}), bf16[2,256,320]{2,0,1:T(2,128)(2,1)S(1)}, u32[]{:S(2)}, u32[]{:S(2)}) async-start(bf16[2,256,320]{2,0,1:T(2,128)(2,1)} %copy.179), calls=%async_computation.1 | async-start | bytes 786432 | tf_op jit(solution)/shard_map/all_to_all | solution.py:143
  208.4 1.8 copy-start.1
  225.9 10.9 %all-to-all-start = ((bf16[2,256,320]{2,0,1:T(2,128)(2,1)}), bf16[2,256,320]{2,0,1:T(2,128)(2,1)S(1)}, u32[]{:S(2)}, u32[]{:S(2)}) async-start(bf16[2,256,320]{2,0,1:T(2,128)(2,1)} %copy.175), calls=%async_computation | async-start | bytes 786432 | tf_op jit(solution)/shard_map/all_to_all | solution.py:142
  236.9 1.3 copy-start.14
  236.9 1.3 copy-start.15
Sparse Core Ops, SparseCore 0:
  12.8 98.0 all-reduce.4
  122.4 85.9 all-reduce.6
where the time goes:
time: 247 us; the launch traced here: 246 us
  waiting for transfers between devices  171 us (69%)
  matrix products  29.2 us (12%)
  between operations  14.4 us (6%)
  starting transfers between devices  11.7 us (5%)
  local copies, waits for them, and re-layouts  10.8 us (4%)
  other arithmetic  8.92 us (4%)
    psum x2, waiting for transfers between devices, on_device(): update = local_orthogonalize(lax.psum(grads, 'tok'))  137 us
    ppermute x2, waiting for transfers between devices, passed_along(): lax.ppermute(array, axis, [(i, (i + by) % peers) for i in range(peers)])  21.4 us
    dot_general x6, matrix products, local_orthogonalize(): jnp.einsum('mij,mjk->mik', mixing, iterate, preferred_element_type=jnp.fl...  11 us
    dot_general x8, matrix products, product(): return jnp.dot(left, right, preferred_element_type=jnp.float32)  6.92 us
    all_to_all x1, waiting for transfers between devices, on_device(): lax.all_to_all(attended, 'head', split_axis=1, concat_axis=2, tiled=True)  6.6 us
    all_to_all x1, waiting for transfers between devices, on_device(): lax.all_to_all(fast, 'head', split_axis=1, concat_axis=2, tiled=True)  6.13 us
    dot_general x6, matrix products, local_orthogonalize(): jnp.einsum('mij,mkj->mik', iterate, iterate, preferred_element_type=jnp.f...  5.74 us
    unnamed x37, local copies, waits for them, and re-layouts  5.1 us
  transfers between devices with their start and end apart: 6, of which 6 were waited for; matrix products, arithmetic and copies ran while one was open for 4% of the time, Pallas kernels for 0%

commit v1 on v0

v1 whole, which is shorter than its diff:
```python
import math

import jax
import jax.numpy as jnp
from jax import lax
from jax.sharding import PartitionSpec as P

WINDOW = 256
NS_STEPS = 3
NEWTON_A = 3.4445
NEWTON_B = -4.775
NEWTON_C = 2.0315
NORM_EPS = 1e-06
FROB_EPS = 1e-07
BOTH = ("head", "tok")
RATE_ROWS = 16


def moved(array, heads, toks, where):
    pairs = []
    for h in range(heads):
        for t in range(toks):
            to_h, to_t = where(h, t)
            pairs.append((h * toks + t, to_h * toks + to_t))
    return lax.ppermute(array, BOTH, pairs)


def product(left, right):
    return jnp.dot(left, right, preferred_element_type=jnp.float32)


def over_tokens(left, right):
    return lax.dot_general(
        left, right, (((0,), (0,)), ((), ())), preferred_element_type=jnp.float32
    )


def gradients(keys, values, rates, weights):
    pre_gate = product(keys, weights[0])
    pre_up = product(keys, weights[1])
    sig_gate = jax.nn.sigmoid(pre_gate)
    swish = pre_gate * sig_gate
    hidden = (swish * pre_up).astype(jnp.bfloat16)
    target = (-(rates[:, None] * values.astype(jnp.float32))).astype(jnp.bfloat16)
    grad_down = over_tokens(hidden, target)
    backward = lax.dot_general(
        target, weights[2], (((1,), (1,)), ((), ())), preferred_element_type=jnp.float32
    )
    d_gate = (backward * pre_up * sig_gate * (1.0 + pre_gate * (1.0 - sig_gate))).astype(
        jnp.bfloat16
    )
    d_up = (backward * swish).astype(jnp.bfloat16)
    return jnp.stack([over_tokens(keys, d_gate), over_tokens(keys, d_up), grad_down])


def local_orthogonalize(stacked):
    norms = jnp.sqrt(jnp.sum(stacked * stacked, axis=(1, 2), keepdims=True))
    iterate = (stacked / (norms + FROB_EPS)).astype(jnp.bfloat16)
    for _ in range(NS_STEPS):
        square = jnp.einsum(
            "mij,mkj->mik", iterate, iterate, preferred_element_type=jnp.float32
        ).astype(jnp.bfloat16)
        mixing = (
            NEWTON_B * square.astype(jnp.float32)
            + NEWTON_C
            * jnp.einsum("mij,mjk->mik", square, square, preferred_element_type=jnp.float32)
        ).astype(jnp.bfloat16)
        iterate = (
            NEWTON_A * iterate.astype(jnp.float32)
            + jnp.einsum("mij,mjk->mik", mixing, iterate, preferred_element_type=jnp.float32)
        ).astype(jnp.bfloat16)
    return iterate


def apply_fast(query_part, weights):
    gate = product(query_part, weights[0])
    up_part = product(query_part, weights[1])
    hidden = (jax.nn.silu(gate) * up_part).astype(jnp.bfloat16)
    return product(hidden, weights[2]).astype(jnp.bfloat16)


def attention(query, prev, own, prev_live):
    rows, width = query.shape
    keys = jnp.concatenate([prev[:rows, :width], own[:rows, :width]], 0)
    values = jnp.concatenate([prev[:rows, width:], own[:rows, width:]], 0)
    scores = lax.dot_general(
        query, keys, (((1,), (1,)), ((), ())), preferred_element_type=jnp.float32
    ) * (1.0 / math.sqrt(width))
    query_index = jnp.arange(rows)[:, None]
    key_index = jnp.arange(2 * rows)[None, :]
    band = (key_index > query_index) & (key_index <= query_index + WINDOW)
    live = band & ((key_index >= WINDOW) | prev_live)
    scores = jnp.where(live, scores, -1e30)
    top = jnp.max(scores, axis=-1, keepdims=True)
    expo = jnp.exp(scores - top)
    probs = (expo / jnp.sum(expo, axis=-1, keepdims=True)).astype(jnp.bfloat16)
    return product(probs, values).astype(jnp.bfloat16)


def packed_block(keys, values, rates):
    width = keys.shape[1]
    high = lax.reduce_precision(rates, 8, 7)
    middle = lax.reduce_precision(rates - high, 8, 7)
    low = lax.reduce_precision(rates - high - middle, 8, 7)
    terms = jnp.stack([high, middle, low]).astype(jnp.bfloat16)
    terms = jnp.pad(terms, ((0, RATE_ROWS - 3), (0, 2 * width - rates.shape[0])))
    return jnp.concatenate([jnp.concatenate([keys, values], 1), terms], 0)


def block_rates(block, rows):
    terms = block[rows : rows + 3, :rows].astype(jnp.float32)
    return terms[0] + terms[1] + terms[2]


def on_device(
    query_rows,
    key_rows,
    value_rows,
    token_rates,
    gate_weight,
    up_weight,
    down_weight,
    step_size,
    branch_gains,
    *,
    heads,
    toks,
):
    segments, rows, width = query_rows.shape
    half = toks // 2
    full_width = width * heads

    def regroup(h, t):
        return h - h % 2 + t // half, (h % 2) * half + t % half

    def other_core(h, t):
        return h ^ 1, t

    def send(array, where):
        return moved(array, heads, toks, where)

    blocks = [
        packed_block(key_rows[s], value_rows[s], token_rates[s, 0]) for s in range(segments)
    ]
    own = [send(block, regroup) for block in blocks]
    queries = send(query_rows, regroup)
    weights = jnp.stack([gate_weight[0], up_weight[0], down_weight[0]])
    core = lax.axis_index("head") % 2
    tok = lax.axis_index("tok")
    group = tok // half
    place = tok % half
    other_weights = send(weights, other_core)
    weights = jnp.where(core == group, weights, other_weights)
    steps = step_size[0]
    steps = jnp.where(core == group, steps, send(step_size, other_core)[0])

    outputs, attended = [], []
    held = []
    for s in range(segments):
        here = [own[s]]
        for mask in range(1, half):
            here.append(send(own[s], lambda h, t, mask=mask: (h, t ^ mask)))
        there = [send(block, other_core) for block in here]
        held.append((here, there))

    for s in range(segments):
        here, there = held[s]
        everything = here + there
        keys = jnp.concatenate([b[:rows, :width] for b in everything], 0)
        values = jnp.concatenate([b[:rows, width:] for b in everything], 0)
        rates = jnp.concatenate([block_rates(b, rows) for b in everything], 0)
        update = local_orthogonalize(gradients(keys, values, rates, weights))
        weights = (weights.astype(jnp.float32) - steps * update.astype(jnp.float32)).astype(
            jnp.bfloat16
        )
        outputs.append(apply_fast(queries[s], weights))
        prev = there[half - 1]
        if s > 0:
            prev = jnp.where(core == 0, held[s - 1][1][half - 1], prev)
        mask = 1
        while mask < half:
            prev = jnp.where((place ^ (place - 1)) == mask, here[mask], prev)
            mask = 2 * mask + 1
        prev_live = (s > 0) | (core > 0) | (place > 0)
        attended.append(attention(queries[s], prev, own[s], prev_live))

    share = rows // heads
    head_of = (lax.axis_index("head") - core) + group

    def spread(array):
        parts = array.reshape(heads, share, array.shape[-1])
        got = []
        for shift in range(heads):
            to = (head_of + shift) % heads

            def where(h, t, shift=shift):
                mine = h - h % 2 + t // half
                return (mine + shift) % heads, (h % 2) * half + t % half

            got.append(send(lax.dynamic_index_in_dim(parts, to, 0, False), where))
        stacked = jnp.stack(got)
        me = lax.axis_index("head")
        return jnp.concatenate(
            [
                lax.dynamic_index_in_dim(stacked, (me - j) % heads, 0, False)
                for j in range(heads)
            ],
            -1,
        )

    def normed(branch, gain):
        wide = branch.astype(jnp.float32)
        total = jnp.sum(wide * wide, axis=-1, keepdims=True)
        return wide * lax.rsqrt(total / full_width + NORM_EPS) * gain

    mixed = []
    for s in range(segments):
        mixed.append(
            normed(spread(outputs[s]), branch_gains[0])
            + normed(spread(attended[s]), branch_gains[1])
        )
    return jnp.stack(mixed)[:, None]


def solution(mesh):
    placed = (
        P(None, "tok", "head"),
        P(None, "tok", "head"),
        P(None, "tok", "head"),
        P(None, "head", "tok"),
        P("head", None, None),
        P("head", None, None),
        P("head", None, None),
        P("head"),
        P(),
    )
    heads, toks = mesh.shape["head"], mesh.shape["tok"]

    def program(*arrays):
        return on_device(*arrays, heads=heads, toks=toks)

    return jax.shard_map(
        program,
        mesh=mesh,
        in_specs=placed,
        out_specs=P(None, "tok", "head", None),
        check_vma=False,
    )
```

time: 247 us -> 191 us (0.77)
  waiting for transfers between devices: 171 us -> 28 us
  starting transfers between devices: 11.7 us -> 75.4 us
  matrix products: 29.2 us -> 42.1 us
  local copies, waits for them, and re-layouts: 10.8 us -> 22.9 us
  between operations: 14.4 us -> 2.47 us
  other arithmetic: 8.92 us -> 17.4 us
    psum x2 -> x0, waiting for transfers between devices: 137 us -> none  [on_device(): update = local_orthogonalize(lax.psum(grads, 'tok'))]
    ppermute x2 -> x35, starting transfers between devices: 4.54 us -> 75.4 us  [moved(): return lax.ppermute(array, BOTH, pairs)]
    all_to_all x2 -> x0, waiting for transfers between devices: 12.7 us -> none  [the longest x1 6.6 us: on_device(): lax.all_to_all(attended, 'head', split_axis=1, concat_axis=2, tiled=True)]
    unnamed x37 -> x83, local copies, waits for them, and re-layouts: 5.1 us -> 12.9 us
    all_to_all x2 -> x0, starting transfers between devices: 7.1 us -> none  [the longest x1 3.64 us: on_device(): lax.all_to_all(attended, 'head', split_axis=1, concat_axis=2, tiled=True)]
    convert_element_type x2 -> x16, other arithmetic: 0.11 us -> 6.91 us  [block_rates(): terms = block[rows:rows + 3, :rows].astype(jnp.float32)]
    ppermute x2 -> x35, waiting for transfers between devices: 21.4 us -> 28 us  [moved(): return lax.ppermute(array, BOTH, pairs)]
    dot_general x6, matrix products: 1.78 us -> 7.98 us  [over_tokens(): lax.dot_general(left, right, (((0,), (0,)), ((), ())), preferred_element_...]
  transfers between devices with their start and end apart: 6 -> 35, of which waited for: 6 -> 6; matrix products, arithmetic and copies ran while one was open for 4% -> 39% of each run, Pallas kernels for 0% -> 0%
where the time goes in v1:
time: 191 us; the launch traced here: 188 us
  starting transfers between devices  75.4 us (39%)
  matrix products  42.1 us (22%)
  waiting for transfers between devices  28 us (15%)
  local copies, waits for them, and re-layouts  22.9 us (12%)
  other arithmetic  17.4 us (9%)
  between operations  2.47 us (1%)
    ppermute x35, starting transfers between devices, moved(): return lax.ppermute(array, BOTH, pairs)  75.4 us
    ppermute x35, waiting for transfers between devices, moved(): return lax.ppermute(array, BOTH, pairs)  28 us
    unnamed x83, local copies, waits for them, and re-layouts  12.9 us
    dot_general x6, matrix products, local_orthogonalize(): jnp.einsum('mij,mjk->mik', mixing, iterate, preferred_element_type=jnp.fl...  11.8 us
    dot_general x10, matrix products, product(): return jnp.dot(left, right, preferred_element_type=jnp.float32)  10.4 us
    dot_general x6, matrix products, over_tokens(): lax.dot_general(left, right, (((0,), (0,)), ((), ())), preferred_element_...  7.98 us
    convert_element_type x16, other arithmetic, block_rates(): terms = block[rows:rows + 3, :rows].astype(jnp.float32)  6.91 us
    dot_general x6, matrix products, local_orthogonalize(): jnp.einsum('mij,mkj->mik', iterate, iterate, preferred_element_type=jnp.f...  6.37 us
  transfers between devices with their start and end apart: 35, of which 6 were waited for; matrix products, arithmetic and copies ran while one was open for 39% of the time, Pallas kernels for 0%

profile of v1, /device:TPU:0, one launch (start us, length us, event | category | flops | bytes accessed | tf_op | source)
XLA Modules:
  0.0 188.2 jit_solution(13674205091616242580)
XLA Ops:
  2.2 1.6 collective-permute-start.2
  5.4 3.9 %collective-permute-start.10 = (bf16[2,256,320]{1,2,0:T(8,128)(2,1)}, bf16[2,256,320]{1,2,0:T(8,128)(2,1)}, u32[]{:S(2)}, u32[]{:S(2)}) collective-permute-start(bf16[2,256,320]{1,2,0:T(8,128)(2,1)} %param.9), channel_id=1, source_target_pairs={{0,0},{1,1},{2,2},{3,3},{4,8},{5,9},{6,10},{7,11},{8,4},{9,5},{10,... | collective-permute-start | bytes 983048 | tf_op jit(solution)/shard_map/ppermute | solution.py:25
  9.4 5.9 %collective-permute-start = (bf16[3,320,320]{2,1,0:T(8,128)(2,1)S(1)}, bf16[3,320,320]{2,1,0:T(8,128)(2,1)S(1)}, u32[]{:S(2)}, u32[]{:S(2)}) collective-permute-start(bf16[3,320,320]{2,1,0:T(8,128)(2,1)S(1)} %constant_dynamic-update-slice_fusion), channel_id=1, source_target_pairs={{0,8},{1,9},{2,10},{3,11},{4,12},{5,13},{6,14},{7,15},{8,0},{9,1},... | collective-permute-start | bytes 1843208 | tf_op jit(solution)/shard_map/ppermute | solution.py:25
  20.1 2.6 %collective-permute-start.5 = (bf16[272,640]{0,1:T(8,128)(2,1)}, bf16[272,640]{0,1:T(8,128)(2,1)S(1)}, u32[]{:S(2)}, u32[]{:S(2)}) collective-permute-start(bf16[272,640]{0,1:T(8,128)(2,1)} %collective-permute-done.2), channel_id=1, source_target_pairs={{0,3},{1,2},{2,1},{3,0},{4,7},{5,6},{6,5},{7,4},{8,11},{9,10},{10,... | collective-permute-start | bytes 1044488 | tf_op jit(solution)/shard_map/ppermute | solution.py:25
  24.6 1.8 fusion.111
  26.4 1.8 constant_dynamic-update-slice_fusion.8
  28.9 3.7 %collective-permute-done.3 = bf16[272,640]{0,1:T(8,128)(2,1)S(1)} collective-permute-done((bf16[272,640]{0,1:T(8,128)(2,1)}, bf16[272,640]{0,1:T(8,128)(2,1)S(1)}, u32[]{:S(2)}, u32[]{:S(2)}) %collective-permute-start.3) | collective-permute-done | bytes 348192 | tf_op jit(solution)/shard_map/ppermute | solution.py:25
  32.6 22.4 %collective-permute-start.4 = (bf16[272,640]{0,1:T(8,128)(2,1)}, bf16[272,640]{0,1:T(8,128)(2,1)S(1)}, u32[]{:S(2)}, u32[]{:S(2)}) collective-permute-start(bf16[272,640]{0,1:T(8,128)(2,1)} %collective-permute-done.2), channel_id=1, source_target_pairs={{0,2},{1,3},{2,0},{3,1},{4,6},{5,7},{6,4},{7,5},{8,10},{9,11},{10,... | collective-permute-start | bytes 1044488 | tf_op jit(solution)/shard_map/ppermute | solution.py:25
  55.2 8.5 %collective-permute-done.4 = bf16[272,640]{0,1:T(8,128)(2,1)S(1)} collective-permute-done((bf16[272,640]{0,1:T(8,128)(2,1)}, bf16[272,640]{0,1:T(8,128)(2,1)S(1)}, u32[]{:S(2)}, u32[]{:S(2)}) %collective-permute-start.4) | collective-permute-done | bytes 348192 | tf_op jit(solution)/shard_map/ppermute | solution.py:25
  63.7 7.9 %collective-permute-start.6 = (bf16[272,640]{0,1:T(8,128)(2,1)}, bf16[272,640]{0,1:T(8,128)(2,1)S(1)}, u32[]{:S(2)}, u32[]{:S(2)}) collective-permute-start(bf16[272,640]{0,1:T(8,128)(2,1)} %collective-permute-done.2), channel_id=1, source_target_pairs={{0,8},{1,9},{2,10},{3,11},{4,12},{5,13},{6,14},{7,15},{8,0},{9,1},... | collective-permute-start | bytes 1044488 | tf_op jit(solution)/shard_map/ppermute | solution.py:25
  75.0 10.4 %collective-permute-done.21 = bf16[272,640]{0,1:T(8,128)(2,1)} collective-permute-done((bf16[272,640]{0,1:T(8,128)(2,1)}, bf16[272,640]{0,1:T(8,128)(2,1)}, u32[]{:S(2)}, u32[]{:S(2)}) %collective-permute-start.21) | collective-permute-done | bytes 348192 | tf_op jit(solution)/shard_map/ppermute | solution.py:25
  89.1 1.7 slice_dynamic-update-slice_fusion.6
  90.9 1.8 slice_dynamic-update-slice_fusion.5
  92.6 1.7 slice_dynamic-update-slice_fusion.4
  104.5 2.8 %add_convert_fusion.10 = bf16[3,320,320]{2,1,0:T(8,128)(2,1)S(1)} fusion(bf16[3,320,320]{2,1,0:T(8,128)(2,1)S(1)} %divide_convert_fusion.1, bf16[3,320,320]{2,1,0:T(8,128)(2,1)} %convolution_convert_fusion.5), kind=kOutput, calls=%fused_computation.28 | convolution fusion | flops 395980800 | bytes 1843200 | tf_op jit(solution)/shard_map/mij,mjk->mik/dot_general | solution.py:70
  108.7 3.0 %add_convert_fusion.8 = bf16[3,320,320]{2,1,0:T(8,128)(2,1)S(1)} fusion(bf16[3,320,320]{2,1,0:T(8,128)(2,1)S(1)} %add_convert_fusion.10, bf16[3,320,320]{2,1,0:T(8,128)(2,1)} %convolution_convert_fusion.4), kind=kOutput, calls=%fused_computation.26 | convolution fusion | flops 395980800 | bytes 1843200 | tf_op jit(solution)/shard_map/mij,mjk->mik/dot_general | solution.py:70
  111.7 1.7 slice_dynamic-update-slice_fusion.2
  115.0 1.7 slice_dynamic-update-slice_fusion.1
  116.6 2.8 %subtract_convert_fusion.1 = bf16[3,320,320]{2,1,0:T(8,128)(2,1)S(1)} fusion(bf16[3,320,320]{2,1,0:T(8,128)(2,1)S(1)} %broadcast_select_fusion, bf16[3,320,320]{2,1,0:T(8,128)(2,1)S(1)} %add_convert_fusion.8, bf16[3,320,320]{2,1,0:T(8,128)(2,1)} %convolution_convert_fusion.3, f32[]{:T(128)S(6)} %select_n.195), kind=kOutput, calls=%fused_computation.23 | convolution fusion | flops 397516800 | bytes 2457604 | tf_op jit(solution)/shard_map/mij,mjk->mik/dot_general | solution.py:70
  119.5 2.0 %slice_dynamic-update-slice_fusion = (bf16[2048,320]{0,1:T(8,128)(2,1)}, bf16[2048,320]{0,1:T(8,128)(2,1)S(1)}) fusion(bf16[2048,320]{0,1:T(8,128)(2,1)} %get-tuple-element.17, bf16[272,640]{0,1:T(8,128)(2,1)} %collective-permute-done.26, bf16[2048,320]{0,1:T(8,128)(2,1)S(1)} %get-tuple-element.18), kind=kLoop, calls=%fused_computation.138 | loop fusion | bytes 655360 | tf_op jit(solution)/shard_map/concatenate | solution.py:170
  126.5 2.2 %fusion.19 = f32[2048,320]{0,1:T(8,128)S(1)} fusion(bf16[2048,320]{0,1:T(8,128)(2,1)} %get-tuple-element.15, f32[2048]{0:T(1024)S(1)} %constant_dynamic-update-slice_fusion.10, bf16[3,320,320]{2,1,0:T(8,128)(2,1)S(1)} %subtract_convert_fusion.1), kind=kOutput, calls=%fused_computation.65 | convolution fusion | flops 422051840 | bytes 4186112 | tf_op jit(solution)/shard_map/dot_general | solution.py:46
  128.7 2.4 %fusion.14 = f32[1,320,320]{2,1,0:T(8,128)S(1)} fusion(f32[2048,320]{0,1:T(8,128)S(1)} %fusion.62, bf16[2048,320]{0,1:T(8,128)(2,1)} %get-tuple-element.15, f32[2048]{0:T(1024)S(1)} %constant_dynamic-update-slice_fusion.10, f32[2048,320]{0,1:T(8,128)S(1)} %fusion.61), kind=kOutput, calls=%fused_computation.52 | convolution fusion | flops 425984000 | bytes 6971392 | tf_op jit(solution)/shard_map/dot_general | solution.py:33
  138.5 1.7 collective-permute-start.18
  140.8 1.7 collective-permute-start.16
  142.5 2.1 %collective-permute-start.15 = (bf16[64,320]{1,0:T(8,128)(2,1)}, bf16[64,320]{1,0:T(8,128)(2,1)}, u32[]{:S(2)}, u32[]{:S(2)}) collective-permute-start(bf16[64,320]{1,0:T(8,128)(2,1)} %get-tuple-element.65), channel_id=1, source_target_pairs={{0,0},{1,1},{2,2},{3,3},{4,8},{5,9},{6,10},{7,11},{8,4},{9,5},{10,... | collective-permute-start | bytes 122888 | tf_op jit(solution)/shard_map/ppermute | solution.py:25
  145.8 1.6 convolution_convert_fusion.9
  148.2 3.2 %collective-permute-start.14 = (bf16[64,320]{1,0:T(8,128)(2,1)}, bf16[64,320]{1,0:T(8,128)(2,1)}, u32[]{:S(2)}, u32[]{:S(2)}) collective-permute-start(bf16[64,320]{1,0:T(8,128)(2,1)} %get-tuple-element.58), channel_id=1, source_target_pairs={{0,24},{1,25},{2,26},{3,27},{4,0},{5,1},{6,2},{7,3},{8,28},{9,29},... | collective-permute-start | bytes 122888 | tf_op jit(solution)/shard_map/ppermute | solution.py:25
  161.5 1.6 convolution_convert_fusion.8
  164.7 5.4 %collective-permute-start.34 = (bf16[64,320]{1,0:T(8,128)(2,1)S(1)}, bf16[64,320]{1,0:T(8,128)(2,1)S(1)}, u32[]{:S(2)}, u32[]{:S(2)}) collective-permute-start(bf16[64,320]{1,0:T(8,128)(2,1)S(1)} %copy-done.19), channel_id=1, source_target_pairs={{0,24},{1,25},{2,26},{3,27},{4,0},{5,1},{6,2},{7,3},{8,28},{9,29},... | collective-permute-start | bytes 122888 | tf_op jit(solution)/shard_map/ppermute | solution.py:25
  173.2 5.4 %collective-permute-start.30 = (bf16[64,320]{1,0:T(8,128)(2,1)S(1)}, bf16[64,320]{1,0:T(8,128)(2,1)S(1)}, u32[]{:S(2)}, u32[]{:S(2)}) collective-permute-start(bf16[64,320]{1,0:T(8,128)(2,1)S(1)} %get-tuple-element.74), channel_id=1, source_target_pairs={{0,24},{1,25},{2,26},{3,27},{4,0},{5,1},{6,2},{7,3},{8,28},{9,29},... | collective-permute-start | bytes 122888 | tf_op jit(solution)/shard_map/ppermute | solution.py:25
  182.2 2.6 %collective-permute-done.29 = bf16[64,320]{1,0:T(8,128)(2,1)S(1)} collective-permute-done((bf16[64,320]{1,0:T(8,128)(2,1)S(1)}, bf16[64,320]{1,0:T(8,128)(2,1)S(1)}, u32[]{:S(2)}, u32[]{:S(2)}) %collective-permute-start.29) | collective-permute-done | bytes 40992 | tf_op jit(solution)/shard_map/ppermute | solution.py:25
  184.8 1.8 collective-permute-done.28
  (247 shorter events, 64.6 us)
Async XLA Ops:
  2.2 15.7 %collective-permute-start.2 = (bf16[272,640]{0,1:T(8,128)(2,1)S(1)}, bf16[272,640]{0,1:T(8,128)(2,1)}, u32[]{:S(2)}, u32[]{:S(2)}) collective-permute-start(bf16[272,640]{0,1:T(8,128)(2,1)S(1)} %fusion.35), channel_id=1, source_target_pairs={{0,0},{1,1},{2,2},{3,3},{4,8},{5,9},{6,10},{7,11},{8,4},{9,5},{10,... | collective-permute-start | bytes 1044488 | tf_op jit(solution)/shard_map/ppermute | solution.py:25
  4.0 15.0 %collective-permute-start.19 = (bf16[272,640]{0,1:T(8,128)(2,1)S(1)}, bf16[272,640]{0,1:T(8,128)(2,1)}, u32[]{:S(2)}, u32[]{:S(2)}) collective-permute-start(bf16[272,640]{0,1:T(8,128)(2,1)S(1)} %fusion.36), channel_id=1, source_target_pairs={{0,0},{1,1},{2,2},{3,3},{4,8},{5,9},{6,10},{7,11},{8,4},{9,5},{10,... | collective-permute-start | bytes 1044488 | tf_op jit(solution)/shard_map/ppermute | solution.py:25
  5.4 128.4 %collective-permute-start.10 = (bf16[2,256,320]{1,2,0:T(8,128)(2,1)}, bf16[2,256,320]{1,2,0:T(8,128)(2,1)}, u32[]{:S(2)}, u32[]{:S(2)}) collective-permute-start(bf16[2,256,320]{1,2,0:T(8,128)(2,1)} %param.9), channel_id=1, source_target_pairs={{0,0},{1,1},{2,2},{3,3},{4,8},{5,9},{6,10},{7,11},{8,4},{9,5},{10,... | collective-permute-start | bytes 983048 | tf_op jit(solution)/shard_map/ppermute | solution.py:25
  9.4 18.8 %collective-permute-start = (bf16[3,320,320]{2,1,0:T(8,128)(2,1)S(1)}, bf16[3,320,320]{2,1,0:T(8,128)(2,1)S(1)}, u32[]{:S(2)}, u32[]{:S(2)}) collective-permute-start(bf16[3,320,320]{2,1,0:T(8,128)(2,1)S(1)} %constant_dynamic-update-slice_fusion), channel_id=1, source_target_pairs={{0,8},{1,9},{2,10},{3,11},{4,12},{5,13},{6,14},{7,15},{8,0},{9,1},... | collective-permute-start | bytes 1843208 | tf_op jit(solution)/shard_map/ppermute | solution.py:25
  20.1 51.8 %collective-permute-start.5 = (bf16[272,640]{0,1:T(8,128)(2,1)}, bf16[272,640]{0,1:T(8,128)(2,1)S(1)}, u32[]{:S(2)}, u32[]{:S(2)}) collective-permute-start(bf16[272,640]{0,1:T(8,128)(2,1)} %collective-permute-done.2), channel_id=1, source_target_pairs={{0,3},{1,2},{2,1},{3,0},{4,7},{5,6},{6,5},{7,4},{8,11},{9,10},{10,... | collective-permute-start | bytes 1044488 | tf_op jit(solution)/shard_map/ppermute | solution.py:25
  22.7 9.9 %collective-permute-start.3 = (bf16[272,640]{0,1:T(8,128)(2,1)}, bf16[272,640]{0,1:T(8,128)(2,1)S(1)}, u32[]{:S(2)}, u32[]{:S(2)}) collective-permute-start(bf16[272,640]{0,1:T(8,128)(2,1)} %collective-permute-done.2), channel_id=1, source_target_pairs={{0,1},{1,0},{2,3},{3,2},{4,5},{5,4},{6,7},{7,6},{8,9},{9,8},{10,11... | collective-permute-start | bytes 1044488 | tf_op jit(solution)/shard_map/ppermute | solution.py:25
  23.2 63.3 %collective-permute-start.22 = (bf16[272,640]{0,1:T(8,128)(2,1)}, bf16[272,640]{0,1:T(8,128)(2,1)}, u32[]{:S(2)}, u32[]{:S(2)}) collective-permute-start(bf16[272,640]{0,1:T(8,128)(2,1)} %collective-permute-done.19), channel_id=1, source_target_pairs={{0,3},{1,2},{2,1},{3,0},{4,7},{5,6},{6,5},{7,4},{8,11},{9,10},{10,... | collective-permute-start | bytes 1044488 | tf_op jit(solution)/shard_map/ppermute | solution.py:25
  28.2 45.7 %collective-permute-start.20 = (bf16[272,640]{0,1:T(8,128)(2,1)}, bf16[272,640]{0,1:T(8,128)(2,1)}, u32[]{:S(2)}, u32[]{:S(2)}) collective-permute-start(bf16[272,640]{0,1:T(8,128)(2,1)} %collective-permute-done.19), channel_id=1, source_target_pairs={{0,1},{1,0},{2,3},{3,2},{4,5},{5,4},{6,7},{7,6},{8,9},{9,8},{10,11... | collective-permute-start | bytes 1044488 | tf_op jit(solution)/shard_map/ppermute | solution.py:25
  32.6 31.1 %collective-permute-start.4 = (bf16[272,640]{0,1:T(8,128)(2,1)}, bf16[272,640]{0,1:T(8,128)(2,1)S(1)}, u32[]{:S(2)}, u32[]{:S(2)}) collective-permute-start(bf16[272,640]{0,1:T(8,128)(2,1)} %collective-permute-done.2), channel_id=1, source_target_pairs={{0,2},{1,3},{2,0},{3,1},{4,6},{5,7},{6,4},{7,5},{8,10},{9,11},{10,... | collective-permute-start | bytes 1044488 | tf_op jit(solution)/shard_map/ppermute | solution.py:25
  63.7 9.6 %collective-permute-start.6 = (bf16[272,640]{0,1:T(8,128)(2,1)}, bf16[272,640]{0,1:T(8,128)(2,1)S(1)}, u32[]{:S(2)}, u32[]{:S(2)}) collective-permute-start(bf16[272,640]{0,1:T(8,128)(2,1)} %collective-permute-done.2), channel_id=1, source_target_pairs={{0,8},{1,9},{2,10},{3,11},{4,12},{5,13},{6,14},{7,15},{8,0},{9,1},... | collective-permute-start | bytes 1044488 | tf_op jit(solution)/shard_map/ppermute | solution.py:25
  71.9 13.5 %collective-permute-start.21 = (bf16[272,640]{0,1:T(8,128)(2,1)}, bf16[272,640]{0,1:T(8,128)(2,1)}, u32[]{:S(2)}, u32[]{:S(2)}) collective-permute-start(bf16[272,640]{0,1:T(8,128)(2,1)} %collective-permute-done.19), channel_id=1, source_target_pairs={{0,2},{1,3},{2,0},{3,1},{4,6},{5,7},{6,4},{7,5},{8,10},{9,11},{10,... | collective-permute-start | bytes 1044488 | tf_op jit(solution)/shard_map/ppermute | solution.py:25
  73.3 14.2 %collective-permute-start.23 = (bf16[272,640]{0,1:T(8,128)(2,1)}, bf16[272,640]{0,1:T(8,128)(2,1)S(1)}, u32[]{:S(2)}, u32[]{:S(2)}) collective-permute-start(bf16[272,640]{0,1:T(8,128)(2,1)} %collective-permute-done.19), channel_id=1, source_target_pairs={{0,8},{1,9},{2,10},{3,11},{4,12},{5,13},{6,14},{7,15},{8,0},{9,1},... | collective-permute-start | bytes 1044488 | tf_op jit(solution)/shard_map/ppermute | solution.py:25
  87.9 7.8 %collective-permute-start.9 = (bf16[272,640]{0,1:T(8,128)(2,1)S(1)}, bf16[272,640]{0,1:T(8,128)(2,1)S(1)}, u32[]{:S(2)}, u32[]{:S(2)}) collective-permute-start(bf16[272,640]{0,1:T(8,128)(2,1)S(1)} %collective-permute-done.5), channel_id=1, source_target_pairs={{0,8},{1,9},{2,10},{3,11},{4,12},{5,13},{6,14},{7,15},{8,0},{9,1},... | collective-permute-start | bytes 1044488 | tf_op jit(solution)/shard_map/ppermute | solution.py:25
  87.9 31.5 %collective-permute-start.26 = (bf16[272,640]{0,1:T(8,128)(2,1)}, bf16[272,640]{0,1:T(8,128)(2,1)}, u32[]{:S(2)}, u32[]{:S(2)}) collective-permute-start(bf16[272,640]{0,1:T(8,128)(2,1)} %collective-permute-done.22), channel_id=1, source_target_pairs={{0,8},{1,9},{2,10},{3,11},{4,12},{5,13},{6,14},{7,15},{8,0},{9,1},... | collective-permute-start | bytes 1044488 | tf_op jit(solution)/shard_map/ppermute | solution.py:25
  88.4 6.6 %collective-permute-start.7 = (bf16[272,640]{0,1:T(8,128)(2,1)S(1)}, bf16[272,640]{0,1:T(8,128)(2,1)S(1)}, u32[]{:S(2)}, u32[]{:S(2)}) collective-permute-start(bf16[272,640]{0,1:T(8,128)(2,1)S(1)} %collective-permute-done.3), channel_id=1, source_target_pairs={{0,8},{1,9},{2,10},{3,11},{4,12},{5,13},{6,14},{7,15},{8,0},{9,1},... | collective-permute-start | bytes 1044488 | tf_op jit(solution)/shard_map/ppermute | solution.py:25
  88.5 6.6 %collective-permute-start.8 = (bf16[272,640]{0,1:T(8,128)(2,1)S(1)}, bf16[272,640]{0,1:T(8,128)(2,1)S(1)}, u32[]{:S(2)}, u32[]{:S(2)}) collective-permute-start(bf16[272,640]{0,1:T(8,128)(2,1)S(1)} %collective-permute-done.4), channel_id=1, source_target_pairs={{0,8},{1,9},{2,10},{3,11},{4,12},{5,13},{6,14},{7,15},{8,0},{9,1},... | collective-permute-start | bytes 1044488 | tf_op jit(solution)/shard_map/ppermute | solution.py:25
  95.0 16.7 %collective-permute-start.24 = (bf16[272,640]{0,1:T(8,128)(2,1)}, bf16[272,640]{0,1:T(8,128)(2,1)}, u32[]{:S(2)}, u32[]{:S(2)}) collective-permute-start(bf16[272,640]{0,1:T(8,128)(2,1)} %collective-permute-done.20), channel_id=1, source_target_pairs={{0,8},{1,9},{2,10},{3,11},{4,12},{5,13},{6,14},{7,15},{8,0},{9,1},... | collective-permute-start | bytes 1044488 | tf_op jit(solution)/shard_map/ppermute | solution.py:25
  95.2 19.8 %collective-permute-start.25 = (bf16[272,640]{0,1:T(8,128)(2,1)}, bf16[272,640]{0,1:T(8,128)(2,1)}, u32[]{:S(2)}, u32[]{:S(2)}) collective-permute-start(bf16[272,640]{0,1:T(8,128)(2,1)} %collective-permute-done.21), channel_id=1, source_target_pairs={{0,8},{1,9},{2,10},{3,11},{4,12},{5,13},{6,14},{7,15},{8,0},{9,1},... | collective-permute-start | bytes 1044488 | tf_op jit(solution)/shard_map/ppermute | solution.py:25
  138.5 24.8 %collective-permute-start.18 = (bf16[64,320]{1,0:T(8,128)(2,1)}, bf16[64,320]{1,0:T(8,128)(2,1)}, u32[]{:S(2)}, u32[]{:S(2)}) collective-permute-start(bf16[64,320]{1,0:T(8,128)(2,1)} %get-tuple-element.66), channel_id=1, source_target_pairs={{0,24},{1,25},{2,26},{3,27},{4,0},{5,1},{6,2},{7,3},{8,28},{9,29},... | collective-permute-start | bytes 122888 | tf_op jit(solution)/shard_map/ppermute | solution.py:25
  140.2 23.7 %collective-permute-start.17 = (bf16[64,320]{1,0:T(8,128)(2,1)}, bf16[64,320]{1,0:T(8,128)(2,1)}, u32[]{:S(2)}, u32[]{:S(2)}) collective-permute-start(bf16[64,320]{1,0:T(8,128)(2,1)} %get-tuple-element.67), channel_id=1, source_target_pairs={{0,16},{1,17},{2,18},{3,19},{4,24},{5,25},{6,26},{7,27},{8,20},{9,... | collective-permute-start | bytes 122888 | tf_op jit(solution)/shard_map/ppermute | solution.py:25
  140.8 23.2 %collective-permute-start.16 = (bf16[64,320]{1,0:T(8,128)(2,1)}, bf16[64,320]{1,0:T(8,128)(2,1)}, u32[]{:S(2)}, u32[]{:S(2)}) collective-permute-start(bf16[64,320]{1,0:T(8,128)(2,1)} %get-tuple-element.68), channel_id=1, source_target_pairs={{0,8},{1,9},{2,10},{3,11},{4,16},{5,17},{6,18},{7,19},{8,12},{9,13... | collective-permute-start | bytes 122888 | tf_op jit(solution)/shard_map/ppermute | solution.py:25
  142.5 22.1 %collective-permute-start.15 = (bf16[64,320]{1,0:T(8,128)(2,1)}, bf16[64,320]{1,0:T(8,128)(2,1)}, u32[]{:S(2)}, u32[]{:S(2)}) collective-permute-start(bf16[64,320]{1,0:T(8,128)(2,1)} %get-tuple-element.65), channel_id=1, source_target_pairs={{0,0},{1,1},{2,2},{3,3},{4,8},{5,9},{6,10},{7,11},{8,4},{9,5},{10,... | collective-permute-start | bytes 122888 | tf_op jit(solution)/shard_map/ppermute | solution.py:25
  148.2 22.7 %collective-permute-start.14 = (bf16[64,320]{1,0:T(8,128)(2,1)}, bf16[64,320]{1,0:T(8,128)(2,1)}, u32[]{:S(2)}, u32[]{:S(2)}) collective-permute-start(bf16[64,320]{1,0:T(8,128)(2,1)} %get-tuple-element.58), channel_id=1, source_target_pairs={{0,24},{1,25},{2,26},{3,27},{4,0},{5,1},{6,2},{7,3},{8,28},{9,29},... | collective-permute-start | bytes 122888 | tf_op jit(solution)/shard_map/ppermute | solution.py:25
  163.3 9.2 %collective-permute-start.13 = (bf16[64,320]{1,0:T(8,128)(2,1)S(1)}, bf16[64,320]{1,0:T(8,128)(2,1)S(1)}, u32[]{:S(2)}, u32[]{:S(2)}) collective-permute-start(bf16[64,320]{1,0:T(8,128)(2,1)S(1)} %copy-done.22), channel_id=1, source_target_pairs={{0,16},{1,17},{2,18},{3,19},{4,24},{5,25},{6,26},{7,27},{8,20},{9,... | collective-permute-start | bytes 122888 | tf_op jit(solution)/shard_map/ppermute | solution.py:25
  163.9 8.6 %collective-permute-start.12 = (bf16[64,320]{1,0:T(8,128)(2,1)S(1)}, bf16[64,320]{1,0:T(8,128)(2,1)S(1)}, u32[]{:S(2)}, u32[]{:S(2)}) collective-permute-start(bf16[64,320]{1,0:T(8,128)(2,1)S(1)} %copy-done.21), channel_id=1, source_target_pairs={{0,8},{1,9},{2,10},{3,11},{4,16},{5,17},{6,18},{7,19},{8,12},{9,13... | collective-permute-start | bytes 122888 | tf_op jit(solution)/shard_map/ppermute | solution.py:25
  164.0 9.3 %collective-permute-start.11 = (bf16[64,320]{1,0:T(8,128)(2,1)S(1)}, bf16[64,320]{1,0:T(8,128)(2,1)S(1)}, u32[]{:S(2)}, u32[]{:S(2)}) collective-permute-start(bf16[64,320]{1,0:T(8,128)(2,1)S(1)} %copy-done.20), channel_id=1, source_target_pairs={{0,0},{1,1},{2,2},{3,3},{4,8},{5,9},{6,10},{7,11},{8,4},{9,5},{10,... | collective-permute-start | bytes 122888 | tf_op jit(solution)/shard_map/ppermute | solution.py:25
  164.7 15.5 %collective-permute-start.34 = (bf16[64,320]{1,0:T(8,128)(2,1)S(1)}, bf16[64,320]{1,0:T(8,128)(2,1)S(1)}, u32[]{:S(2)}, u32[]{:S(2)}) collective-permute-start(bf16[64,320]{1,0:T(8,128)(2,1)S(1)} %copy-done.19), channel_id=1, source_target_pairs={{0,24},{1,25},{2,26},{3,27},{4,0},{5,1},{6,2},{7,3},{8,28},{9,29},... | collective-permute-start | bytes 122888 | tf_op jit(solution)/shard_map/ppermute | solution.py:25
  171.0 9.8 %collective-permute-start.33 = (bf16[64,320]{1,0:T(8,128)(2,1)S(1)}, bf16[64,320]{1,0:T(8,128)(2,1)S(1)}, u32[]{:S(2)}, u32[]{:S(2)}) collective-permute-start(bf16[64,320]{1,0:T(8,128)(2,1)S(1)} %copy-done.18), channel_id=1, source_target_pairs={{0,16},{1,17},{2,18},{3,19},{4,24},{5,25},{6,26},{7,27},{8,20},{9,... | collective-permute-start | bytes 122888 | tf_op jit(solution)/shard_map/ppermute | solution.py:25
  172.5 8.2 %collective-permute-start.32 = (bf16[64,320]{1,0:T(8,128)(2,1)S(1)}, bf16[64,320]{1,0:T(8,128)(2,1)S(1)}, u32[]{:S(2)}, u32[]{:S(2)}) collective-permute-start(bf16[64,320]{1,0:T(8,128)(2,1)S(1)} %copy-done.17), channel_id=1, source_target_pairs={{0,8},{1,9},{2,10},{3,11},{4,16},{5,17},{6,18},{7,19},{8,12},{9,13... | collective-permute-start | bytes 122888 | tf_op jit(solution)/shard_map/ppermute | solution.py:25
  172.5 8.9 %collective-permute-start.31 = (bf16[64,320]{1,0:T(8,128)(2,1)S(1)}, bf16[64,320]{1,0:T(8,128)(2,1)S(1)}, u32[]{:S(2)}, u32[]{:S(2)}) collective-permute-start(bf16[64,320]{1,0:T(8,128)(2,1)S(1)} %copy-done.16), channel_id=1, source_target_pairs={{0,0},{1,1},{2,2},{3,3},{4,8},{5,9},{6,10},{7,11},{8,4},{9,5},{10,... | collective-permute-start | bytes 122888 | tf_op jit(solution)/shard_map/ppermute | solution.py:25
  173.2 9.0 %collective-permute-start.30 = (bf16[64,320]{1,0:T(8,128)(2,1)S(1)}, bf16[64,320]{1,0:T(8,128)(2,1)S(1)}, u32[]{:S(2)}, u32[]{:S(2)}) collective-permute-start(bf16[64,320]{1,0:T(8,128)(2,1)S(1)} %get-tuple-element.74), channel_id=1, source_target_pairs={{0,24},{1,25},{2,26},{3,27},{4,0},{5,1},{6,2},{7,3},{8,28},{9,29},... | collective-permute-start | bytes 122888 | tf_op jit(solution)/shard_map/ppermute | solution.py:25
  180.7 5.9 %collective-permute-start.28 = (bf16[64,320]{1,0:T(8,128)(2,1)S(1)}, bf16[64,320]{1,0:T(8,128)(2,1)S(1)}, u32[]{:S(2)}, u32[]{:S(2)}) collective-permute-start(bf16[64,320]{1,0:T(8,128)(2,1)S(1)} %get-tuple-element.76), channel_id=1, source_target_pairs={{0,8},{1,9},{2,10},{3,11},{4,16},{5,17},{6,18},{7,19},{8,12},{9,13... | collective-permute-start | bytes 122888 | tf_op jit(solution)/shard_map/ppermute | solution.py:25
  (29 other events, 201.2 us)

commit v2 on v0

v2 whole, which is shorter than its diff:
```python
import functools
import math

import jax
import jax.numpy as jnp
from jax import lax
from jax.experimental import pallas as pl
from jax.experimental.pallas import tpu as pltpu
from jax.sharding import PartitionSpec as P

WINDOW = 256
NS_STEPS = 3
NEWTON_A = 3.4445
NEWTON_B = -4.775
NEWTON_C = 2.0315
NORM_EPS = 1e-06
FROB_EPS = 1e-07
BOTH = ("head", "tok")
EXTRA = 16
VMEM_BYTES = 20 * 1024 * 1024
F32 = jnp.float32
BF16 = jnp.bfloat16


def moved(array, heads, toks, where):
    pairs = []
    for h in range(heads):
        for t in range(toks):
            to = where(h, t)
            if to is not None:
                pairs.append((h * toks + t, to[0] * toks + to[1]))
    return lax.ppermute(array, BOTH, pairs)


def after(arrays, others):
    return lax.optimization_barrier((arrays, others))[0]


def turned(array):
    return jnp.swapaxes(array, 1, 2)


def dot_nn(left, right):
    return jnp.dot(left, right, preferred_element_type=F32)


def dot_nt(left, right):
    return lax.dot_general(left, right, (((1,), (1,)), ((), ())), preferred_element_type=F32)


def call(kernel, out_shape, args, scratch=(), smem=(), loose=(), vmem=VMEM_BYTES, flops=0):
    def space(i):
        return pltpu.SMEM if i in smem else pl.ANY if i in loose else pltpu.VMEM

    specs = [pl.BlockSpec(memory_space=space(i)) for i in range(len(args))]
    return pl.pallas_call(
        kernel,
        out_shape=out_shape,
        in_specs=specs,
        out_specs=jax.tree.map(lambda _: pl.BlockSpec(memory_space=pltpu.VMEM), out_shape),
        scratch_shapes=list(scratch),
        compiler_params=pltpu.CompilerParams(vmem_limit_bytes=vmem),
        cost_estimate=pl.CostEstimate(flops=flops, bytes_accessed=1 << 20, transcendentals=0),
    )(*args)


def pack_kernel(segments, key_ref, value_ref, rate_ref, step_ref, *refs):
    outs, sems = refs[:segments], refs[segments]
    width, rows = key_ref.shape[1:]
    copies = []
    for s, out_ref in enumerate(outs):
        for i, ref in enumerate((key_ref, value_ref)):
            copies.append(
                pltpu.make_async_copy(
                    ref.at[s], out_ref.at[pl.ds(i * width, width)], sems.at[s, i]
                )
            )
    for copy in copies:
        copy.start()
    for s, out_ref in enumerate(outs):
        rate = rate_ref[s]
        step = jnp.full_like(rate, step_ref[0])
        row = lax.broadcasted_iota(jnp.int32, (EXTRA, rows), 0)
        filled = jnp.zeros((EXTRA, rows), F32)
        at = 0
        for value in (rate, step):
            for _ in range(3):
                term = value.astype(BF16).astype(F32)
                filled = jnp.where(row == at, term, filled)
                value = value - term
                at += 1
        out_ref[2 * width :] = filled.astype(BF16)
    for copy in copies:
        copy.wait()


def weight_kernel(gate_ref, up_ref, down_ref, out_ref):
    width = down_ref.shape[0]
    for i, ref in enumerate((gate_ref, up_ref)):
        out_ref[i * width : (i + 1) * width, :width] = ref[...].T
    out_ref[2 * width :, :width] = down_ref[...]
    out_ref[:, width:] = jnp.zeros((3 * width, out_ref.shape[1] - width), BF16)


def add_gradients(blocks, weights, total_ref):
    width = weights.shape[1]
    first = True
    for block in blocks:
        keys = block[:width]
        values = block[width : 2 * width]
        terms = block[2 * width :].astype(F32)
        rate = -(terms[0:1] + terms[1:2] + terms[2:3])
        both = dot_nn(weights[: 2 * width], keys)
        gate, up = both[:width], both[width:]
        back = dot_nn(weights[2 * width :], values) * rate
        sig = jax.nn.sigmoid(gate)
        swish = gate * sig
        hidden = (swish * up * rate).astype(BF16)
        d_gate = (back * up * (sig + swish * (1.0 - sig))).astype(BF16)
        d_up = (back * swish).astype(BF16)
        parts = (dot_nt(d_gate, keys), dot_nt(d_up, keys), dot_nt(hidden, values))
        for i, part in enumerate(parts):
            at = pl.ds(i * width, width)
            total_ref[at] = part if first else total_ref[at] + part
        first = False


def orthogonalized(stacked, width):
    iterates = []
    for i in range(3):
        one = stacked[i * width : (i + 1) * width]
        norm = jnp.sqrt(jnp.sum(one * one, keepdims=True))
        iterates.append((one / (norm + FROB_EPS)).astype(BF16))
    for _ in range(NS_STEPS):
        squares = [dot_nt(x, x).astype(BF16) for x in iterates]
        mixings = [
            (NEWTON_B * s.astype(F32) + NEWTON_C * dot_nn(s, s)).astype(BF16) for s in squares
        ]
        iterates = [
            (NEWTON_A * x.astype(F32) + dot_nn(m, x)).astype(BF16)
            for m, x in zip(mixings, iterates)
        ]
    return iterates


def updated(mine, other, weights, step_block, out_ref):
    width = out_ref.shape[1]
    terms = step_block[2 * width :].astype(F32)
    step = (terms[3:4] + terms[4:5] + terms[5:6])[:, 0:1]
    total = mine[:, :width].astype(F32) + other[:, :width].astype(F32)
    for i, x in enumerate(orthogonalized(total, width)):
        at = pl.ds(i * width, width)
        out_ref[at] = (weights[at].astype(F32) - step * x.astype(F32)).astype(BF16)


def write_sum(total_ref, out_ref):
    width = total_ref.shape[1]
    out_ref[:, :width] = total_ref[...].astype(BF16)
    out_ref[:, width:] = jnp.zeros((out_ref.shape[0], out_ref.shape[1] - width), BF16)


def fast_rows(query, weights):
    width = weights.shape[1]
    both = dot_nt(query, weights[: 2 * width])
    gate, up = both[:, :width], both[:, width:]
    hidden = (gate * jax.nn.sigmoid(gate) * up).astype(BF16)
    return dot_nn(hidden, weights[2 * width :]).astype(BF16)


def first_kernel(count, place_ref, *refs):
    blocks = refs[:count]
    mine, other, held_ref, out_ref, total_ref = refs[count:]
    width = held_ref.shape[1]
    held_ref[...] = jnp.where(place_ref[3] == 1, mine[:, :width], other[:, :width])
    add_gradients(blocks, held_ref, total_ref)
    write_sum(total_ref, out_ref)


def update_kernel(mine, other, weight_ref, block, next_ref):
    updated(mine, other, weight_ref, block, next_ref)


def middle_kernel(count, *refs):
    blocks, (weight_ref, out_ref, total_ref) = refs[:count], refs[count:]
    add_gradients(blocks, weight_ref, total_ref)
    write_sum(total_ref, out_ref)


def last_kernel(heads, place_ref, mine, other, weight_ref, block, query_ref, *refs):
    outs, (next_ref, fast_ref) = refs[:heads], refs[heads:]
    updated(mine, other, weight_ref, block, next_ref)
    fast_ref[...] = fast_rows(query_ref[...], next_ref)
    share = fast_ref.shape[0] // heads
    for shift in range(heads):
        to = lax.rem(place_ref[0] + shift, heads)
        outs[shift][...] = fast_ref[pl.ds(pl.multiple_of(to * share, share), share)]


def query_kernel(heads, segments, choices, *refs):
    place_ref, query_ref = refs[:2]
    weight_refs = refs[2 : 1 + segments]
    at = 1 + segments
    owns = refs[at : at + segments]
    at += segments
    cands = [refs[at + s * choices : at + (s + 1) * choices] for s in range(segments)]
    at += segments * choices
    outs = refs[at : at + heads]
    last_query_ref, rows_ref = refs[at + heads :]
    head, place, core = place_ref[0], place_ref[1], place_ref[2]
    width, rows = query_ref.shape[1:]
    share = rows // heads
    scale = 1.0 / math.sqrt(width)
    for s in range(segments):
        query = query_ref[s].T
        if s == segments - 1:
            last_query_ref[...] = query
        else:
            rows_ref[segments + s] = fast_rows(query, weight_refs[s])
        prev = cands[s][choices - 1][: 2 * width]
        if s > 0:
            prev = jnp.where(core == 0, cands[s - 1][choices - 1][: 2 * width], prev)
        for i in range(choices - 1):
            low = lax.rem(place, 2 << i) == (1 << i)
            prev = jnp.where(low, cands[s][i][: 2 * width], prev)
        own = owns[s]
        own_scores = dot_nn(query, own[:width]) * scale
        prev_scores = dot_nn(query, prev[:width]) * scale
        q_at = lax.broadcasted_iota(jnp.int32, (rows, rows), 0)
        k_at = lax.broadcasted_iota(jnp.int32, (rows, rows), 1)
        own_live = (k_at <= q_at) & (k_at > q_at - WINDOW)
        prev_live = k_at - rows > q_at - WINDOW
        if s == 0:
            reach = jnp.where((core == 0) & (place == 0), -rows, 0)
            prev_live = prev_live & (k_at < rows + reach)
        own_scores = jnp.where(own_live, own_scores, -1e30)
        prev_scores = jnp.where(prev_live, prev_scores, -1e30)
        top = jnp.maximum(
            jnp.max(own_scores, axis=-1, keepdims=True),
            jnp.max(prev_scores, axis=-1, keepdims=True),
        )
        own_expo = jnp.exp(own_scores - top)
        prev_expo = jnp.exp(prev_scores - top)
        total = jnp.sum(own_expo, axis=-1, keepdims=True) + jnp.sum(
            prev_expo, axis=-1, keepdims=True
        )
        over = 1.0 / total
        attended = dot_nt((own_expo * over).astype(BF16), own[width : 2 * width]) + dot_nt(
            (prev_expo * over).astype(BF16), prev[width:]
        )
        rows_ref[s] = attended.astype(BF16)
    for shift in range(heads):
        to = lax.rem(head + shift, heads)
        for i in range(2 * segments - 1):
            outs[shift][i] = rows_ref[i, pl.ds(pl.multiple_of(to * share, share), share)]


def normed(parts, gain_row, full_width):
    total = 0.0
    wides = []
    for part in parts:
        wide = part.astype(F32)
        wides.append(wide)
        total = total + jnp.sum(wide * wide, axis=-1, keepdims=True)
    factor = lax.rsqrt(total / full_width + NORM_EPS)
    width = parts[0].shape[1]
    return [
        wide * factor * gain_row[:, i * width : (i + 1) * width] for i, wide in enumerate(wides)
    ]


def final_kernel(heads, segments, me_ref, gain_ref, *refs):
    early, late, out_ref = refs[:heads], refs[heads : 2 * heads], refs[2 * heads]
    held = refs[2 * heads + 1]
    share, width = late[0].shape
    me = me_ref[0]
    for k in range(heads):
        at = lax.rem(me - k + heads, heads)
        held[at, : 2 * segments - 1] = early[k][...]
        held[at, 2 * segments - 1] = late[k][...]
    for s in range(segments):
        fast = normed([held[j, segments + s] for j in range(heads)], gain_ref[0:1], heads * width)
        att = normed([held[j, s] for j in range(heads)], gain_ref[1:2], heads * width)
        out_ref[s, 0] = jnp.concatenate([a + b for a, b in zip(fast, att)], -1)


def on_device(
    query_rows,
    key_rows,
    value_rows,
    token_rates,
    gate_weight,
    up_weight,
    down_weight,
    step_size,
    branch_gains,
    *,
    heads,
    toks,
):
    segments, rows, width = query_rows.shape
    half = toks // 2
    share = rows // heads

    def regroup(h, t):
        return h - h % 2 + t // half, (h % 2) * half + t % half

    def other_core(h, t):
        return h ^ 1, t

    def send(array, where):
        return moved(array, heads, toks, where)

    me = lax.axis_index("head")
    core = me % 2
    tok = lax.axis_index("tok")
    group = tok // half
    place = tok % half
    head_of = me - core + group

    position = jnp.stack([head_of, place, core, (core == group).astype(jnp.int32)])
    position = position.astype(jnp.int32)
    block_shape = jax.ShapeDtypeStruct((2 * width + EXTRA, rows), BF16)
    blocks = call(
        functools.partial(pack_kernel, segments),
        (block_shape,) * segments,
        (turned(key_rows), turned(value_rows), token_rates, step_size),
        (pltpu.SemaphoreType.DMA((segments, 2)),),
        smem=(3,),
        loose=(0, 1),
        vmem=56 * 1024 * 1024,
    )
    own = [send(block, regroup) for block in blocks]
    padded = -(-width // 128) * 128
    stacked = call(
        weight_kernel,
        jax.ShapeDtypeStruct((3 * width, padded), BF16),
        after((gate_weight[0], up_weight[0], down_weight[0]), blocks),
    )
    lent = send(
        stacked, lambda h, t: (h ^ 1, t) if h % 2 == t // half else None
    )
    queries = send(turned(query_rows), regroup)

    here = []
    for s in range(segments):
        here.append(
            [own[s]]
            + [
                send(own[s], lambda h, t, mask=mask: (h, t ^ mask)) for mask in range(1, half)
            ]
        )

    grad_shape = jax.ShapeDtypeStruct((3 * width, padded), BF16)
    weight_shape = jax.ShapeDtypeStruct((3 * width, width), BF16)
    total = pltpu.VMEM((3 * width, width), F32)
    grad_flops = 2 * 6 * half * rows * width * width
    ns_flops = 2 * 27 * width**3

    weights, mine = call(
        functools.partial(first_kernel, half),
        (weight_shape, grad_shape),
        (position, *after(here[0], own), stacked, lent),
        (total,),
        smem=(0,),
        flops=grad_flops,
    )
    all_weights = []
    for s in range(1, segments):
        other = send(mine, other_core)
        if s == 1:
            other, queries = lax.optimization_barrier((other, queries))
        weights = call(
            update_kernel, weight_shape, (mine, other, weights, own[s - 1]), flops=ns_flops
        )
        mine = call(
            functools.partial(middle_kernel, half),
            grad_shape,
            (*here[s], weights),
            (total,),
            flops=grad_flops,
        )
        all_weights.append(weights)
    other = send(mine, other_core)

    lasts = [
        send(here[s][half - 1], lambda h, t: (h ^ 1, t) if t % half == 0 else None)
        for s in range(segments)
    ]
    cands = []
    for s in range(segments):
        one = []
        mask = 1
        while mask < half:
            one.append(here[s][mask])
            mask = 2 * mask + 1
        cands.append(one + [lasts[s]])
    choices = len(cands[0])
    *early, last_query = call(
        functools.partial(query_kernel, heads, segments, choices),
        tuple(
            jax.ShapeDtypeStruct((2 * segments - 1, share, width), BF16) for _ in range(heads)
        )
        + (jax.ShapeDtypeStruct((rows, width), BF16),),
        (position, queries, *all_weights, *own, *[c for one in cands for c in one]),
        (pltpu.VMEM((2 * segments - 1, rows, width), BF16),),
        smem=(0,),
        flops=2 * segments * 4 * rows * rows * width,
    )
    late = call(
        functools.partial(last_kernel, heads),
        tuple(jax.ShapeDtypeStruct((share, width), BF16) for _ in range(heads)),
        (position, mine, other, weights, own[-1], last_query),
        (pltpu.VMEM((3 * width, width), BF16), pltpu.VMEM((rows, width), BF16)),
        smem=(0,),
        flops=ns_flops,
    )

    def spread(parts):
        got = []
        for shift in range(heads):

            def where(h, t, shift=shift):
                mine = h - h % 2 + t // half
                return (mine + shift) % heads, (h % 2) * half + t % half

            got.append(send(parts[shift], where))
        return got

    return call(
        functools.partial(final_kernel, heads, segments),
        jax.ShapeDtypeStruct((segments, 1, share, heads * width), F32),
        (me[None].astype(jnp.int32), branch_gains, *spread(early), *spread(late)),
        (pltpu.VMEM((heads, 2 * segments, share, width), BF16),),
        smem=(0,),
    )


def solution(mesh):
    placed = (
        P(None, "tok", "head"),
        P(None, "tok", "head"),
        P(None, "tok", "head"),
        P(None, "head", "tok"),
        P("head", None, None),
        P("head", None, None),
        P("head", None, None),
        P("head"),
        P(),
    )
    heads, toks = mesh.shape["head"], mesh.shape["tok"]

    def program(*arrays):
        return on_device(*arrays, heads=heads, toks=toks)

    return jax.shard_map(
        program,
        mesh=mesh,
        in_specs=placed,
        out_specs=P(None, "tok", "head", None),
        check_vma=False,
    )
```

time: 247 us -> 97.3 us (0.39)
  waiting for transfers between devices: 171 us -> 35.4 us
  matrix products: 29.2 us -> 0 us
  starting transfers between devices: 11.7 us -> 36.1 us
  Pallas kernels: 0 us -> 23.6 us
  between operations: 14.4 us -> 0.86 us
  local copies, waits for them, and re-layouts: 10.8 us -> 0.96 us
  other arithmetic: 8.92 us -> 0.08 us
    psum x2 -> x0, waiting for transfers between devices: 137 us -> none  [on_device(): update = local_orthogonalize(lax.psum(grads, 'tok'))]
    ppermute x2 -> x22, starting transfers between devices: 4.54 us -> 36.1 us  [moved(): return lax.ppermute(array, BOTH, pairs)]
    dot_general x29 -> x0, matrix products: 27.5 us -> none  [the longest x6 11 us: local_orthogonalize(): jnp.einsum('mij,mjk->mik', mixing, iterate, preferred_element_type=jnp.fl...]
    pallas_call x0 -> x8, Pallas kernels: none -> 23.6 us  [call(): pl.pallas_call(kernel, out_shape=out_shape, in_specs=specs, out_specs=jax...]
    ppermute x2 -> x22, waiting for transfers between devices: 21.4 us -> 35.4 us  [moved(): return lax.ppermute(array, BOTH, pairs)]
    all_to_all x2 -> x0, waiting for transfers between devices: 12.7 us -> none  [the longest x1 6.6 us: on_device(): lax.all_to_all(attended, 'head', split_axis=1, concat_axis=2, tiled=True)]
    all_to_all x2 -> x0, starting transfers between devices: 7.1 us -> none  [the longest x1 3.64 us: on_device(): lax.all_to_all(attended, 'head', split_axis=1, concat_axis=2, tiled=True)]
    unnamed x37 -> x14, local copies, waits for them, and re-layouts: 5.1 us -> 0.96 us
  transfers between devices with their start and end apart: 6 -> 22, of which waited for: 6 -> 10; matrix products, arithmetic and copies ran while one was open for 4% -> 0% of each run, Pallas kernels for 0% -> 13%
where the time goes in v2:
time: 97.3 us; the launch traced here: 96.9 us
  starting transfers between devices  36.1 us (37%)
  waiting for transfers between devices  35.4 us (36%)
  Pallas kernels  23.6 us (24%)
    ppermute x22, starting transfers between devices, moved(): return lax.ppermute(array, BOTH, pairs)  36.1 us
    ppermute x22, waiting for transfers between devices, moved(): return lax.ppermute(array, BOTH, pairs)  35.4 us
    pallas_call x8, Pallas kernels, call(): pl.pallas_call(kernel, out_shape=out_shape, in_specs=specs, out_specs=jax...  23.6 us
  transfers between devices with their start and end apart: 22, of which 10 were waited for; matrix products, arithmetic and copies ran while one was open for 0% of the time, Pallas kernels for 13%

profile of v2, /device:TPU:0, one launch (start us, length us, event | category | flops | bytes accessed | tf_op | source)
XLA Modules:
  0.0 96.9 jit_solution(11962694002130648979)
XLA Ops:
  0.7 2.8 %shard_map.91 = (bf16[656,256]{1,0:T(8,128)(2,1)}, bf16[656,256]{1,0:T(8,128)(2,1)}) custom-call(bf16[2,320,256]{2,1,0:T(8,128)(2,1)} %bitcast.14, bf16[2,320,256]{2,1,0:T(8,128)(2,1)} %bitcast.15, f32[2,1,256]{2,1,0:T(1,128)} %rate_ref.1, f32[1]{0:T(128)S(6)} %copy.10.step_ref), custom_call_target="tpu_custom_call" | custom-call | bytes 1048576 | tf_op jit(solution)/shard_map/pallas_call | solution.py:56
  3.5 0.9 copy-done.2
  4.6 2.4 %collective-permute-start.5 = (bf16[960,384]{1,0:T(8,128)(2,1)S(1)}, bf16[960,384]{1,0:T(8,128)(2,1)S(1)}, u32[]{:S(2)}, u32[]{:S(2)}) collective-permute-start(bf16[960,384]{1,0:T(8,128)(2,1)S(1)} %shard_map.92.refs_4_), channel_id=1, source_target_pairs={{0,8},{1,9},{2,10},{3,11},{12,4},{13,5},{14,6},{15,7},{16,24},{17,... | collective-permute-start | bytes 2211848 | tf_op jit(solution)/shard_map/ppermute | solution.py:32
  7.0 0.7 collective-permute-start
  7.7 0.7 collective-permute-start.4
  8.4 2.4 %collective-permute-start.1 = (bf16[656,256]{1,0:T(8,128)(2,1)S(1)}, bf16[656,256]{1,0:T(8,128)(2,1)S(1)}, u32[]{:S(2)}, u32[]{:S(2)}) collective-permute-start(bf16[656,256]{1,0:T(8,128)(2,1)S(1)} %collective-permute-done.refs_0_.block.refs_3_), channel_id=1, source_target_pairs={{0,1},{1,0},{2,3},{3,2},{4,5},{5,4},{6,7},{7,6},{8,9},{9,8},{10,11... | collective-permute-start | bytes 1007624 | tf_op jit(solution)/shard_map/ppermute | solution.py:32
  10.8 1.6 %collective-permute-start.2 = (bf16[656,256]{1,0:T(8,128)(2,1)S(1)}, bf16[656,256]{1,0:T(8,128)(2,1)S(1)}, u32[]{:S(2)}, u32[]{:S(2)}) collective-permute-start(bf16[656,256]{1,0:T(8,128)(2,1)S(1)} %collective-permute-done.refs_0_.block.refs_3_), channel_id=1, source_target_pairs={{0,2},{1,3},{2,0},{3,1},{4,6},{5,7},{6,4},{7,5},{8,10},{9,11},{10,... | collective-permute-start | bytes 1007624 | tf_op jit(solution)/shard_map/ppermute | solution.py:32
  12.5 3.5 %collective-permute-done.1.refs_1_.refs_5_ = bf16[656,256]{1,0:T(8,128)(2,1)S(1)} collective-permute-done((bf16[656,256]{1,0:T(8,128)(2,1)S(1)}, bf16[656,256]{1,0:T(8,128)(2,1)S(1)}, u32[]{:S(2)}, u32[]{:S(2)}) %collective-permute-start.1) | collective-permute-done | bytes 335904 | tf_op jit(solution)/shard_map/ppermute | solution.py:32
  16.0 4.7 %collective-permute-done.2.refs_2_ = bf16[656,256]{1,0:T(8,128)(2,1)S(1)} collective-permute-done((bf16[656,256]{1,0:T(8,128)(2,1)S(1)}, bf16[656,256]{1,0:T(8,128)(2,1)S(1)}, u32[]{:S(2)}, u32[]{:S(2)}) %collective-permute-start.2) | collective-permute-done | bytes 335904 | tf_op jit(solution)/shard_map/ppermute | solution.py:32
  20.7 9.5 %collective-permute-done.3.refs_3_.refs_6_ = bf16[656,256]{1,0:T(8,128)(2,1)S(1)} collective-permute-done((bf16[656,256]{1,0:T(8,128)(2,1)S(1)}, bf16[656,256]{1,0:T(8,128)(2,1)S(1)}, u32[]{:S(2)}, u32[]{:S(2)}) %collective-permute-start.3) | collective-permute-done | bytes 335904 | tf_op jit(solution)/shard_map/ppermute | solution.py:32
  30.2 3.4 %shard_map.93 = (bf16[960,320]{1,0:T(8,128)(2,1)S(1)}, bf16[960,384]{1,0:T(8,128)(2,1)S(1)}) custom-call(s32[4]{0:T(128)S(1)} %pad_add_fusion.place_ref.refs_0_, bf16[656,256]{1,0:T(8,128)(2,1)S(1)} %collective-permute-done.refs_0_.block.refs_3_, bf16[656,256]{1,0:T(8,128)(2,1)S(1)} %collective-permute-done.1.refs_1_.refs_5_, ...), custom_call_target="tpu_custom_call" | custom-call | flops 1258291200 | bytes 1048576 | tf_op jit(solution)/shard_map/pallas_call | solution.py:56
  33.6 5.2 %collective-permute-start.6 = (bf16[960,384]{1,0:T(8,128)(2,1)S(1)}, bf16[960,384]{1,0:T(8,128)(2,1)S(1)}, u32[]{:S(2)}, u32[]{:S(2)}) collective-permute-start(bf16[960,384]{1,0:T(8,128)(2,1)S(1)} %get-tuple-element.36.mine), channel_id=1, source_target_pairs={{0,8},{1,9},{2,10},{3,11},{4,12},{5,13},{6,14},{7,15},{8,0},{9,1},... | collective-permute-start | bytes 2211848 | tf_op jit(solution)/shard_map/ppermute | solution.py:32
  39.5 1.0 %collective-permute-start.9 = (bf16[656,256]{1,0:T(8,128)(2,1)S(1)}, bf16[656,256]{1,0:T(8,128)(2,1)S(1)}, u32[]{:S(2)}, u32[]{:S(2)}) collective-permute-start(bf16[656,256]{1,0:T(8,128)(2,1)S(1)} %collective-permute-done.4.refs_4_.refs_0_.block), channel_id=1, source_target_pairs={{0,1},{1,0},{2,3},{3,2},{4,5},{5,4},{6,7},{7,6},{8,9},{9,8},{10,11... | collective-permute-start | bytes 1007624 | tf_op jit(solution)/shard_map/ppermute | solution.py:32
  40.5 2.4 %collective-permute-start.10 = (bf16[656,256]{1,0:T(8,128)(2,1)S(1)}, bf16[656,256]{1,0:T(8,128)(2,1)S(1)}, u32[]{:S(2)}, u32[]{:S(2)}) collective-permute-start(bf16[656,256]{1,0:T(8,128)(2,1)S(1)} %collective-permute-done.4.refs_4_.refs_0_.block), channel_id=1, source_target_pairs={{0,3},{1,2},{2,1},{3,0},{4,7},{5,6},{6,5},{7,4},{8,11},{9,10},{10,... | collective-permute-start | bytes 1007624 | tf_op jit(solution)/shard_map/ppermute | solution.py:32
  43.0 4.7 %shard_map.94.refs_2_.refs_4_.weight_ref = bf16[960,320]{1,0:T(8,128)(2,1)S(1)} custom-call(bf16[960,384]{1,0:T(8,128)(2,1)S(1)} %get-tuple-element.36.mine, bf16[960,384]{1,0:T(8,128)(2,1)S(1)} %collective-permute-done.6.other, bf16[960,320]{1,0:T(8,128)(2,1)S(1)} %get-tuple-element.39.weight_ref, ...), custom_call_target="tpu_custom_call" | custom-call | flops 1769472000 | bytes 1048576 | tf_op jit(solution)/shard_map/pallas_call | solution.py:56
  47.7 1.9 %collective-permute-done.9.refs_8_.refs_1_ = bf16[656,256]{1,0:T(8,128)(2,1)S(1)} collective-permute-done((bf16[656,256]{1,0:T(8,128)(2,1)S(1)}, bf16[656,256]{1,0:T(8,128)(2,1)S(1)}, u32[]{:S(2)}, u32[]{:S(2)}) %collective-permute-start.9) | collective-permute-done | bytes 335904 | tf_op jit(solution)/shard_map/ppermute | solution.py:32
  49.6 5.6 %collective-permute-done.10.refs_9_.refs_3_ = bf16[656,256]{1,0:T(8,128)(2,1)S(1)} collective-permute-done((bf16[656,256]{1,0:T(8,128)(2,1)S(1)}, bf16[656,256]{1,0:T(8,128)(2,1)S(1)}, u32[]{:S(2)}, u32[]{:S(2)}) %collective-permute-start.10) | collective-permute-done | bytes 335904 | tf_op jit(solution)/shard_map/ppermute | solution.py:32
  55.3 6.3 %collective-permute-done.16.refs_2_ = bf16[656,256]{1,0:T(8,128)(2,1)S(1)} collective-permute-done((bf16[656,256]{1,0:T(8,128)(2,1)S(1)}, bf16[656,256]{1,0:T(8,128)(2,1)S(1)}, u32[]{:S(2)}, u32[]{:S(2)}) %collective-permute-start.16) | collective-permute-done | bytes 335904 | tf_op jit(solution)/shard_map/ppermute | solution.py:32
  61.6 2.8 %shard_map.96.mine = bf16[960,384]{1,0:T(8,128)(2,1)S(1)} custom-call(bf16[656,256]{1,0:T(8,128)(2,1)S(1)} %collective-permute-done.4.refs_4_.refs_0_.block, bf16[656,256]{1,0:T(8,128)(2,1)S(1)} %collective-permute-done.9.refs_8_.refs_1_, bf16[656,256]{1,0:T(8,128)(2,1)S(1)} %collective-permute-done.16.refs_2_, ...), custom_call_target="tpu_custom_call" | custom-call | flops 1258291200 | bytes 1048576 | tf_op jit(solution)/shard_map/pallas_call | solution.py:56
  64.4 0.8 collective-permute-start.17
  65.2 1.9 %collective-permute-start.8 = (bf16[656,256]{1,0:T(8,128)(2,1)S(1)}, bf16[656,256]{1,0:T(8,128)(2,1)S(1)}, u32[]{:S(2)}, u32[]{:S(2)}) collective-permute-start(bf16[656,256]{1,0:T(8,128)(2,1)S(1)} %collective-permute-done.3.refs_3_.refs_6_), channel_id=1, source_target_pairs={{0,8},{4,12},{8,0},{12,4},{16,24},{20,28},{24,16},{28,20}} | collective-permute-start | bytes 1007624 | tf_op jit(solution)/shard_map/ppermute | solution.py:32
  67.1 2.6 %collective-permute-start.11 = (bf16[656,256]{1,0:T(8,128)(2,1)S(1)}, bf16[656,256]{1,0:T(8,128)(2,1)S(1)}, u32[]{:S(2)}, u32[]{:S(2)}) collective-permute-start(bf16[656,256]{1,0:T(8,128)(2,1)S(1)} %collective-permute-done.10.refs_9_.refs_3_), channel_id=1, source_target_pairs={{0,8},{4,12},{8,0},{12,4},{16,24},{20,28},{24,16},{28,20}} | collective-permute-start | bytes 1007624 | tf_op jit(solution)/shard_map/ppermute | solution.py:32
  69.7 1.1 %collective-permute-done.11.refs_10_ = bf16[656,256]{1,0:T(8,128)(2,1)S(1)} collective-permute-done((bf16[656,256]{1,0:T(8,128)(2,1)S(1)}, bf16[656,256]{1,0:T(8,128)(2,1)S(1)}, u32[]{:S(2)}, u32[]{:S(2)}) %collective-permute-start.11) | collective-permute-done | bytes 335904 | tf_op jit(solution)/shard_map/ppermute | solution.py:32
  70.8 2.4 %shard_map.95 = (bf16[3,64,320]{2,1,0:T(8,128)(2,1)S(1)}, bf16[3,64,320]{2,1,0:T(8,128)(2,1)S(1)}, bf16[3,64,320]{2,1,0:T(8,128)(2,1)S(1)}, bf16[3,64,320]{2,1,0:T(8,128)(2,1)S(1)}, bf16[256,320]{1,0:T(8,128)(2,1)S(1)}) custom-call(s32[4]{0:T(128)S(1)} %pad_add_fusion.place_ref.refs_0_, bf16[2,320,256]{2,1,0:T(8,128)(2,1)S(1)} %collective-permute-done.7.refs_1_, ...), custom_call_target="tpu_custom_call" | custom-call | flops 335544320 | bytes 1048576 | tf_op jit(solution)/shard_map/pallas_call | solution.py:56
  73.9 3.7 %collective-permute-start.13 = (bf16[3,64,320]{2,1,0:T(8,128)(2,1)S(1)}, bf16[3,64,320]{2,1,0:T(8,128)(2,1)S(1)}, u32[]{:S(2)}, u32[]{:S(2)}) collective-permute-start(bf16[3,64,320]{2,1,0:T(8,128)(2,1)S(1)} %get-tuple-element.41), channel_id=1, source_target_pairs={{0,8},{1,9},{2,10},{3,11},{4,16},{5,17},{6,18},{7,19},{8,12},{9,13... | collective-permute-start | bytes 368648 | tf_op jit(solution)/shard_map/ppermute | solution.py:32
  77.6 1.5 %collective-permute-start.14 = (bf16[3,64,320]{2,1,0:T(8,128)(2,1)S(1)}, bf16[3,64,320]{2,1,0:T(8,128)(2,1)S(1)}, u32[]{:S(2)}, u32[]{:S(2)}) collective-permute-start(bf16[3,64,320]{2,1,0:T(8,128)(2,1)S(1)} %get-tuple-element.42), channel_id=1, source_target_pairs={{0,16},{1,17},{2,18},{3,19},{4,24},{5,25},{6,26},{7,27},{8,20},{9,... | collective-permute-start | bytes 368648 | tf_op jit(solution)/shard_map/ppermute | solution.py:32
  79.4 5.8 %shard_map.97 = (bf16[64,320]{1,0:T(8,128)(2,1)S(1)}, bf16[64,320]{1,0:T(8,128)(2,1)S(1)}, bf16[64,320]{1,0:T(8,128)(2,1)S(1)}, bf16[64,320]{1,0:T(8,128)(2,1)S(1)}) custom-call(s32[4]{0:T(128)S(1)} %pad_add_fusion.place_ref.refs_0_, bf16[960,384]{1,0:T(8,128)(2,1)S(1)} %shard_map.96.mine, bf16[960,384]{1,0:T(8,128)(2,1)S(1)} %collective-permute-done.17.other, ...), custom_call_target="tpu_custom_call" | custom-call | flops 1769472000 | bytes 1048576 | tf_op jit(solution)/shard_map/pallas_call | solution.py:56
  85.9 4.0 %collective-permute-start.19 = (bf16[64,320]{1,0:T(8,128)(2,1)S(1)}, bf16[64,320]{1,0:T(8,128)(2,1)S(1)}, u32[]{:S(2)}, u32[]{:S(2)}) collective-permute-start(bf16[64,320]{1,0:T(8,128)(2,1)S(1)} %get-tuple-element.46), channel_id=1, source_target_pairs={{0,8},{1,9},{2,10},{3,11},{4,16},{5,17},{6,18},{7,19},{8,12},{9,13... | collective-permute-start | bytes 122888 | tf_op jit(solution)/shard_map/ppermute | solution.py:32
  90.4 2.2 %collective-permute-start.21 = (bf16[64,320]{1,0:T(8,128)(2,1)S(1)}, bf16[64,320]{1,0:T(8,128)(2,1)S(1)}, u32[]{:S(2)}, u32[]{:S(2)}) collective-permute-start(bf16[64,320]{1,0:T(8,128)(2,1)S(1)} %get-tuple-element.48), channel_id=1, source_target_pairs={{0,24},{1,25},{2,26},{3,27},{4,0},{5,1},{6,2},{7,3},{8,28},{9,29},... | collective-permute-start | bytes 122888 | tf_op jit(solution)/shard_map/ppermute | solution.py:32
  92.7 1.6 %collective-permute-done.19.refs_5_ = bf16[64,320]{1,0:T(8,128)(2,1)S(1)} collective-permute-done((bf16[64,320]{1,0:T(8,128)(2,1)S(1)}, bf16[64,320]{1,0:T(8,128)(2,1)S(1)}, u32[]{:S(2)}, u32[]{:S(2)}) %collective-permute-start.19) | collective-permute-done | bytes 40992 | tf_op jit(solution)/shard_map/ppermute | solution.py:32
  94.5 0.9 collective-permute-done.21.refs_7_
  95.4 1.5 %shard_map.98 = f32[2,1,64,1280]{3,2,1,0:T(8,128)} custom-call(s32[1]{0:T(128)} %bitcast.me_ref, f32[2,1280]{1,0:T(2,128)S(1)} %copy-done.3, bf16[3,64,320]{2,1,0:T(8,128)(2,1)S(1)} %collective-permute-done.12.refs_0_, bf16[3,64,320]{2,1,0:T(8,128)(2,1)S(1)} %collective-permute-done.13.refs_1_, bf16[3,64,320]{2,1,0:T(8,128)(2,1)S(1)} %collective-permute-done.14.refs_2_, ...), custom_call_target="tpu_custom_call" | custom-call | bytes 1048576 | tf_op jit(solution)/shard_map/pallas_call | solution.py:56
  (35 shorter events, 3.7 us)
Async XLA Ops:
  0.7 2.8 %copy-start = (bf16[1,320,320]{2,1,0:T(8,128)(2,1)S(1)}, bf16[1,320,320]{2,1,0:T(8,128)(2,1)}, u32[]{:S(2)}) copy-start(bf16[1,320,320]{2,1,0:T(8,128)(2,1)} %param.13) | copy-start | bytes 614404
  0.7 2.8 %copy-start.1 = (bf16[1,320,320]{2,1,0:T(8,128)(2,1)S(1)}, bf16[1,320,320]{2,1,0:T(8,128)(2,1)}, u32[]{:S(2)}) copy-start(bf16[1,320,320]{2,1,0:T(8,128)(2,1)} %param.14) | copy-start | bytes 614404
  3.5 0.9 copy-start.2
  4.4 2.6 %copy-start.5 = (bf16[656,256]{1,0:T(8,128)(2,1)S(1)}, bf16[656,256]{1,0:T(8,128)(2,1)}, u32[]{:S(2)}) copy-start(bf16[656,256]{1,0:T(8,128)(2,1)} %get-tuple-element.27) | copy-start | bytes 1007620
  4.4 3.3 %copy-start.4 = (bf16[656,256]{1,0:T(8,128)(2,1)S(1)}, bf16[656,256]{1,0:T(8,128)(2,1)}, u32[]{:S(2)}) copy-start(bf16[656,256]{1,0:T(8,128)(2,1)} %get-tuple-element.28) | copy-start | bytes 1007620
  4.6 25.6 %collective-permute-start.5 = (bf16[960,384]{1,0:T(8,128)(2,1)S(1)}, bf16[960,384]{1,0:T(8,128)(2,1)S(1)}, u32[]{:S(2)}, u32[]{:S(2)}) collective-permute-start(bf16[960,384]{1,0:T(8,128)(2,1)S(1)} %shard_map.92.refs_4_), channel_id=1, source_target_pairs={{0,8},{1,9},{2,10},{3,11},{12,4},{13,5},{14,6},{15,7},{16,24},{17,... | collective-permute-start | bytes 2211848 | tf_op jit(solution)/shard_map/ppermute | solution.py:32
  7.0 1.4 %collective-permute-start = (bf16[656,256]{1,0:T(8,128)(2,1)S(1)}, bf16[656,256]{1,0:T(8,128)(2,1)S(1)}, u32[]{:S(2)}, u32[]{:S(2)}) collective-permute-start(bf16[656,256]{1,0:T(8,128)(2,1)S(1)} %copy-done.5), channel_id=1, source_target_pairs={{0,0},{1,1},{2,2},{3,3},{4,8},{5,9},{6,10},{7,11},{8,4},{9,5},{10,... | collective-permute-start | bytes 1007624 | tf_op jit(solution)/shard_map/ppermute | solution.py:32
  7.7 4.8 %collective-permute-start.4 = (bf16[656,256]{1,0:T(8,128)(2,1)S(1)}, bf16[656,256]{1,0:T(8,128)(2,1)S(1)}, u32[]{:S(2)}, u32[]{:S(2)}) collective-permute-start(bf16[656,256]{1,0:T(8,128)(2,1)S(1)} %copy-done.4), channel_id=1, source_target_pairs={{0,0},{1,1},{2,2},{3,3},{4,8},{5,9},{6,10},{7,11},{8,4},{9,5},{10,... | collective-permute-start | bytes 1007624 | tf_op jit(solution)/shard_map/ppermute | solution.py:32
  8.4 7.6 %collective-permute-start.1 = (bf16[656,256]{1,0:T(8,128)(2,1)S(1)}, bf16[656,256]{1,0:T(8,128)(2,1)S(1)}, u32[]{:S(2)}, u32[]{:S(2)}) collective-permute-start(bf16[656,256]{1,0:T(8,128)(2,1)S(1)} %collective-permute-done.refs_0_.block.refs_3_), channel_id=1, source_target_pairs={{0,1},{1,0},{2,3},{3,2},{4,5},{5,4},{6,7},{7,6},{8,9},{9,8},{10,11... | collective-permute-start | bytes 1007624 | tf_op jit(solution)/shard_map/ppermute | solution.py:32
  10.8 9.9 %collective-permute-start.2 = (bf16[656,256]{1,0:T(8,128)(2,1)S(1)}, bf16[656,256]{1,0:T(8,128)(2,1)S(1)}, u32[]{:S(2)}, u32[]{:S(2)}) collective-permute-start(bf16[656,256]{1,0:T(8,128)(2,1)S(1)} %collective-permute-done.refs_0_.block.refs_3_), channel_id=1, source_target_pairs={{0,2},{1,3},{2,0},{3,1},{4,6},{5,7},{6,4},{7,5},{8,10},{9,11},{10,... | collective-permute-start | bytes 1007624 | tf_op jit(solution)/shard_map/ppermute | solution.py:32
  12.4 17.8 %collective-permute-start.3 = (bf16[656,256]{1,0:T(8,128)(2,1)S(1)}, bf16[656,256]{1,0:T(8,128)(2,1)S(1)}, u32[]{:S(2)}, u32[]{:S(2)}) collective-permute-start(bf16[656,256]{1,0:T(8,128)(2,1)S(1)} %collective-permute-done.refs_0_.block.refs_3_), channel_id=1, source_target_pairs={{0,3},{1,2},{2,1},{3,0},{4,7},{5,6},{6,5},{7,4},{8,11},{9,10},{10,... | collective-permute-start | bytes 1007624 | tf_op jit(solution)/shard_map/ppermute | solution.py:32
  12.5 26.3 %copy-start.6 = (bf16[2,256,320]{1,2,0:T(8,128)(2,1)S(1)}, bf16[2,256,320]{1,2,0:T(8,128)(2,1)}, u32[]{:S(2)}) copy-start(bf16[2,256,320]{1,2,0:T(8,128)(2,1)} %param.9) | copy-start | bytes 983044
  33.6 9.5 %collective-permute-start.6 = (bf16[960,384]{1,0:T(8,128)(2,1)S(1)}, bf16[960,384]{1,0:T(8,128)(2,1)S(1)}, u32[]{:S(2)}, u32[]{:S(2)}) collective-permute-start(bf16[960,384]{1,0:T(8,128)(2,1)S(1)} %get-tuple-element.36.mine), channel_id=1, source_target_pairs={{0,8},{1,9},{2,10},{3,11},{4,12},{5,13},{6,14},{7,15},{8,0},{9,1},... | collective-permute-start | bytes 2211848 | tf_op jit(solution)/shard_map/ppermute | solution.py:32
  38.8 4.2 %collective-permute-start.7 = (bf16[2,320,256]{2,1,0:T(8,128)(2,1)S(1)}, bf16[2,320,256]{2,1,0:T(8,128)(2,1)S(1)}, u32[]{:S(2)}, u32[]{:S(2)}) collective-permute-start(bf16[2,320,256]{2,1,0:T(8,128)(2,1)S(1)} %bitcast.16), channel_id=1, source_target_pairs={{0,0},{1,1},{2,2},{3,3},{4,8},{5,9},{6,10},{7,11},{8,4},{9,5},{10,... | collective-permute-start | bytes 983048 | tf_op jit(solution)/shard_map/ppermute | solution.py:32
  39.5 10.1 %collective-permute-start.9 = (bf16[656,256]{1,0:T(8,128)(2,1)S(1)}, bf16[656,256]{1,0:T(8,128)(2,1)S(1)}, u32[]{:S(2)}, u32[]{:S(2)}) collective-permute-start(bf16[656,256]{1,0:T(8,128)(2,1)S(1)} %collective-permute-done.4.refs_4_.refs_0_.block), channel_id=1, source_target_pairs={{0,1},{1,0},{2,3},{3,2},{4,5},{5,4},{6,7},{7,6},{8,9},{9,8},{10,11... | collective-permute-start | bytes 1007624 | tf_op jit(solution)/shard_map/ppermute | solution.py:32
  40.5 14.8 %collective-permute-start.10 = (bf16[656,256]{1,0:T(8,128)(2,1)S(1)}, bf16[656,256]{1,0:T(8,128)(2,1)S(1)}, u32[]{:S(2)}, u32[]{:S(2)}) collective-permute-start(bf16[656,256]{1,0:T(8,128)(2,1)S(1)} %collective-permute-done.4.refs_4_.refs_0_.block), channel_id=1, source_target_pairs={{0,3},{1,2},{2,1},{3,0},{4,7},{5,6},{6,5},{7,4},{8,11},{9,10},{10,... | collective-permute-start | bytes 1007624 | tf_op jit(solution)/shard_map/ppermute | solution.py:32
  42.9 18.7 %collective-permute-start.16 = (bf16[656,256]{1,0:T(8,128)(2,1)S(1)}, bf16[656,256]{1,0:T(8,128)(2,1)S(1)}, u32[]{:S(2)}, u32[]{:S(2)}) collective-permute-start(bf16[656,256]{1,0:T(8,128)(2,1)S(1)} %collective-permute-done.4.refs_4_.refs_0_.block), channel_id=1, source_target_pairs={{0,2},{1,3},{2,0},{3,1},{4,6},{5,7},{6,4},{7,5},{8,10},{9,11},{10,... | collective-permute-start | bytes 1007624 | tf_op jit(solution)/shard_map/ppermute | solution.py:32
  64.4 15.0 %collective-permute-start.17 = (bf16[960,384]{1,0:T(8,128)(2,1)S(1)}, bf16[960,384]{1,0:T(8,128)(2,1)S(1)}, u32[]{:S(2)}, u32[]{:S(2)}) collective-permute-start(bf16[960,384]{1,0:T(8,128)(2,1)S(1)} %shard_map.96.mine), channel_id=1, source_target_pairs={{0,8},{1,9},{2,10},{3,11},{4,12},{5,13},{6,14},{7,15},{8,0},{9,1},... | collective-permute-start | bytes 2211848 | tf_op jit(solution)/shard_map/ppermute | solution.py:32
  65.2 4.5 %collective-permute-start.8 = (bf16[656,256]{1,0:T(8,128)(2,1)S(1)}, bf16[656,256]{1,0:T(8,128)(2,1)S(1)}, u32[]{:S(2)}, u32[]{:S(2)}) collective-permute-start(bf16[656,256]{1,0:T(8,128)(2,1)S(1)} %collective-permute-done.3.refs_3_.refs_6_), channel_id=1, source_target_pairs={{0,8},{4,12},{8,0},{12,4},{16,24},{20,28},{24,16},{28,20}} | collective-permute-start | bytes 1007624 | tf_op jit(solution)/shard_map/ppermute | solution.py:32
  67.1 3.6 %collective-permute-start.11 = (bf16[656,256]{1,0:T(8,128)(2,1)S(1)}, bf16[656,256]{1,0:T(8,128)(2,1)S(1)}, u32[]{:S(2)}, u32[]{:S(2)}) collective-permute-start(bf16[656,256]{1,0:T(8,128)(2,1)S(1)} %collective-permute-done.10.refs_9_.refs_3_), channel_id=1, source_target_pairs={{0,8},{4,12},{8,0},{12,4},{16,24},{20,28},{24,16},{28,20}} | collective-permute-start | bytes 1007624 | tf_op jit(solution)/shard_map/ppermute | solution.py:32
  73.2 12.7 %collective-permute-start.12 = (bf16[3,64,320]{2,1,0:T(8,128)(2,1)S(1)}, bf16[3,64,320]{2,1,0:T(8,128)(2,1)S(1)}, u32[]{:S(2)}, u32[]{:S(2)}) collective-permute-start(bf16[3,64,320]{2,1,0:T(8,128)(2,1)S(1)} %get-tuple-element.40), channel_id=1, source_target_pairs={{0,0},{1,1},{2,2},{3,3},{4,8},{5,9},{6,10},{7,11},{8,4},{9,5},{10,... | collective-permute-start | bytes 368648 | tf_op jit(solution)/shard_map/ppermute | solution.py:32
  73.9 16.0 %collective-permute-start.13 = (bf16[3,64,320]{2,1,0:T(8,128)(2,1)S(1)}, bf16[3,64,320]{2,1,0:T(8,128)(2,1)S(1)}, u32[]{:S(2)}, u32[]{:S(2)}) collective-permute-start(bf16[3,64,320]{2,1,0:T(8,128)(2,1)S(1)} %get-tuple-element.41), channel_id=1, source_target_pairs={{0,8},{1,9},{2,10},{3,11},{4,16},{5,17},{6,18},{7,19},{8,12},{9,13... | collective-permute-start | bytes 368648 | tf_op jit(solution)/shard_map/ppermute | solution.py:32
  77.6 12.9 %collective-permute-start.14 = (bf16[3,64,320]{2,1,0:T(8,128)(2,1)S(1)}, bf16[3,64,320]{2,1,0:T(8,128)(2,1)S(1)}, u32[]{:S(2)}, u32[]{:S(2)}) collective-permute-start(bf16[3,64,320]{2,1,0:T(8,128)(2,1)S(1)} %get-tuple-element.42), channel_id=1, source_target_pairs={{0,16},{1,17},{2,18},{3,19},{4,24},{5,25},{6,26},{7,27},{8,20},{9,... | collective-permute-start | bytes 368648 | tf_op jit(solution)/shard_map/ppermute | solution.py:32
  79.1 13.6 %collective-permute-start.15 = (bf16[3,64,320]{2,1,0:T(8,128)(2,1)S(1)}, bf16[3,64,320]{2,1,0:T(8,128)(2,1)S(1)}, u32[]{:S(2)}, u32[]{:S(2)}) collective-permute-start(bf16[3,64,320]{2,1,0:T(8,128)(2,1)S(1)} %get-tuple-element.43), channel_id=1, source_target_pairs={{0,24},{1,25},{2,26},{3,27},{4,0},{5,1},{6,2},{7,3},{8,28},{9,29},... | collective-permute-start | bytes 368648 | tf_op jit(solution)/shard_map/ppermute | solution.py:32
  79.4 16.0 %copy-start.3 = (f32[2,1280]{1,0:T(2,128)S(1)}, f32[2,1280]{1,0:T(2,128)}, u32[]{:S(2)}) copy-start(f32[2,1280]{1,0:T(2,128)} %gain_ref.1) | copy-start | bytes 30724
  85.2 7.4 %collective-permute-start.18 = (bf16[64,320]{1,0:T(8,128)(2,1)S(1)}, bf16[64,320]{1,0:T(8,128)(2,1)S(1)}, u32[]{:S(2)}, u32[]{:S(2)}) collective-permute-start(bf16[64,320]{1,0:T(8,128)(2,1)S(1)} %get-tuple-element.45), channel_id=1, source_target_pairs={{0,0},{1,1},{2,2},{3,3},{4,8},{5,9},{6,10},{7,11},{8,4},{9,5},{10,... | collective-permute-start | bytes 122888 | tf_op jit(solution)/shard_map/ppermute | solution.py:32
  85.9 8.3 %collective-permute-start.19 = (bf16[64,320]{1,0:T(8,128)(2,1)S(1)}, bf16[64,320]{1,0:T(8,128)(2,1)S(1)}, u32[]{:S(2)}, u32[]{:S(2)}) collective-permute-start(bf16[64,320]{1,0:T(8,128)(2,1)S(1)} %get-tuple-element.46), channel_id=1, source_target_pairs={{0,8},{1,9},{2,10},{3,11},{4,16},{5,17},{6,18},{7,19},{8,12},{9,13... | collective-permute-start | bytes 122888 | tf_op jit(solution)/shard_map/ppermute | solution.py:32
  89.9 4.6 %collective-permute-start.20 = (bf16[64,320]{1,0:T(8,128)(2,1)S(1)}, bf16[64,320]{1,0:T(8,128)(2,1)S(1)}, u32[]{:S(2)}, u32[]{:S(2)}) collective-permute-start(bf16[64,320]{1,0:T(8,128)(2,1)S(1)} %get-tuple-element.47), channel_id=1, source_target_pairs={{0,16},{1,17},{2,18},{3,19},{4,24},{5,25},{6,26},{7,27},{8,20},{9,... | collective-permute-start | bytes 122888 | tf_op jit(solution)/shard_map/ppermute | solution.py:32
  90.4 5.0 %collective-permute-start.21 = (bf16[64,320]{1,0:T(8,128)(2,1)S(1)}, bf16[64,320]{1,0:T(8,128)(2,1)S(1)}, u32[]{:S(2)}, u32[]{:S(2)}) collective-permute-start(bf16[64,320]{1,0:T(8,128)(2,1)S(1)} %get-tuple-element.48), channel_id=1, source_target_pairs={{0,24},{1,25},{2,26},{3,27},{4,0},{5,1},{6,2},{7,3},{8,28},{9,29},... | collective-permute-start | bytes 122888 | tf_op jit(solution)/shard_map/ppermute | solution.py:32

commit v3 on v2

--- a/solution.py
+++ b/solution.py
@@ -32,8 +32,13 @@
     return lax.ppermute(array, BOTH, pairs)
 
 
-def after(arrays, others):
-    return lax.optimization_barrier((arrays, others))[0]
+def hold_kernel(in_ref, out_ref):
+    out_ref[...] = in_ref[...]
+
+
+def tied(array, *others):
+    shape = jax.ShapeDtypeStruct(array.shape, array.dtype)
+    return call(hold_kernel, shape, (array,), waits=others)
 
 
 def turned(array):
@@ -48,26 +53,54 @@
     return lax.dot_general(left, right, (((1,), (1,)), ((), ())), preferred_element_type=F32)
 
 
-def call(kernel, out_shape, args, scratch=(), smem=(), loose=(), vmem=VMEM_BYTES, flops=0):
+def call(
+    kernel,
+    out_shape,
+    args,
+    scratch=(),
+    smem=(),
+    loose=(),
+    loose_out=(),
+    aliases={},
+    waits=(),
+    vmem=VMEM_BYTES,
+    flops=0,
+):
     def space(i):
         return pltpu.SMEM if i in smem else pl.ANY if i in loose else pltpu.VMEM
 
-    specs = [pl.BlockSpec(memory_space=space(i)) for i in range(len(args))]
-    return pl.pallas_call(
-        kernel,
-        out_shape=out_shape,
+    count = len(args)
+    specs = [pl.BlockSpec(memory_space=space(i)) for i in range(count)]
+    specs += [pl.BlockSpec(memory_space=pltpu.VMEM) for _ in waits]
+    single = not isinstance(out_shape, tuple)
+    shapes = (out_shape,) if single else out_shape
+
+    def body(*refs):
+        kernel(*refs[:count], *refs[count + len(waits) :])
+
+    outs = pl.pallas_call(
+        body,
+        out_shape=shapes,
         in_specs=specs,
-        out_specs=jax.tree.map(lambda _: pl.BlockSpec(memory_space=pltpu.VMEM), out_shape),
+        out_specs=tuple(
+            pl.BlockSpec(memory_space=pl.ANY if i in loose_out else pltpu.VMEM)
+            for i in range(len(shapes))
+        ),
         scratch_shapes=list(scratch),
+        input_output_aliases=aliases,
         compiler_params=pltpu.CompilerParams(vmem_limit_bytes=vmem),
         cost_estimate=pl.CostEstimate(flops=flops, bytes_accessed=1 << 20, transcendentals=0),
-    )(*args)
+    )(*args, *waits)
+    return outs[0] if single else outs
 
 
 def pack_kernel(segments, key_ref, value_ref, rate_ref, step_ref, *refs):
-    outs, sems = refs[:segments], refs[segments]
+    outs, (held_rate, held_step, sems) = refs[:segments], refs[segments:]
     width, rows = key_ref.shape[1:]
-    copies = []
+    copies = [
+        pltpu.make_async_copy(rate_ref, held_rate, sems.at[segments, 0]),
+        pltpu.make_async_copy(step_ref, held_step, sems.at[segments, 1]),
+    ]
     for s, out_ref in enumerate(outs):
         for i, ref in enumerate((key_ref, value_ref)):
             copies.append(
@@ -77,9 +110,11 @@
             )
     for copy in copies:
         copy.start()
+    for copy in copies[:2]:
+        copy.wait()
     for s, out_ref in enumerate(outs):
-        rate = rate_ref[s]
-        step = jnp.full_like(rate, step_ref[0])
+        rate = held_rate[s]
+        step = jnp.full_like(rate, held_step[0])
         row = lax.broadcasted_iota(jnp.int32, (EXTRA, rows), 0)
         filled = jnp.zeros((EXTRA, rows), F32)
         at = 0
@@ -90,21 +125,37 @@
                 value = value - term
                 at += 1
         out_ref[2 * width :] = filled.astype(BF16)
-    for copy in copies:
+    for copy in copies[2:]:
         copy.wait()
 
 
-def weight_kernel(gate_ref, up_ref, down_ref, out_ref):
-    width = down_ref.shape[0]
-    for i, ref in enumerate((gate_ref, up_ref)):
-        out_ref[i * width : (i + 1) * width, :width] = ref[...].T
-    out_ref[2 * width :, :width] = down_ref[...]
-    out_ref[:, width:] = jnp.zeros((3 * width, out_ref.shape[1] - width), BF16)
-
-
-def add_gradients(blocks, weights, total_ref):
+def weight_kernel(place_ref, *refs):
+    mine, other, (out_ref, held, sems) = refs[:3], refs[3:6], refs[6:]
+    width = out_ref.shape[1]
+
+    def load(parts):
+        copies = [
+            pltpu.make_async_copy(ref, held.at[i], sems.at[i]) for i, ref in enumerate(parts)
+        ]
+        for copy in copies:
+            copy.start()
+        for copy in copies:
+            copy.wait()
+
+    @pl.when(place_ref[3] == 1)
+    def _():
+        load(mine)
+
+    @pl.when(place_ref[3] != 1)
+    def _():
+        load(other)
+
+    for i in range(3):
+        out_ref[i * width : (i + 1) * width] = held[i].T if i < 2 else held[i]
+
+
+def add_gradients(blocks, weights, total_ref, first=True):
     width = weights.shape[1]
-    first = True
     for block in blocks:
         keys = block[:width]
         values = block[width : 2 * width]
@@ -125,10 +176,9 @@
         first = False
 
 
-def orthogonalized(stacked, width):
+def orthogonalized(totals):
     iterates = []
-    for i in range(3):
-        one = stacked[i * width : (i + 1) * width]
+    for one in totals:
         norm = jnp.sqrt(jnp.sum(one * one, keepdims=True))
         iterates.append((one / (norm + FROB_EPS)).astype(BF16))
     for _ in range(NS_STEPS):
@@ -147,16 +197,17 @@
     width = out_ref.shape[1]
     terms = step_block[2 * width :].astype(F32)
     step = (terms[3:4] + terms[4:5] + terms[5:6])[:, 0:1]
-    total = mine[:, :width].astype(F32) + other[:, :width].astype(F32)
-    for i, x in enumerate(orthogonalized(total, width)):
+    totals = [a[:, :width].astype(F32) + b[:, :width].astype(F32) for a, b in zip(mine, other)]
+    for i, x in enumerate(orthogonalized(totals)):
         at = pl.ds(i * width, width)
         out_ref[at] = (weights[at].astype(F32) - step * x.astype(F32)).astype(BF16)
 
 
-def write_sum(total_ref, out_ref):
+def write_sums(total_ref, outs):
     width = total_ref.shape[1]
-    out_ref[:, :width] = total_ref[...].astype(BF16)
-    out_ref[:, width:] = jnp.zeros((out_ref.shape[0], out_ref.shape[1] - width), BF16)
+    for i, out_ref in enumerate(outs):
+        out_ref[:, :width] = total_ref[i * width : (i + 1) * width].astype(BF16)
+        out_ref[:, width:] = jnp.zeros((width, out_ref.shape[1] - width), BF16)
 
 
 def fast_rows(query, weights):
@@ -167,28 +218,31 @@
     return dot_nn(hidden, weights[2 * width :]).astype(BF16)
 
 
-def first_kernel(count, place_ref, *refs):
-    blocks = refs[:count]
-    mine, other, held_ref, out_ref, total_ref = refs[count:]
-    width = held_ref.shape[1]
-    held_ref[...] = jnp.where(place_ref[3] == 1, mine[:, :width], other[:, :width])
-    add_gradients(blocks, held_ref, total_ref)
-    write_sum(total_ref, out_ref)
-
-
-def update_kernel(mine, other, weight_ref, block, next_ref):
-    updated(mine, other, weight_ref, block, next_ref)
+def first_kernel(count, *refs):
+    blocks, (weight_ref, total_ref) = refs[:count], refs[count:]
+    add_gradients(blocks, weight_ref, total_ref)
+
+
+def second_kernel(block, weight_ref, before_ref, *refs):
+    *outs, total_ref = refs
+    total_ref[...] = before_ref[...]
+    add_gradients((block,), weight_ref, total_ref, first=False)
+    write_sums(total_ref, outs)
+
+
+def update_kernel(*refs):
+    updated(refs[:3], refs[3:6], *refs[6:])
 
 
 def middle_kernel(count, *refs):
-    blocks, (weight_ref, out_ref, total_ref) = refs[:count], refs[count:]
+    blocks, (weight_ref, *outs, total_ref) = refs[:count], refs[count:]
     add_gradients(blocks, weight_ref, total_ref)
-    write_sum(total_ref, out_ref)
-
-
-def last_kernel(heads, place_ref, mine, other, weight_ref, block, query_ref, *refs):
-    outs, (next_ref, fast_ref) = refs[:heads], refs[heads:]
-    updated(mine, other, weight_ref, block, next_ref)
+    write_sums(total_ref, outs)
+
+
+def last_kernel(heads, place_ref, *refs):
+    weight_ref, block, query_ref, *outs, next_ref, fast_ref = refs[6:]
+    updated(refs[:3], refs[3:6], weight_ref, block, next_ref)
     fast_ref[...] = fast_rows(query_ref[...], next_ref)
     share = fast_ref.shape[0] // heads
     for shift in range(heads):
@@ -268,19 +322,36 @@
     ]
 
 
-def final_kernel(heads, segments, me_ref, gain_ref, *refs):
-    early, late, out_ref = refs[:heads], refs[heads : 2 * heads], refs[2 * heads]
-    held = refs[2 * heads + 1]
-    share, width = late[0].shape
+def early_kernel(heads, segments, me_ref, gain_ref, *refs):
+    early, (out_ref, last_ref, held, made, sem) = refs[:heads], refs[heads:]
+    width = held.shape[-1]
     me = me_ref[0]
     for k in range(heads):
-        at = lax.rem(me - k + heads, heads)
-        held[at, : 2 * segments - 1] = early[k][...]
-        held[at, 2 * segments - 1] = late[k][...]
+        held[lax.rem(me - k + heads, heads)] = early[k][...]
     for s in range(segments):
-        fast = normed([held[j, segments + s] for j in range(heads)], gain_ref[0:1], heads * width)
         att = normed([held[j, s] for j in range(heads)], gain_ref[1:2], heads * width)
-        out_ref[s, 0] = jnp.concatenate([a + b for a, b in zip(fast, att)], -1)
+        if s == segments - 1:
+            last_ref[...] = jnp.concatenate(att, -1)
+        else:
+            fast = [held[j, segments + s] for j in range(heads)]
+            fast = normed(fast, gain_ref[0:1], heads * width)
+            made[s, 0] = jnp.concatenate([a + b for a, b in zip(fast, att)], -1)
+    copy = pltpu.make_async_copy(made, out_ref.at[pl.ds(0, segments - 1)], sem)
+    copy.start()
+    copy.wait()
+
+
+def final_kernel(heads, segments, me_ref, gain_ref, out_in_ref, last_ref, *refs):
+    late, (out_ref, held, made, sem) = refs[:heads], refs[heads:]
+    width = held.shape[-1]
+    me = me_ref[0]
+    for k in range(heads):
+        held[lax.rem(me - k + heads, heads)] = late[k][...]
+    fast = normed([held[j] for j in range(heads)], gain_ref[0:1], heads * width)
+    made[0, 0] = jnp.concatenate(fast, -1) + last_ref[...]
+    copy = pltpu.make_async_copy(made, out_ref.at[pl.ds(segments - 1, 1)], sem)
+    copy.start()
+    copy.wait()
 
 
 def on_device(
@@ -307,8 +378,9 @@
     def other_core(h, t):
         return h ^ 1, t
 
-    def send(array, where):
-        return moved(array, heads, toks, where)
+    def send(array, where, name):
+        with jax.named_scope(name):
+            return moved(array, heads, toks, where)
 
     me = lax.axis_index("head")
     core = me % 2
@@ -324,66 +396,85 @@
         functools.partial(pack_kernel, segments),
         (block_shape,) * segments,
         (turned(key_rows), turned(value_rows), token_rates, step_size),
-        (pltpu.SemaphoreType.DMA((segments, 2)),),
-        smem=(3,),
-        loose=(0, 1),
+        (
+            pltpu.VMEM((segments, 1, rows), F32),
+            pltpu.SMEM((1,), F32),
+            pltpu.SemaphoreType.DMA((segments + 1, 2)),
+        ),
+        loose=(0, 1, 2, 3),
         vmem=56 * 1024 * 1024,
     )
-    own = [send(block, regroup) for block in blocks]
+    first = send(blocks[0], regroup, "regroup_0")
+    parts = [gate_weight[0], up_weight[0], down_weight[0]]
+    lent = [send(part, other_core, f"lend_{i}") for i, part in enumerate(parts)]
     padded = -(-width // 128) * 128
-    stacked = call(
+    weight_shape = jax.ShapeDtypeStruct((3 * width, width), BF16)
+    weights = call(
         weight_kernel,
-        jax.ShapeDtypeStruct((3 * width, padded), BF16),
-        after((gate_weight[0], up_weight[0], down_weight[0]), blocks),
-    )
-    lent = send(
-        stacked, lambda h, t: (h ^ 1, t) if h % 2 == t // half else None
-    )
-    queries = send(turned(query_rows), regroup)
+        weight_shape,
+        (position, *parts, *lent),
+        (pltpu.VMEM((3, width, width), BF16), pltpu.SemaphoreType.DMA((3,))),
+        smem=(0,),
+        loose=range(1, 7),
+        vmem=VMEM_BYTES,
+    )
+    own = [tied(first, weights)]
+    for s in range(1, segments):
+        own.append(send(tied(blocks[s], own[-1]), regroup, f"regroup_{s}"))
+    queries = send(turned(query_rows), regroup, "regroup_queries")
 
     here = []
     for s in range(segments):
-        here.append(
-            [own[s]]
-            + [
-                send(own[s], lambda h, t, mask=mask: (h, t ^ mask)) for mask in range(1, half)
-            ]
-        )
-
-    grad_shape = jax.ShapeDtypeStruct((3 * width, padded), BF16)
-    weight_shape = jax.ShapeDtypeStruct((3 * width, width), BF16)
+        got = {0: tied(own[s], gate) if s else own[s]}
+        step = half // 2
+        while step:
+            for mask in sorted(got):
+                block = got[mask]
+                if s == 0 and mask and step == 1:
+                    block = gate = tied(block, got[1])
+                got[mask | step] = send(
+                    block,
+                    lambda h, t, step=step: (h, t ^ step),
+                    f"gather_{s}_{mask | step}",
+                )
+            step //= 2
+        here.append([got[mask] for mask in range(half)])
+
+    grad_shapes = (jax.ShapeDtypeStruct((width, padded), BF16),) * 3
     total = pltpu.VMEM((3 * width, width), F32)
     grad_flops = 2 * 6 * half * rows * width * width
     ns_flops = 2 * 27 * width**3
 
-    weights, mine = call(
-        functools.partial(first_kernel, half),
-        (weight_shape, grad_shape),
-        (position, *after(here[0], own), stacked, lent),
-        (total,),
-        smem=(0,),
+    before = call(
+        functools.partial(first_kernel, half - 1),
+        jax.ShapeDtypeStruct((3 * width, width), F32),
+        (*here[0][:-1], weights),
+        waits=own[1:],
         flops=grad_flops,
     )
+    mine = call(second_kernel, grad_shapes, (here[0][-1], weights, before), (total,))
     all_weights = []
     for s in range(1, segments):
-        other = send(mine, other_core)
-        if s == 1:
-            other, queries = lax.optimization_barrier((other, queries))
+        other = [send(one, other_core, f"swap_{s - 1}") for one in mine]
         weights = call(
-            update_kernel, weight_shape, (mine, other, weights, own[s - 1]), flops=ns_flops
+            update_kernel,
+            weight_shape,
+            (*mine, *other, weights, own[s - 1]),
+            waits=(queries,),
+            flops=ns_flops,
         )
         mine = call(
             functools.partial(middle_kernel, half),
-            grad_shape,
+            grad_shapes,
             (*here[s], weights),
             (total,),
             flops=grad_flops,
         )
         all_weights.append(weights)
-    other = send(mine, other_core)
+    other = [send(one, other_core, f"swap_{segments - 1}") for one in mine]
 
     lasts = [
-        send(here[s][half - 1], lambda h, t: (h ^ 1, t) if t % half == 0 else None)
+        send(here[s][half - 1], other_core, f"last_{s}")
         for s in range(segments)
     ]
     cands = []
@@ -409,13 +500,13 @@
     late = call(
         functools.partial(last_kernel, heads),
         tuple(jax.ShapeDtypeStruct((share, width), BF16) for _ in range(heads)),
-        (position, mine, other, weights, own[-1], last_query),
+        (position, *mine, *other, weights, own[-1], last_query),
         (pltpu.VMEM((3 * width, width), BF16), pltpu.VMEM((rows, width), BF16)),
         smem=(0,),
         flops=ns_flops,
     )
 
-    def spread(parts):
+    def spread(parts, name):
         got = []
         for shift in range(heads):
 
@@ -423,15 +514,36 @@
                 mine = h - h % 2 + t // half
                 return (mine + shift) % heads, (h % 2) * half + t % half
 
-            got.append(send(parts[shift], where))
+            got.append(send(parts[shift], where, f"{name}_{shift}"))
         return got
 
+    mine_at = me[None].astype(jnp.int32)
+    out_shape = jax.ShapeDtypeStruct((segments, 1, share, heads * width), F32)
+    begun, last = call(
+        functools.partial(early_kernel, heads, segments),
+        (out_shape, jax.ShapeDtypeStruct((share, heads * width), F32)),
+        (mine_at, branch_gains, *spread(early, "spread_early")),
+        (
+            pltpu.VMEM((heads, 2 * segments - 1, share, width), BF16),
+            pltpu.VMEM((segments - 1, 1, share, heads * width), F32),
+            pltpu.SemaphoreType.DMA,
+        ),
+        smem=(0,),
+        loose_out=(0,),
+    )
     return call(
         functools.partial(final_kernel, heads, segments),
-        jax.ShapeDtypeStruct((segments, 1, share, heads * width), F32),
-        (me[None].astype(jnp.int32), branch_gains, *spread(early), *spread(late)),
-        (pltpu.VMEM((heads, 2 * segments, share, width), BF16),),
+        out_shape,
+        (mine_at, branch_gains, begun, last, *spread(late, "spread_late")),
+        (
+            pltpu.VMEM((heads, share, width), BF16),
+            pltpu.VMEM((1, 1, share, heads * width), F32),
+            pltpu.SemaphoreType.DMA,
+        ),
         smem=(0,),
+        loose=(2,),
+        loose_out=(0,),
+        aliases={2: 0},
     )
 
 

time: 97.3 us -> 84.9 us (0.87)
  waiting for transfers between devices: 35.4 us -> 18.7 us
  local copies, waits for them, and re-layouts: 0.96 us -> 2.85 us
  Pallas kernels: 23.6 us -> 25 us
    ppermute x22 -> x28, waiting for transfers between devices: 35.4 us -> 18.7 us  [moved(): return lax.ppermute(array, BOTH, pairs)]
    unnamed x14 -> x12, local copies, waits for them, and re-layouts: 0.96 us -> 2.85 us
    pallas_call x8 -> x14, Pallas kernels: 23.6 us -> 25 us  [call(): pl.pallas_call(body, out_shape=shapes, in_specs=specs, out_specs=tuple((p...]
    ppermute x22 -> x28, starting transfers between devices: 36.1 us -> 37 us  [moved(): return lax.ppermute(array, BOTH, pairs)]
  transfers between devices with their start and end apart: 22 -> 28, of which waited for: 10 -> 9; matrix products, arithmetic and copies ran while one was open for 0% -> 0% of each run, Pallas kernels for 13% -> 26%
where the time goes in v3:
time: 84.9 us; the launch traced here: 84.6 us
  starting transfers between devices  37 us (44%)
  Pallas kernels  25 us (29%)
  waiting for transfers between devices  18.7 us (22%)
  local copies, waits for them, and re-layouts  2.85 us (3%)
  between operations  1.02 us (1%)
    ppermute x28, starting transfers between devices, moved(): return lax.ppermute(array, BOTH, pairs)  37 us
    pallas_call x14, Pallas kernels, call(): pl.pallas_call(body, out_shape=shapes, in_specs=specs, out_specs=tuple((p...  25 us
    ppermute x28, waiting for transfers between devices, moved(): return lax.ppermute(array, BOTH, pairs)  18.7 us
    unnamed x12, local copies, waits for them, and re-layouts  2.85 us
  transfers between devices with their start and end apart: 28, of which 9 were waited for; matrix products, arithmetic and copies ran while one was open for 0% of the time, Pallas kernels for 26%

profile of v3, /device:TPU:0, one launch (start us, length us, event | category | flops | bytes accessed | tf_op | source)
XLA Modules:
  0.0 84.6 jit_solution(10500724518430432525)
XLA Ops:
  0.7 2.1 %shard_map.91 = (bf16[656,256]{1,0:T(8,128)(2,1)}, bf16[656,256]{1,0:T(8,128)(2,1)}) custom-call(bf16[2,320,256]{2,1,0:T(8,128)(2,1)} %bitcast.17, bf16[2,320,256]{2,1,0:T(8,128)(2,1)} %bitcast.18, f32[2,1,256]{2,1,0:T(1,128)} %refs_2_.1, f32[1]{0:T(128)S(6)} %copy.12.refs_3_), custom_call_target="tpu_custom_call" | custom-call | bytes 1048576 | tf_op jit(solution)/shard_map/pallas_call | solution.py:81
  2.7 1.6 %collective-permute-start.1 = (bf16[656,256]{1,0:T(8,128)(2,1)}, bf16[656,256]{1,0:T(8,128)(2,1)S(1)}, u32[]{:S(2)}, u32[]{:S(2)}) collective-permute-start(bf16[656,256]{1,0:T(8,128)(2,1)} %get-tuple-element.24), channel_id=1, source_target_pairs={{0,0},{1,1},{2,2},{3,3},{4,8},{5,9},{6,10},{7,11},{8,4},{9,5},{10,... | collective-permute-start | bytes 1007624 | tf_op jit(solution)/shard_map/regroup_0/ppermute | solution.py:32
  4.4 4.5 %collective-permute-start.2 = (bf16[320,320]{1,0:T(8,128)(2,1)}, bf16[320,320]{1,0:T(8,128)(2,1)S(1)}, u32[]{:S(2)}, u32[]{:S(2)}) collective-permute-start(bf16[320,320]{1,0:T(8,128)(2,1)} %bitcast.11), channel_id=1, source_target_pairs={{0,8},{1,9},{2,10},{3,11},{4,12},{5,13},{6,14},{7,15},{8,0},{9,1},... | collective-permute-start | bytes 614408 | tf_op jit(solution)/shard_map/lend_0/ppermute | solution.py:32
  10.9 0.9 %copy-done.1 = bf16[1,320,320]{2,1,0:T(8,128)(2,1)S(1)} copy-done((bf16[1,320,320]{2,1,0:T(8,128)(2,1)S(1)}, bf16[1,320,320]{2,1,0:T(8,128)(2,1)}, u32[]{:S(2)}) %copy-start.1) | copy-done | bytes 204824
  11.9 0.9 %copy-done.2 = bf16[1,320,320]{2,1,0:T(8,128)(2,1)S(1)} copy-done((bf16[1,320,320]{2,1,0:T(8,128)(2,1)S(1)}, bf16[1,320,320]{2,1,0:T(8,128)(2,1)}, u32[]{:S(2)}) %copy-start.2) | copy-done | bytes 204824
  12.8 0.9 %copy-done.3 = bf16[1,320,320]{2,1,0:T(8,128)(2,1)S(1)} copy-done((bf16[1,320,320]{2,1,0:T(8,128)(2,1)S(1)}, bf16[1,320,320]{2,1,0:T(8,128)(2,1)}, u32[]{:S(2)}) %copy-start.3) | copy-done | bytes 204824
  13.8 1.7 %shard_map.92.refs_1_.refs_3_.refs_6_ = bf16[960,320]{1,0:T(8,128)(2,1)S(1)} custom-call(s32[4]{0:T(128)S(1)} %pad_add_fusion.refs_0_, bf16[320,320]{1,0:T(8,128)(2,1)S(1)} %bitcast.12, bf16[320,320]{1,0:T(8,128)(2,1)S(1)} %bitcast.14, bf16[320,320]{1,0:T(8,128)(2,1)S(1)} %bitcast.16, bf16[320,320]{1,0:T(8,128)(2,1)S(1)} %collective-permute-done.2.refs_4_, ...), custom_call_target="tpu_custom_call" | custom-call | bytes 1048576 | tf_op jit(solution)/shard_map/pallas_call | solution.py:81
  15.6 1.6 %collective-permute-start.5 = (bf16[656,256]{1,0:T(8,128)(2,1)S(1)}, bf16[656,256]{1,0:T(8,128)(2,1)S(1)}, u32[]{:S(2)}, u32[]{:S(2)}) collective-permute-start(bf16[656,256]{1,0:T(8,128)(2,1)S(1)} %shard_map.93.refs_1_.refs_0_.refs_7_.refs_3_), channel_id=1, source_target_pairs={{0,2},{1,3},{2,0},{3,1},{4,6},{5,7},{6,4},{7,5},{8,10},{9,11},{10,... | collective-permute-start | bytes 1007624 | tf_op jit(solution)/shard_map/gather_0_2/ppermute | solution.py:32
  17.2 1.5 %collective-permute-start.6 = (bf16[656,256]{1,0:T(8,128)(2,1)S(1)}, bf16[656,256]{1,0:T(8,128)(2,1)S(1)}, u32[]{:S(2)}, u32[]{:S(2)}) collective-permute-start(bf16[656,256]{1,0:T(8,128)(2,1)S(1)} %shard_map.93.refs_1_.refs_0_.refs_7_.refs_3_), channel_id=1, source_target_pairs={{0,1},{1,0},{2,3},{3,2},{4,5},{5,4},{6,7},{7,6},{8,9},{9,8},{10,11... | collective-permute-start | bytes 1007624 | tf_op jit(solution)/shard_map/gather_0_1/ppermute | solution.py:32
  18.7 0.8 collective-permute-start.8
  19.6 5.9 %collective-permute-done.5.refs_0_.refs_2_ = bf16[656,256]{1,0:T(8,128)(2,1)S(1)} collective-permute-done((bf16[656,256]{1,0:T(8,128)(2,1)S(1)}, bf16[656,256]{1,0:T(8,128)(2,1)S(1)}, u32[]{:S(2)}, u32[]{:S(2)}) %collective-permute-start.5) | collective-permute-done | bytes 335904 | tf_op jit(solution)/shard_map/gather_0_2/ppermute | solution.py:32
  25.5 2.4 %collective-permute-done.6.refs_1_.refs_5_ = bf16[656,256]{1,0:T(8,128)(2,1)S(1)} collective-permute-done((bf16[656,256]{1,0:T(8,128)(2,1)S(1)}, bf16[656,256]{1,0:T(8,128)(2,1)S(1)}, u32[]{:S(2)}, u32[]{:S(2)}) %collective-permute-start.6) | collective-permute-done | bytes 335904 | tf_op jit(solution)/shard_map/gather_0_1/ppermute | solution.py:32
  28.0 1.6 %collective-permute-start.7 = (bf16[656,256]{1,0:T(8,128)(2,1)S(1)}, bf16[656,256]{1,0:T(8,128)(2,1)S(1)}, u32[]{:S(2)}, u32[]{:S(2)}) collective-permute-start(bf16[656,256]{1,0:T(8,128)(2,1)S(1)} %shard_map.94.refs_1_), channel_id=1, source_target_pairs={{0,1},{1,0},{2,3},{3,2},{4,5},{5,4},{6,7},{7,6},{8,9},{9,8},{10,11... | collective-permute-start | bytes 1007624 | tf_op jit(solution)/shard_map/gather_0_3/ppermute | solution.py:32
  30.3 6.1 %collective-permute-done.14.refs_2_ = bf16[656,256]{1,0:T(8,128)(2,1)S(1)} collective-permute-done((bf16[656,256]{1,0:T(8,128)(2,1)S(1)}, bf16[656,256]{1,0:T(8,128)(2,1)S(1)}, u32[]{:S(2)}, u32[]{:S(2)}) %collective-permute-start.14) | collective-permute-done | bytes 335904 | tf_op jit(solution)/shard_map/gather_1_2/ppermute | solution.py:32
  36.3 1.3 %collective-permute-start.15 = (bf16[656,256]{1,0:T(8,128)(2,1)S(1)}, bf16[656,256]{1,0:T(8,128)(2,1)S(1)}, u32[]{:S(2)}, u32[]{:S(2)}) collective-permute-start(bf16[656,256]{1,0:T(8,128)(2,1)S(1)} %collective-permute-done.14.refs_2_), channel_id=1, source_target_pairs={{0,1},{1,0},{2,3},{3,2},{4,5},{5,4},{6,7},{7,6},{8,9},{9,8},{10,11... | collective-permute-start | bytes 1007624 | tf_op jit(solution)/shard_map/gather_1_3/ppermute | solution.py:32
  37.6 2.1 %shard_map.96.refs_2_ = f32[960,320]{1,0:T(8,128)S(1)} custom-call(bf16[656,256]{1,0:T(8,128)(2,1)S(1)} %shard_map.93.refs_1_.refs_0_.refs_7_.refs_3_, bf16[656,256]{1,0:T(8,128)(2,1)S(1)} %collective-permute-done.6.refs_1_.refs_5_, bf16[656,256]{1,0:T(8,128)(2,1)S(1)} %collective-permute-done.5.refs_0_.refs_2_, ...), custom_call_target="tpu_custom_call" | custom-call | flops 1258291200 | bytes 1048576 | tf_op jit(solution)/shard_map/pallas_call | solution.py:81
  39.8 1.0 %shard_map.97 = (bf16[320,384]{1,0:T(8,128)(2,1)S(1)}, bf16[320,384]{1,0:T(8,128)(2,1)S(1)}, bf16[320,384]{1,0:T(8,128)(2,1)S(1)}) custom-call(bf16[656,256]{1,0:T(8,128)(2,1)S(1)} %collective-permute-done.7.refs_0_.refs_6_, bf16[960,320]{1,0:T(8,128)(2,1)S(1)} %shard_map.92.refs_1_.refs_3_.refs_6_, f32[960,320]{1,0:T(8,128)S(1)} %shard_map.96.refs_2_), custom_call_target="tpu_custom_call" | custom-call | bytes 1048576 | tf_op jit(solution)/shard_map/pallas_call | solution.py:81
  40.8 2.8 %collective-permute-start.9 = (bf16[320,384]{1,0:T(8,128)(2,1)S(1)}, bf16[320,384]{1,0:T(8,128)(2,1)S(1)}, u32[]{:S(2)}, u32[]{:S(2)}) collective-permute-start(bf16[320,384]{1,0:T(8,128)(2,1)S(1)} %get-tuple-element.26.refs_0_), channel_id=1, source_target_pairs={{0,8},{1,9},{2,10},{3,11},{4,12},{5,13},{6,14},{7,15},{8,0},{9,1},... | collective-permute-start | bytes 737288 | tf_op jit(solution)/shard_map/swap_0/ppermute | solution.py:32
  44.1 1.2 %collective-permute-start.13 = (bf16[656,256]{1,0:T(8,128)(2,1)S(1)}, bf16[656,256]{1,0:T(8,128)(2,1)S(1)}, u32[]{:S(2)}, u32[]{:S(2)}) collective-permute-start(bf16[656,256]{1,0:T(8,128)(2,1)S(1)} %shard_map.99.refs_0_), channel_id=1, source_target_pairs={{0,1},{1,0},{2,3},{3,2},{4,5},{5,4},{6,7},{7,6},{8,9},{9,8},{10,11... | collective-permute-start | bytes 1007624 | tf_op jit(solution)/shard_map/gather_1_1/ppermute | solution.py:32
  45.3 3.2 %collective-permute-start.12 = (bf16[656,256]{1,0:T(8,128)(2,1)S(1)}, bf16[656,256]{1,0:T(8,128)(2,1)S(1)}, u32[]{:S(2)}, u32[]{:S(2)}) collective-permute-start(bf16[656,256]{1,0:T(8,128)(2,1)S(1)} %collective-permute-done.7.refs_0_.refs_6_), channel_id=1, source_target_pairs={{0,8},{1,9},{2,10},{3,11},{4,12},{5,13},{6,14},{7,15},{8,0},{9,1},... | collective-permute-start | bytes 1007624 | tf_op jit(solution)/shard_map/last_0/ppermute | solution.py:32
  48.6 4.7 %shard_map.98.refs_2_.refs_4_.refs_7_ = bf16[960,320]{1,0:T(8,128)(2,1)S(1)} custom-call(bf16[320,384]{1,0:T(8,128)(2,1)S(1)} %get-tuple-element.26.refs_0_, bf16[320,384]{1,0:T(8,128)(2,1)S(1)} %get-tuple-element.27.refs_1_, bf16[320,384]{1,0:T(8,128)(2,1)S(1)} %get-tuple-element.28.refs_2_, bf16[320,384]{1,0:T(8,128)(2,1)S(1)} %collective-permute-done.9.refs_3_, ...), custom_call_target="tpu_custom_call" | custom-call | flops 1769472000 | bytes 1048576 | tf_op jit(solution)/shard_map/pallas_call | solution.py:81
  53.3 2.9 %shard_map.102 = (bf16[320,384]{1,0:T(8,128)(2,1)S(1)}, bf16[320,384]{1,0:T(8,128)(2,1)S(1)}, bf16[320,384]{1,0:T(8,128)(2,1)S(1)}) custom-call(bf16[656,256]{1,0:T(8,128)(2,1)S(1)} %shard_map.99.refs_0_, bf16[656,256]{1,0:T(8,128)(2,1)S(1)} %collective-permute-done.13.refs_8_.refs_1_, bf16[656,256]{1,0:T(8,128)(2,1)S(1)} %collective-permute-done.14.refs_2_, ...), custom_call_target="tpu_custom_call" | custom-call | flops 1258291200 | bytes 1048576 | tf_op jit(solution)/shard_map/pallas_call | solution.py:81
  56.2 1.4 %collective-permute-start.21 = (bf16[320,384]{1,0:T(8,128)(2,1)S(1)}, bf16[320,384]{1,0:T(8,128)(2,1)S(1)}, u32[]{:S(2)}, u32[]{:S(2)}) collective-permute-start(bf16[320,384]{1,0:T(8,128)(2,1)S(1)} %get-tuple-element.35.refs_1_), channel_id=1, source_target_pairs={{0,8},{1,9},{2,10},{3,11},{4,12},{5,13},{6,14},{7,15},{8,0},{9,1},... | collective-permute-start | bytes 737288 | tf_op jit(solution)/shard_map/swap_1/ppermute | solution.py:32
  58.1 2.5 %shard_map.100 = (bf16[3,64,320]{2,1,0:T(8,128)(2,1)S(1)}, bf16[3,64,320]{2,1,0:T(8,128)(2,1)S(1)}, bf16[3,64,320]{2,1,0:T(8,128)(2,1)S(1)}, bf16[3,64,320]{2,1,0:T(8,128)(2,1)S(1)}, bf16[256,320]{1,0:T(8,128)(2,1)S(1)}) custom-call(s32[4]{0:T(128)S(1)} %pad_add_fusion.refs_0_, bf16[2,320,256]{2,1,0:T(8,128)(2,1)S(1)} %collective-permute-done.refs_8_.refs_1_, ...), custom_call_target="tpu_custom_call" | custom-call | flops 335544320 | bytes 1048576 | tf_op jit(solution)/shard_map/pallas_call | solution.py:81
  61.2 4.0 %collective-permute-start.18 = (bf16[3,64,320]{2,1,0:T(8,128)(2,1)S(1)}, bf16[3,64,320]{2,1,0:T(8,128)(2,1)S(1)}, u32[]{:S(2)}, u32[]{:S(2)}) collective-permute-start(bf16[3,64,320]{2,1,0:T(8,128)(2,1)S(1)} %get-tuple-element.30), channel_id=1, source_target_pairs={{0,8},{1,9},{2,10},{3,11},{4,16},{5,17},{6,18},{7,19},{8,12},{9,13... | collective-permute-start | bytes 368648 | tf_op jit(solution)/shard_map/spread_early_1/ppermute | solution.py:32
  65.2 1.5 %collective-permute-start.19 = (bf16[3,64,320]{2,1,0:T(8,128)(2,1)S(1)}, bf16[3,64,320]{2,1,0:T(8,128)(2,1)S(1)}, u32[]{:S(2)}, u32[]{:S(2)}) collective-permute-start(bf16[3,64,320]{2,1,0:T(8,128)(2,1)S(1)} %get-tuple-element.31), channel_id=1, source_target_pairs={{0,16},{1,17},{2,18},{3,19},{4,24},{5,25},{6,26},{7,27},{8,20},{9,... | collective-permute-start | bytes 368648 | tf_op jit(solution)/shard_map/spread_early_2/ppermute | solution.py:32
  66.8 5.8 %shard_map.103 = (bf16[64,320]{1,0:T(8,128)(2,1)S(1)}, bf16[64,320]{1,0:T(8,128)(2,1)S(1)}, bf16[64,320]{1,0:T(8,128)(2,1)S(1)}, bf16[64,320]{1,0:T(8,128)(2,1)S(1)}) custom-call(s32[4]{0:T(128)S(1)} %pad_add_fusion.refs_0_, bf16[320,384]{1,0:T(8,128)(2,1)S(1)} %get-tuple-element.35.refs_1_, bf16[320,384]{1,0:T(8,128)(2,1)S(1)} %get-tuple-element.36.refs_2_, ...), custom_call_target="tpu_custom_call" | custom-call | flops 1769472000 | bytes 1048576 | tf_op jit(solution)/shard_map/pallas_call | solution.py:81
  73.3 4.3 %collective-permute-start.25 = (bf16[64,320]{1,0:T(8,128)(2,1)S(1)}, bf16[64,320]{1,0:T(8,128)(2,1)S(1)}, u32[]{:S(2)}, u32[]{:S(2)}) collective-permute-start(bf16[64,320]{1,0:T(8,128)(2,1)S(1)} %get-tuple-element.40), channel_id=1, source_target_pairs={{0,8},{1,9},{2,10},{3,11},{4,16},{5,17},{6,18},{7,19},{8,12},{9,13... | collective-permute-start | bytes 122888 | tf_op jit(solution)/shard_map/spread_late_1/ppermute | solution.py:32
  78.1 1.3 %collective-permute-start.27 = (bf16[64,320]{1,0:T(8,128)(2,1)S(1)}, bf16[64,320]{1,0:T(8,128)(2,1)S(1)}, u32[]{:S(2)}, u32[]{:S(2)}) collective-permute-start(bf16[64,320]{1,0:T(8,128)(2,1)S(1)} %get-tuple-element.42), channel_id=1, source_target_pairs={{0,24},{1,25},{2,26},{3,27},{4,0},{5,1},{6,2},{7,3},{8,28},{9,29},... | collective-permute-start | bytes 122888 | tf_op jit(solution)/shard_map/spread_late_3/ppermute | solution.py:32
  79.5 1.1 %shard_map.101 = (f32[2,1,64,1280]{3,2,1,0:T(8,128)}, f32[64,1280]{1,0:T(8,128)S(1)}) custom-call(s32[1]{0:T(128)} %bitcast.refs_0_, f32[2,1280]{1,0:T(2,128)S(1)} %copy-done.4, bf16[3,64,320]{2,1,0:T(8,128)(2,1)S(1)} %collective-permute-done.17.refs_2_, bf16[3,64,320]{2,1,0:T(8,128)(2,1)S(1)} %collective-permute-done.18.refs_3_, ...), custom_call_target="tpu_custom_call" | custom-call | bytes 1048576 | tf_op jit(solution)/shard_map/pallas_call | solution.py:81
  81.7 1.7 %collective-permute-done.27.refs_7_ = bf16[64,320]{1,0:T(8,128)(2,1)S(1)} collective-permute-done((bf16[64,320]{1,0:T(8,128)(2,1)S(1)}, bf16[64,320]{1,0:T(8,128)(2,1)S(1)}, u32[]{:S(2)}, u32[]{:S(2)}) %collective-permute-start.27) | collective-permute-done | bytes 40992 | tf_op jit(solution)/shard_map/spread_late_3/ppermute | solution.py:32
  83.4 1.0 %shard_map.104 = f32[2,1,64,1280]{3,2,1,0:T(8,128)} custom-call(s32[1]{0:T(128)} %bitcast.refs_0_, f32[2,1280]{1,0:T(2,128)S(1)} %copy-done.4, f32[2,1,64,1280]{3,2,1,0:T(8,128)} %get-tuple-element.33.refs_2_, f32[64,1280]{1,0:T(8,128)S(1)} %get-tuple-element.34.refs_3_, ...), custom_call_target="tpu_custom_call", output_to_operand_aliasing={{}: (2, {})} | custom-call | bytes 1048576 | tf_op jit(solution)/shard_map/pallas_call | solution.py:81
  (51 shorter events, 7.1 us)
Async XLA Ops:
  2.7 12.8 %collective-permute-start.1 = (bf16[656,256]{1,0:T(8,128)(2,1)}, bf16[656,256]{1,0:T(8,128)(2,1)S(1)}, u32[]{:S(2)}, u32[]{:S(2)}) collective-permute-start(bf16[656,256]{1,0:T(8,128)(2,1)} %get-tuple-element.24), channel_id=1, source_target_pairs={{0,0},{1,1},{2,2},{3,3},{4,8},{5,9},{6,10},{7,11},{8,4},{9,5},{10,... | collective-permute-start | bytes 1007624 | tf_op jit(solution)/shard_map/regroup_0/ppermute | solution.py:32
  4.4 5.8 %collective-permute-start.2 = (bf16[320,320]{1,0:T(8,128)(2,1)}, bf16[320,320]{1,0:T(8,128)(2,1)S(1)}, u32[]{:S(2)}, u32[]{:S(2)}) collective-permute-start(bf16[320,320]{1,0:T(8,128)(2,1)} %bitcast.11), channel_id=1, source_target_pairs={{0,8},{1,9},{2,10},{3,11},{4,12},{5,13},{6,14},{7,15},{8,0},{9,1},... | collective-permute-start | bytes 614408 | tf_op jit(solution)/shard_map/lend_0/ppermute | solution.py:32
  8.9 1.7 %collective-permute-start.3 = (bf16[320,320]{1,0:T(8,128)(2,1)}, bf16[320,320]{1,0:T(8,128)(2,1)S(1)}, u32[]{:S(2)}, u32[]{:S(2)}) collective-permute-start(bf16[320,320]{1,0:T(8,128)(2,1)} %bitcast.13), channel_id=1, source_target_pairs={{0,8},{1,9},{2,10},{3,11},{4,12},{5,13},{6,14},{7,15},{8,0},{9,1},... | collective-permute-start | bytes 614408 | tf_op jit(solution)/shard_map/lend_1/ppermute | solution.py:32
  8.9 2.0 %collective-permute-start.4 = (bf16[320,320]{1,0:T(8,128)(2,1)}, bf16[320,320]{1,0:T(8,128)(2,1)S(1)}, u32[]{:S(2)}, u32[]{:S(2)}) collective-permute-start(bf16[320,320]{1,0:T(8,128)(2,1)} %bitcast.15), channel_id=1, source_target_pairs={{0,8},{1,9},{2,10},{3,11},{4,12},{5,13},{6,14},{7,15},{8,0},{9,1},... | collective-permute-start | bytes 614408 | tf_op jit(solution)/shard_map/lend_2/ppermute | solution.py:32
  9.4 9.3 %copy-start = (bf16[656,256]{1,0:T(8,128)(2,1)S(1)}, bf16[656,256]{1,0:T(8,128)(2,1)}, u32[]{:S(2)}) copy-start(bf16[656,256]{1,0:T(8,128)(2,1)} %get-tuple-element.25.refs_0_) | copy-start | bytes 1007620
  10.9 0.9 %copy-start.1 = (bf16[1,320,320]{2,1,0:T(8,128)(2,1)S(1)}, bf16[1,320,320]{2,1,0:T(8,128)(2,1)}, u32[]{:S(2)}) copy-start(bf16[1,320,320]{2,1,0:T(8,128)(2,1)} %param.13) | copy-start | bytes 614404
  15.6 9.9 %collective-permute-start.5 = (bf16[656,256]{1,0:T(8,128)(2,1)S(1)}, bf16[656,256]{1,0:T(8,128)(2,1)S(1)}, u32[]{:S(2)}, u32[]{:S(2)}) collective-permute-start(bf16[656,256]{1,0:T(8,128)(2,1)S(1)} %shard_map.93.refs_1_.refs_0_.refs_7_.refs_3_), channel_id=1, source_target_pairs={{0,2},{1,3},{2,0},{3,1},{4,6},{5,7},{6,4},{7,5},{8,10},{9,11},{10,... | collective-permute-start | bytes 1007624 | tf_op jit(solution)/shard_map/gather_0_2/ppermute | solution.py:32
  17.2 10.7 %collective-permute-start.6 = (bf16[656,256]{1,0:T(8,128)(2,1)S(1)}, bf16[656,256]{1,0:T(8,128)(2,1)S(1)}, u32[]{:S(2)}, u32[]{:S(2)}) collective-permute-start(bf16[656,256]{1,0:T(8,128)(2,1)S(1)} %shard_map.93.refs_1_.refs_0_.refs_7_.refs_3_), channel_id=1, source_target_pairs={{0,1},{1,0},{2,3},{3,2},{4,5},{5,4},{6,7},{7,6},{8,9},{9,8},{10,11... | collective-permute-start | bytes 1007624 | tf_op jit(solution)/shard_map/gather_0_1/ppermute | solution.py:32
  18.7 10.9 %copy-start.5 = (bf16[2,256,320]{1,2,0:T(8,128)(2,1)S(1)}, bf16[2,256,320]{1,2,0:T(8,128)(2,1)}, u32[]{:S(2)}) copy-start(bf16[2,256,320]{1,2,0:T(8,128)(2,1)} %param.9) | copy-start | bytes 983044
  18.7 9.1 %collective-permute-start.8 = (bf16[656,256]{1,0:T(8,128)(2,1)S(1)}, bf16[656,256]{1,0:T(8,128)(2,1)S(1)}, u32[]{:S(2)}, u32[]{:S(2)}) collective-permute-start(bf16[656,256]{1,0:T(8,128)(2,1)S(1)} %shard_map.95), channel_id=1, source_target_pairs={{0,0},{1,1},{2,2},{3,3},{4,8},{5,9},{6,10},{7,11},{8,4},{9,5},{10,... | collective-permute-start | bytes 1007624 | tf_op jit(solution)/shard_map/regroup_1/ppermute | solution.py:32
  27.9 8.4 %collective-permute-start.14 = (bf16[656,256]{1,0:T(8,128)(2,1)S(1)}, bf16[656,256]{1,0:T(8,128)(2,1)S(1)}, u32[]{:S(2)}, u32[]{:S(2)}) collective-permute-start(bf16[656,256]{1,0:T(8,128)(2,1)S(1)} %shard_map.99.refs_0_), channel_id=1, source_target_pairs={{0,2},{1,3},{2,0},{3,1},{4,6},{5,7},{6,4},{7,5},{8,10},{9,11},{10,... | collective-permute-start | bytes 1007624 | tf_op jit(solution)/shard_map/gather_1_2/ppermute | solution.py:32
  28.0 11.8 %collective-permute-start.7 = (bf16[656,256]{1,0:T(8,128)(2,1)S(1)}, bf16[656,256]{1,0:T(8,128)(2,1)S(1)}, u32[]{:S(2)}, u32[]{:S(2)}) collective-permute-start(bf16[656,256]{1,0:T(8,128)(2,1)S(1)} %shard_map.94.refs_1_), channel_id=1, source_target_pairs={{0,1},{1,0},{2,3},{3,2},{4,5},{5,4},{6,7},{7,6},{8,9},{9,8},{10,11... | collective-permute-start | bytes 1007624 | tf_op jit(solution)/shard_map/gather_0_3/ppermute | solution.py:32
  29.6 14.5 %collective-permute-start = (bf16[2,320,256]{2,1,0:T(8,128)(2,1)S(1)}, bf16[2,320,256]{2,1,0:T(8,128)(2,1)S(1)}, u32[]{:S(2)}, u32[]{:S(2)}) collective-permute-start(bf16[2,320,256]{2,1,0:T(8,128)(2,1)S(1)} %bitcast.19), channel_id=1, source_target_pairs={{0,0},{1,1},{2,2},{3,3},{4,8},{5,9},{6,10},{7,11},{8,4},{9,5},{10,... | collective-permute-start | bytes 983048 | tf_op jit(solution)/shard_map/regroup_queries/ppermute | solution.py:32
  36.3 12.2 %collective-permute-start.15 = (bf16[656,256]{1,0:T(8,128)(2,1)S(1)}, bf16[656,256]{1,0:T(8,128)(2,1)S(1)}, u32[]{:S(2)}, u32[]{:S(2)}) collective-permute-start(bf16[656,256]{1,0:T(8,128)(2,1)S(1)} %collective-permute-done.14.refs_2_), channel_id=1, source_target_pairs={{0,1},{1,0},{2,3},{3,2},{4,5},{5,4},{6,7},{7,6},{8,9},{9,8},{10,11... | collective-permute-start | bytes 1007624 | tf_op jit(solution)/shard_map/gather_1_3/ppermute | solution.py:32
  40.8 4.5 %collective-permute-start.9 = (bf16[320,384]{1,0:T(8,128)(2,1)S(1)}, bf16[320,384]{1,0:T(8,128)(2,1)S(1)}, u32[]{:S(2)}, u32[]{:S(2)}) collective-permute-start(bf16[320,384]{1,0:T(8,128)(2,1)S(1)} %get-tuple-element.26.refs_0_), channel_id=1, source_target_pairs={{0,8},{1,9},{2,10},{3,11},{4,12},{5,13},{6,14},{7,15},{8,0},{9,1},... | collective-permute-start | bytes 737288 | tf_op jit(solution)/shard_map/swap_0/ppermute | solution.py:32
  43.6 5.0 %collective-permute-start.10 = (bf16[320,384]{1,0:T(8,128)(2,1)S(1)}, bf16[320,384]{1,0:T(8,128)(2,1)S(1)}, u32[]{:S(2)}, u32[]{:S(2)}) collective-permute-start(bf16[320,384]{1,0:T(8,128)(2,1)S(1)} %get-tuple-element.27.refs_1_), channel_id=1, source_target_pairs={{0,8},{1,9},{2,10},{3,11},{4,12},{5,13},{6,14},{7,15},{8,0},{9,1},... | collective-permute-start | bytes 737288 | tf_op jit(solution)/shard_map/swap_0/ppermute | solution.py:32
  43.6 5.0 %collective-permute-start.11 = (bf16[320,384]{1,0:T(8,128)(2,1)S(1)}, bf16[320,384]{1,0:T(8,128)(2,1)S(1)}, u32[]{:S(2)}, u32[]{:S(2)}) collective-permute-start(bf16[320,384]{1,0:T(8,128)(2,1)S(1)} %get-tuple-element.28.refs_2_), channel_id=1, source_target_pairs={{0,8},{1,9},{2,10},{3,11},{4,12},{5,13},{6,14},{7,15},{8,0},{9,1},... | collective-permute-start | bytes 737288 | tf_op jit(solution)/shard_map/swap_0/ppermute | solution.py:32
  44.1 9.2 %collective-permute-start.13 = (bf16[656,256]{1,0:T(8,128)(2,1)S(1)}, bf16[656,256]{1,0:T(8,128)(2,1)S(1)}, u32[]{:S(2)}, u32[]{:S(2)}) collective-permute-start(bf16[656,256]{1,0:T(8,128)(2,1)S(1)} %shard_map.99.refs_0_), channel_id=1, source_target_pairs={{0,1},{1,0},{2,3},{3,2},{4,5},{5,4},{6,7},{7,6},{8,9},{9,8},{10,11... | collective-permute-start | bytes 1007624 | tf_op jit(solution)/shard_map/gather_1_1/ppermute | solution.py:32
  45.3 12.8 %collective-permute-start.12 = (bf16[656,256]{1,0:T(8,128)(2,1)S(1)}, bf16[656,256]{1,0:T(8,128)(2,1)S(1)}, u32[]{:S(2)}, u32[]{:S(2)}) collective-permute-start(bf16[656,256]{1,0:T(8,128)(2,1)S(1)} %collective-permute-done.7.refs_0_.refs_6_), channel_id=1, source_target_pairs={{0,8},{1,9},{2,10},{3,11},{4,12},{5,13},{6,14},{7,15},{8,0},{9,1},... | collective-permute-start | bytes 1007624 | tf_op jit(solution)/shard_map/last_0/ppermute | solution.py:32
  48.5 9.6 %collective-permute-start.16 = (bf16[656,256]{1,0:T(8,128)(2,1)S(1)}, bf16[656,256]{1,0:T(8,128)(2,1)S(1)}, u32[]{:S(2)}, u32[]{:S(2)}) collective-permute-start(bf16[656,256]{1,0:T(8,128)(2,1)S(1)} %collective-permute-done.15.refs_9_.refs_3_), channel_id=1, source_target_pairs={{0,8},{1,9},{2,10},{3,11},{4,12},{5,13},{6,14},{7,15},{8,0},{9,1},... | collective-permute-start | bytes 1007624 | tf_op jit(solution)/shard_map/last_1/ppermute | solution.py:32
  56.2 9.1 %collective-permute-start.21 = (bf16[320,384]{1,0:T(8,128)(2,1)S(1)}, bf16[320,384]{1,0:T(8,128)(2,1)S(1)}, u32[]{:S(2)}, u32[]{:S(2)}) collective-permute-start(bf16[320,384]{1,0:T(8,128)(2,1)S(1)} %get-tuple-element.35.refs_1_), channel_id=1, source_target_pairs={{0,8},{1,9},{2,10},{3,11},{4,12},{5,13},{6,14},{7,15},{8,0},{9,1},... | collective-permute-start | bytes 737288 | tf_op jit(solution)/shard_map/swap_1/ppermute | solution.py:32
  57.6 9.2 %collective-permute-start.22 = (bf16[320,384]{1,0:T(8,128)(2,1)S(1)}, bf16[320,384]{1,0:T(8,128)(2,1)S(1)}, u32[]{:S(2)}, u32[]{:S(2)}) collective-permute-start(bf16[320,384]{1,0:T(8,128)(2,1)S(1)} %get-tuple-element.36.refs_2_), channel_id=1, source_target_pairs={{0,8},{1,9},{2,10},{3,11},{4,12},{5,13},{6,14},{7,15},{8,0},{9,1},... | collective-permute-start | bytes 737288 | tf_op jit(solution)/shard_map/swap_1/ppermute | solution.py:32
  57.7 9.1 %collective-permute-start.23 = (bf16[320,384]{1,0:T(8,128)(2,1)S(1)}, bf16[320,384]{1,0:T(8,128)(2,1)S(1)}, u32[]{:S(2)}, u32[]{:S(2)}) collective-permute-start(bf16[320,384]{1,0:T(8,128)(2,1)S(1)} %get-tuple-element.37.refs_3_), channel_id=1, source_target_pairs={{0,8},{1,9},{2,10},{3,11},{4,12},{5,13},{6,14},{7,15},{8,0},{9,1},... | collective-permute-start | bytes 737288 | tf_op jit(solution)/shard_map/swap_1/ppermute | solution.py:32
  60.6 12.7 %collective-permute-start.17 = (bf16[3,64,320]{2,1,0:T(8,128)(2,1)S(1)}, bf16[3,64,320]{2,1,0:T(8,128)(2,1)S(1)}, u32[]{:S(2)}, u32[]{:S(2)}) collective-permute-start(bf16[3,64,320]{2,1,0:T(8,128)(2,1)S(1)} %get-tuple-element.29), channel_id=1, source_target_pairs={{0,0},{1,1},{2,2},{3,3},{4,8},{5,9},{6,10},{7,11},{8,4},{9,5},{10,... | collective-permute-start | bytes 368648 | tf_op jit(solution)/shard_map/spread_early_0/ppermute | solution.py:32
  61.2 16.4 %collective-permute-start.18 = (bf16[3,64,320]{2,1,0:T(8,128)(2,1)S(1)}, bf16[3,64,320]{2,1,0:T(8,128)(2,1)S(1)}, u32[]{:S(2)}, u32[]{:S(2)}) collective-permute-start(bf16[3,64,320]{2,1,0:T(8,128)(2,1)S(1)} %get-tuple-element.30), channel_id=1, source_target_pairs={{0,8},{1,9},{2,10},{3,11},{4,16},{5,17},{6,18},{7,19},{8,12},{9,13... | collective-permute-start | bytes 368648 | tf_op jit(solution)/shard_map/spread_early_1/ppermute | solution.py:32
  65.2 12.9 %collective-permute-start.19 = (bf16[3,64,320]{2,1,0:T(8,128)(2,1)S(1)}, bf16[3,64,320]{2,1,0:T(8,128)(2,1)S(1)}, u32[]{:S(2)}, u32[]{:S(2)}) collective-permute-start(bf16[3,64,320]{2,1,0:T(8,128)(2,1)S(1)} %get-tuple-element.31), channel_id=1, source_target_pairs={{0,16},{1,17},{2,18},{3,19},{4,24},{5,25},{6,26},{7,27},{8,20},{9,... | collective-permute-start | bytes 368648 | tf_op jit(solution)/shard_map/spread_early_2/ppermute | solution.py:32
  66.7 12.7 %collective-permute-start.20 = (bf16[3,64,320]{2,1,0:T(8,128)(2,1)S(1)}, bf16[3,64,320]{2,1,0:T(8,128)(2,1)S(1)}, u32[]{:S(2)}, u32[]{:S(2)}) collective-permute-start(bf16[3,64,320]{2,1,0:T(8,128)(2,1)S(1)} %get-tuple-element.32), channel_id=1, source_target_pairs={{0,24},{1,25},{2,26},{3,27},{4,0},{5,1},{6,2},{7,3},{8,28},{9,29},... | collective-permute-start | bytes 368648 | tf_op jit(solution)/shard_map/spread_early_3/ppermute | solution.py:32
  66.8 12.7 %copy-start.4 = (f32[2,1280]{1,0:T(2,128)S(1)}, f32[2,1280]{1,0:T(2,128)}, u32[]{:S(2)}) copy-start(f32[2,1280]{1,0:T(2,128)} %refs_1_.3) | copy-start | bytes 30724
  72.6 8.0 %collective-permute-start.24 = (bf16[64,320]{1,0:T(8,128)(2,1)S(1)}, bf16[64,320]{1,0:T(8,128)(2,1)S(1)}, u32[]{:S(2)}, u32[]{:S(2)}) collective-permute-start(bf16[64,320]{1,0:T(8,128)(2,1)S(1)} %get-tuple-element.39), channel_id=1, source_target_pairs={{0,0},{1,1},{2,2},{3,3},{4,8},{5,9},{6,10},{7,11},{8,4},{9,5},{10,... | collective-permute-start | bytes 122888 | tf_op jit(solution)/shard_map/spread_late_0/ppermute | solution.py:32
  73.3 7.9 %collective-permute-start.25 = (bf16[64,320]{1,0:T(8,128)(2,1)S(1)}, bf16[64,320]{1,0:T(8,128)(2,1)S(1)}, u32[]{:S(2)}, u32[]{:S(2)}) collective-permute-start(bf16[64,320]{1,0:T(8,128)(2,1)S(1)} %get-tuple-element.40), channel_id=1, source_target_pairs={{0,8},{1,9},{2,10},{3,11},{4,16},{5,17},{6,18},{7,19},{8,12},{9,13... | collective-permute-start | bytes 122888 | tf_op jit(solution)/shard_map/spread_late_1/ppermute | solution.py:32
  77.6 4.1 %collective-permute-start.26 = (bf16[64,320]{1,0:T(8,128)(2,1)S(1)}, bf16[64,320]{1,0:T(8,128)(2,1)S(1)}, u32[]{:S(2)}, u32[]{:S(2)}) collective-permute-start(bf16[64,320]{1,0:T(8,128)(2,1)S(1)} %get-tuple-element.41), channel_id=1, source_target_pairs={{0,16},{1,17},{2,18},{3,19},{4,24},{5,25},{6,26},{7,27},{8,20},{9,... | collective-permute-start | bytes 122888 | tf_op jit(solution)/shard_map/spread_late_2/ppermute | solution.py:32
  78.1 5.3 %collective-permute-start.27 = (bf16[64,320]{1,0:T(8,128)(2,1)S(1)}, bf16[64,320]{1,0:T(8,128)(2,1)S(1)}, u32[]{:S(2)}, u32[]{:S(2)}) collective-permute-start(bf16[64,320]{1,0:T(8,128)(2,1)S(1)} %get-tuple-element.42), channel_id=1, source_target_pairs={{0,24},{1,25},{2,26},{3,27},{4,0},{5,1},{6,2},{7,3},{8,28},{9,29},... | collective-permute-start | bytes 122888 | tf_op jit(solution)/shard_map/spread_late_3/ppermute | solution.py:32
  (2 other events, 1.9 us)

commit v4 on v3

--- a/solution.py
+++ b/solution.py
@@ -176,16 +176,35 @@
         first = False
 
 
+def symmetric(size, product):
+    main = size - size % 256
+    if main in (0, size):
+        return product(slice(0, size), slice(0, size)).astype(BF16)
+    left = product(slice(0, size), slice(0, main))
+    corner = product(slice(main, size), slice(main, size)).astype(BF16)
+    right = jnp.concatenate([left[main:].T.astype(BF16), corner], 0)
+    return jnp.concatenate([left.astype(BF16), right], 1)
+
+
+def square_of(x):
+    return symmetric(x.shape[0], lambda rows, columns: dot_nt(x[rows], x[columns]))
+
+
+def mixing_of(s):
+    def part(rows, columns):
+        return NEWTON_B * s[rows, columns].astype(F32) + NEWTON_C * dot_nn(s[rows], s[:, columns])
+
+    return symmetric(s.shape[0], part)
+
+
 def orthogonalized(totals):
     iterates = []
     for one in totals:
         norm = jnp.sqrt(jnp.sum(one * one, keepdims=True))
         iterates.append((one / (norm + FROB_EPS)).astype(BF16))
     for _ in range(NS_STEPS):
-        squares = [dot_nt(x, x).astype(BF16) for x in iterates]
-        mixings = [
-            (NEWTON_B * s.astype(F32) + NEWTON_C * dot_nn(s, s)).astype(BF16) for s in squares
-        ]
+        squares = [square_of(x) for x in iterates]
+        mixings = [mixing_of(s) for s in squares]
         iterates = [
             (NEWTON_A * x.astype(F32) + dot_nn(m, x)).astype(BF16)
             for m, x in zip(mixings, iterates)

time: 84.9 us -> 84.1 us (level)
  Pallas kernels: 25 us -> 23.8 us
    pallas_call x14, Pallas kernels: 25 us -> 23.8 us  [call(): pl.pallas_call(body, out_shape=shapes, in_specs=specs, out_specs=tuple((p...]
  transfers between devices with their start and end apart: 28 -> 28, of which waited for: 9 -> 10; matrix products, arithmetic and copies ran while one was open for 0% -> 0% of each run, Pallas kernels for 26% -> 25%
where the time goes in v4:
time: 84.1 us; the launch traced here: 83.8 us
  starting transfers between devices  37.1 us (44%)
  Pallas kernels  23.8 us (28%)
  waiting for transfers between devices  19 us (23%)
  local copies, waits for them, and re-layouts  2.85 us (3%)
  between operations  1.02 us (1%)
    ppermute x28, starting transfers between devices, moved(): return lax.ppermute(array, BOTH, pairs)  37.1 us
    pallas_call x14, Pallas kernels, call(): pl.pallas_call(body, out_shape=shapes, in_specs=specs, out_specs=tuple((p...  23.8 us
    ppermute x28, waiting for transfers between devices, moved(): return lax.ppermute(array, BOTH, pairs)  19 us
    unnamed x12, local copies, waits for them, and re-layouts  2.85 us
  transfers between devices with their start and end apart: 28, of which 10 were waited for; matrix products, arithmetic and copies ran while one was open for 0% of the time, Pallas kernels for 25%

profile of v4, /device:TPU:0, one launch (start us, length us, event | category | flops | bytes accessed | tf_op | source)
XLA Modules:
  0.0 83.8 jit_solution(1895881597372435922)
XLA Ops:
  0.7 2.1 %shard_map.91 = (bf16[656,256]{1,0:T(8,128)(2,1)}, bf16[656,256]{1,0:T(8,128)(2,1)}) custom-call(bf16[2,320,256]{2,1,0:T(8,128)(2,1)} %bitcast.17, bf16[2,320,256]{2,1,0:T(8,128)(2,1)} %bitcast.18, f32[2,1,256]{2,1,0:T(1,128)} %refs_2_.1, f32[1]{0:T(128)S(6)} %copy.12.refs_3_), custom_call_target="tpu_custom_call" | custom-call | bytes 1048576 | tf_op jit(solution)/shard_map/pallas_call | solution.py:81
  2.7 1.6 %collective-permute-start.1 = (bf16[656,256]{1,0:T(8,128)(2,1)}, bf16[656,256]{1,0:T(8,128)(2,1)S(1)}, u32[]{:S(2)}, u32[]{:S(2)}) collective-permute-start(bf16[656,256]{1,0:T(8,128)(2,1)} %get-tuple-element.24), channel_id=1, source_target_pairs={{0,0},{1,1},{2,2},{3,3},{4,8},{5,9},{6,10},{7,11},{8,4},{9,5},{10,... | collective-permute-start | bytes 1007624 | tf_op jit(solution)/shard_map/regroup_0/ppermute | solution.py:32
  4.4 4.5 %collective-permute-start.2 = (bf16[320,320]{1,0:T(8,128)(2,1)}, bf16[320,320]{1,0:T(8,128)(2,1)S(1)}, u32[]{:S(2)}, u32[]{:S(2)}) collective-permute-start(bf16[320,320]{1,0:T(8,128)(2,1)} %bitcast.11), channel_id=1, source_target_pairs={{0,8},{1,9},{2,10},{3,11},{4,12},{5,13},{6,14},{7,15},{8,0},{9,1},... | collective-permute-start | bytes 614408 | tf_op jit(solution)/shard_map/lend_0/ppermute | solution.py:32
  10.9 0.9 %copy-done.1 = bf16[1,320,320]{2,1,0:T(8,128)(2,1)S(1)} copy-done((bf16[1,320,320]{2,1,0:T(8,128)(2,1)S(1)}, bf16[1,320,320]{2,1,0:T(8,128)(2,1)}, u32[]{:S(2)}) %copy-start.1) | copy-done | bytes 204824
  11.9 0.9 %copy-done.2 = bf16[1,320,320]{2,1,0:T(8,128)(2,1)S(1)} copy-done((bf16[1,320,320]{2,1,0:T(8,128)(2,1)S(1)}, bf16[1,320,320]{2,1,0:T(8,128)(2,1)}, u32[]{:S(2)}) %copy-start.2) | copy-done | bytes 204824
  12.8 0.9 %copy-done.3 = bf16[1,320,320]{2,1,0:T(8,128)(2,1)S(1)} copy-done((bf16[1,320,320]{2,1,0:T(8,128)(2,1)S(1)}, bf16[1,320,320]{2,1,0:T(8,128)(2,1)}, u32[]{:S(2)}) %copy-start.3) | copy-done | bytes 204824
  13.8 1.7 %shard_map.92.refs_1_.refs_3_.refs_6_ = bf16[960,320]{1,0:T(8,128)(2,1)S(1)} custom-call(s32[4]{0:T(128)S(1)} %pad_add_fusion.refs_0_, bf16[320,320]{1,0:T(8,128)(2,1)S(1)} %bitcast.12, bf16[320,320]{1,0:T(8,128)(2,1)S(1)} %bitcast.14, bf16[320,320]{1,0:T(8,128)(2,1)S(1)} %bitcast.16, bf16[320,320]{1,0:T(8,128)(2,1)S(1)} %collective-permute-done.2.refs_4_, ...), custom_call_target="tpu_custom_call" | custom-call | bytes 1048576 | tf_op jit(solution)/shard_map/pallas_call | solution.py:81
  15.6 1.6 %collective-permute-start.5 = (bf16[656,256]{1,0:T(8,128)(2,1)S(1)}, bf16[656,256]{1,0:T(8,128)(2,1)S(1)}, u32[]{:S(2)}, u32[]{:S(2)}) collective-permute-start(bf16[656,256]{1,0:T(8,128)(2,1)S(1)} %shard_map.93.refs_1_.refs_0_.refs_7_.refs_3_), channel_id=1, source_target_pairs={{0,2},{1,3},{2,0},{3,1},{4,6},{5,7},{6,4},{7,5},{8,10},{9,11},{10,... | collective-permute-start | bytes 1007624 | tf_op jit(solution)/shard_map/gather_0_2/ppermute | solution.py:32
  17.2 1.5 %collective-permute-start.6 = (bf16[656,256]{1,0:T(8,128)(2,1)S(1)}, bf16[656,256]{1,0:T(8,128)(2,1)S(1)}, u32[]{:S(2)}, u32[]{:S(2)}) collective-permute-start(bf16[656,256]{1,0:T(8,128)(2,1)S(1)} %shard_map.93.refs_1_.refs_0_.refs_7_.refs_3_), channel_id=1, source_target_pairs={{0,1},{1,0},{2,3},{3,2},{4,5},{5,4},{6,7},{7,6},{8,9},{9,8},{10,11... | collective-permute-start | bytes 1007624 | tf_op jit(solution)/shard_map/gather_0_1/ppermute | solution.py:32
  18.7 0.8 collective-permute-start.8
  19.6 5.9 %collective-permute-done.5.refs_0_.refs_2_ = bf16[656,256]{1,0:T(8,128)(2,1)S(1)} collective-permute-done((bf16[656,256]{1,0:T(8,128)(2,1)S(1)}, bf16[656,256]{1,0:T(8,128)(2,1)S(1)}, u32[]{:S(2)}, u32[]{:S(2)}) %collective-permute-start.5) | collective-permute-done | bytes 335904 | tf_op jit(solution)/shard_map/gather_0_2/ppermute | solution.py:32
  25.5 2.4 %collective-permute-done.6.refs_1_.refs_5_ = bf16[656,256]{1,0:T(8,128)(2,1)S(1)} collective-permute-done((bf16[656,256]{1,0:T(8,128)(2,1)S(1)}, bf16[656,256]{1,0:T(8,128)(2,1)S(1)}, u32[]{:S(2)}, u32[]{:S(2)}) %collective-permute-start.6) | collective-permute-done | bytes 335904 | tf_op jit(solution)/shard_map/gather_0_1/ppermute | solution.py:32
  28.0 1.6 %collective-permute-start.7 = (bf16[656,256]{1,0:T(8,128)(2,1)S(1)}, bf16[656,256]{1,0:T(8,128)(2,1)S(1)}, u32[]{:S(2)}, u32[]{:S(2)}) collective-permute-start(bf16[656,256]{1,0:T(8,128)(2,1)S(1)} %shard_map.94.refs_1_), channel_id=1, source_target_pairs={{0,1},{1,0},{2,3},{3,2},{4,5},{5,4},{6,7},{7,6},{8,9},{9,8},{10,11... | collective-permute-start | bytes 1007624 | tf_op jit(solution)/shard_map/gather_0_3/ppermute | solution.py:32
  30.3 6.1 %collective-permute-done.14.refs_2_ = bf16[656,256]{1,0:T(8,128)(2,1)S(1)} collective-permute-done((bf16[656,256]{1,0:T(8,128)(2,1)S(1)}, bf16[656,256]{1,0:T(8,128)(2,1)S(1)}, u32[]{:S(2)}, u32[]{:S(2)}) %collective-permute-start.14) | collective-permute-done | bytes 335904 | tf_op jit(solution)/shard_map/gather_1_2/ppermute | solution.py:32
  36.3 1.3 %collective-permute-start.15 = (bf16[656,256]{1,0:T(8,128)(2,1)S(1)}, bf16[656,256]{1,0:T(8,128)(2,1)S(1)}, u32[]{:S(2)}, u32[]{:S(2)}) collective-permute-start(bf16[656,256]{1,0:T(8,128)(2,1)S(1)} %collective-permute-done.14.refs_2_), channel_id=1, source_target_pairs={{0,1},{1,0},{2,3},{3,2},{4,5},{5,4},{6,7},{7,6},{8,9},{9,8},{10,11... | collective-permute-start | bytes 1007624 | tf_op jit(solution)/shard_map/gather_1_3/ppermute | solution.py:32
  37.6 2.1 %shard_map.96.refs_2_ = f32[960,320]{1,0:T(8,128)S(1)} custom-call(bf16[656,256]{1,0:T(8,128)(2,1)S(1)} %shard_map.93.refs_1_.refs_0_.refs_7_.refs_3_, bf16[656,256]{1,0:T(8,128)(2,1)S(1)} %collective-permute-done.6.refs_1_.refs_5_, bf16[656,256]{1,0:T(8,128)(2,1)S(1)} %collective-permute-done.5.refs_0_.refs_2_, ...), custom_call_target="tpu_custom_call" | custom-call | flops 1258291200 | bytes 1048576 | tf_op jit(solution)/shard_map/pallas_call | solution.py:81
  39.8 1.0 %shard_map.97 = (bf16[320,384]{1,0:T(8,128)(2,1)S(1)}, bf16[320,384]{1,0:T(8,128)(2,1)S(1)}, bf16[320,384]{1,0:T(8,128)(2,1)S(1)}) custom-call(bf16[656,256]{1,0:T(8,128)(2,1)S(1)} %collective-permute-done.7.refs_0_.refs_6_, bf16[960,320]{1,0:T(8,128)(2,1)S(1)} %shard_map.92.refs_1_.refs_3_.refs_6_, f32[960,320]{1,0:T(8,128)S(1)} %shard_map.96.refs_2_), custom_call_target="tpu_custom_call" | custom-call | bytes 1048576 | tf_op jit(solution)/shard_map/pallas_call | solution.py:81
  40.8 2.8 %collective-permute-start.9 = (bf16[320,384]{1,0:T(8,128)(2,1)S(1)}, bf16[320,384]{1,0:T(8,128)(2,1)S(1)}, u32[]{:S(2)}, u32[]{:S(2)}) collective-permute-start(bf16[320,384]{1,0:T(8,128)(2,1)S(1)} %get-tuple-element.26.refs_0_), channel_id=1, source_target_pairs={{0,8},{1,9},{2,10},{3,11},{4,12},{5,13},{6,14},{7,15},{8,0},{9,1},... | collective-permute-start | bytes 737288 | tf_op jit(solution)/shard_map/swap_0/ppermute | solution.py:32
  44.1 1.2 %collective-permute-start.13 = (bf16[656,256]{1,0:T(8,128)(2,1)S(1)}, bf16[656,256]{1,0:T(8,128)(2,1)S(1)}, u32[]{:S(2)}, u32[]{:S(2)}) collective-permute-start(bf16[656,256]{1,0:T(8,128)(2,1)S(1)} %shard_map.99.refs_0_), channel_id=1, source_target_pairs={{0,1},{1,0},{2,3},{3,2},{4,5},{5,4},{6,7},{7,6},{8,9},{9,8},{10,11... | collective-permute-start | bytes 1007624 | tf_op jit(solution)/shard_map/gather_1_1/ppermute | solution.py:32
  45.3 3.2 %collective-permute-start.12 = (bf16[656,256]{1,0:T(8,128)(2,1)S(1)}, bf16[656,256]{1,0:T(8,128)(2,1)S(1)}, u32[]{:S(2)}, u32[]{:S(2)}) collective-permute-start(bf16[656,256]{1,0:T(8,128)(2,1)S(1)} %collective-permute-done.7.refs_0_.refs_6_), channel_id=1, source_target_pairs={{0,8},{1,9},{2,10},{3,11},{4,12},{5,13},{6,14},{7,15},{8,0},{9,1},... | collective-permute-start | bytes 1007624 | tf_op jit(solution)/shard_map/last_0/ppermute | solution.py:32
  48.6 4.1 %shard_map.98.refs_2_.refs_4_.refs_7_ = bf16[960,320]{1,0:T(8,128)(2,1)S(1)} custom-call(bf16[320,384]{1,0:T(8,128)(2,1)S(1)} %get-tuple-element.26.refs_0_, bf16[320,384]{1,0:T(8,128)(2,1)S(1)} %get-tuple-element.27.refs_1_, bf16[320,384]{1,0:T(8,128)(2,1)S(1)} %get-tuple-element.28.refs_2_, bf16[320,384]{1,0:T(8,128)(2,1)S(1)} %collective-permute-done.9.refs_3_, ...), custom_call_target="tpu_custom_call" | custom-call | flops 1769472000 | bytes 1048576 | tf_op jit(solution)/shard_map/pallas_call | solution.py:81
  52.8 2.9 %shard_map.102 = (bf16[320,384]{1,0:T(8,128)(2,1)S(1)}, bf16[320,384]{1,0:T(8,128)(2,1)S(1)}, bf16[320,384]{1,0:T(8,128)(2,1)S(1)}) custom-call(bf16[656,256]{1,0:T(8,128)(2,1)S(1)} %shard_map.99.refs_0_, bf16[656,256]{1,0:T(8,128)(2,1)S(1)} %collective-permute-done.13.refs_8_.refs_1_, bf16[656,256]{1,0:T(8,128)(2,1)S(1)} %collective-permute-done.14.refs_2_, ...), custom_call_target="tpu_custom_call" | custom-call | flops 1258291200 | bytes 1048576 | tf_op jit(solution)/shard_map/pallas_call | solution.py:81
  55.6 2.0 %collective-permute-start.21 = (bf16[320,384]{1,0:T(8,128)(2,1)S(1)}, bf16[320,384]{1,0:T(8,128)(2,1)S(1)}, u32[]{:S(2)}, u32[]{:S(2)}) collective-permute-start(bf16[320,384]{1,0:T(8,128)(2,1)S(1)} %get-tuple-element.35.refs_1_), channel_id=1, source_target_pairs={{0,8},{1,9},{2,10},{3,11},{4,12},{5,13},{6,14},{7,15},{8,0},{9,1},... | collective-permute-start | bytes 737288 | tf_op jit(solution)/shard_map/swap_1/ppermute | solution.py:32
  58.1 2.5 %shard_map.100 = (bf16[3,64,320]{2,1,0:T(8,128)(2,1)S(1)}, bf16[3,64,320]{2,1,0:T(8,128)(2,1)S(1)}, bf16[3,64,320]{2,1,0:T(8,128)(2,1)S(1)}, bf16[3,64,320]{2,1,0:T(8,128)(2,1)S(1)}, bf16[256,320]{1,0:T(8,128)(2,1)S(1)}) custom-call(s32[4]{0:T(128)S(1)} %pad_add_fusion.refs_0_, bf16[2,320,256]{2,1,0:T(8,128)(2,1)S(1)} %collective-permute-done.refs_8_.refs_1_, ...), custom_call_target="tpu_custom_call" | custom-call | flops 335544320 | bytes 1048576 | tf_op jit(solution)/shard_map/pallas_call | solution.py:81
  61.2 3.8 %collective-permute-start.18 = (bf16[3,64,320]{2,1,0:T(8,128)(2,1)S(1)}, bf16[3,64,320]{2,1,0:T(8,128)(2,1)S(1)}, u32[]{:S(2)}, u32[]{:S(2)}) collective-permute-start(bf16[3,64,320]{2,1,0:T(8,128)(2,1)S(1)} %get-tuple-element.30), channel_id=1, source_target_pairs={{0,8},{1,9},{2,10},{3,11},{4,16},{5,17},{6,18},{7,19},{8,12},{9,13... | collective-permute-start | bytes 368648 | tf_op jit(solution)/shard_map/spread_early_1/ppermute | solution.py:32
  65.1 1.5 %collective-permute-start.19 = (bf16[3,64,320]{2,1,0:T(8,128)(2,1)S(1)}, bf16[3,64,320]{2,1,0:T(8,128)(2,1)S(1)}, u32[]{:S(2)}, u32[]{:S(2)}) collective-permute-start(bf16[3,64,320]{2,1,0:T(8,128)(2,1)S(1)} %get-tuple-element.31), channel_id=1, source_target_pairs={{0,16},{1,17},{2,18},{3,19},{4,24},{5,25},{6,26},{7,27},{8,20},{9,... | collective-permute-start | bytes 368648 | tf_op jit(solution)/shard_map/spread_early_2/ppermute | solution.py:32
  66.6 5.2 %shard_map.103 = (bf16[64,320]{1,0:T(8,128)(2,1)S(1)}, bf16[64,320]{1,0:T(8,128)(2,1)S(1)}, bf16[64,320]{1,0:T(8,128)(2,1)S(1)}, bf16[64,320]{1,0:T(8,128)(2,1)S(1)}) custom-call(s32[4]{0:T(128)S(1)} %pad_add_fusion.refs_0_, bf16[320,384]{1,0:T(8,128)(2,1)S(1)} %get-tuple-element.35.refs_1_, bf16[320,384]{1,0:T(8,128)(2,1)S(1)} %get-tuple-element.36.refs_2_, ...), custom_call_target="tpu_custom_call" | custom-call | flops 1769472000 | bytes 1048576 | tf_op jit(solution)/shard_map/pallas_call | solution.py:81
  72.4 4.3 %collective-permute-start.25 = (bf16[64,320]{1,0:T(8,128)(2,1)S(1)}, bf16[64,320]{1,0:T(8,128)(2,1)S(1)}, u32[]{:S(2)}, u32[]{:S(2)}) collective-permute-start(bf16[64,320]{1,0:T(8,128)(2,1)S(1)} %get-tuple-element.40), channel_id=1, source_target_pairs={{0,8},{1,9},{2,10},{3,11},{4,16},{5,17},{6,18},{7,19},{8,12},{9,13... | collective-permute-start | bytes 122888 | tf_op jit(solution)/shard_map/spread_late_1/ppermute | solution.py:32
  77.5 1.1 %collective-permute-start.27 = (bf16[64,320]{1,0:T(8,128)(2,1)S(1)}, bf16[64,320]{1,0:T(8,128)(2,1)S(1)}, u32[]{:S(2)}, u32[]{:S(2)}) collective-permute-start(bf16[64,320]{1,0:T(8,128)(2,1)S(1)} %get-tuple-element.42), channel_id=1, source_target_pairs={{0,24},{1,25},{2,26},{3,27},{4,0},{5,1},{6,2},{7,3},{8,28},{9,29},... | collective-permute-start | bytes 122888 | tf_op jit(solution)/shard_map/spread_late_3/ppermute | solution.py:32
  79.2 1.1 %shard_map.101 = (f32[2,1,64,1280]{3,2,1,0:T(8,128)}, f32[64,1280]{1,0:T(8,128)S(1)}) custom-call(s32[1]{0:T(128)} %bitcast.refs_0_, f32[2,1280]{1,0:T(2,128)S(1)} %copy-done.4, bf16[3,64,320]{2,1,0:T(8,128)(2,1)S(1)} %collective-permute-done.17.refs_2_, bf16[3,64,320]{2,1,0:T(8,128)(2,1)S(1)} %collective-permute-done.18.refs_3_, ...), custom_call_target="tpu_custom_call" | custom-call | bytes 1048576 | tf_op jit(solution)/shard_map/pallas_call | solution.py:81
  80.4 2.0 %collective-permute-done.25.refs_5_ = bf16[64,320]{1,0:T(8,128)(2,1)S(1)} collective-permute-done((bf16[64,320]{1,0:T(8,128)(2,1)S(1)}, bf16[64,320]{1,0:T(8,128)(2,1)S(1)}, u32[]{:S(2)}, u32[]{:S(2)}) %collective-permute-start.25) | collective-permute-done | bytes 40992 | tf_op jit(solution)/shard_map/spread_late_1/ppermute | solution.py:32
  82.6 1.0 %shard_map.104 = f32[2,1,64,1280]{3,2,1,0:T(8,128)} custom-call(s32[1]{0:T(128)} %bitcast.refs_0_, f32[2,1280]{1,0:T(2,128)S(1)} %copy-done.4, f32[2,1,64,1280]{3,2,1,0:T(8,128)} %get-tuple-element.33.refs_2_, f32[64,1280]{1,0:T(8,128)S(1)} %get-tuple-element.34.refs_3_, ...), custom_call_target="tpu_custom_call", output_to_operand_aliasing={{}: (2, {})} | custom-call | bytes 1048576 | tf_op jit(solution)/shard_map/pallas_call | solution.py:81
  (51 shorter events, 7.0 us)
Async XLA Ops:
  2.7 12.8 %collective-permute-start.1 = (bf16[656,256]{1,0:T(8,128)(2,1)}, bf16[656,256]{1,0:T(8,128)(2,1)S(1)}, u32[]{:S(2)}, u32[]{:S(2)}) collective-permute-start(bf16[656,256]{1,0:T(8,128)(2,1)} %get-tuple-element.24), channel_id=1, source_target_pairs={{0,0},{1,1},{2,2},{3,3},{4,8},{5,9},{6,10},{7,11},{8,4},{9,5},{10,... | collective-permute-start | bytes 1007624 | tf_op jit(solution)/shard_map/regroup_0/ppermute | solution.py:32
  4.4 5.8 %collective-permute-start.2 = (bf16[320,320]{1,0:T(8,128)(2,1)}, bf16[320,320]{1,0:T(8,128)(2,1)S(1)}, u32[]{:S(2)}, u32[]{:S(2)}) collective-permute-start(bf16[320,320]{1,0:T(8,128)(2,1)} %bitcast.11), channel_id=1, source_target_pairs={{0,8},{1,9},{2,10},{3,11},{4,12},{5,13},{6,14},{7,15},{8,0},{9,1},... | collective-permute-start | bytes 614408 | tf_op jit(solution)/shard_map/lend_0/ppermute | solution.py:32
  8.9 1.7 %collective-permute-start.3 = (bf16[320,320]{1,0:T(8,128)(2,1)}, bf16[320,320]{1,0:T(8,128)(2,1)S(1)}, u32[]{:S(2)}, u32[]{:S(2)}) collective-permute-start(bf16[320,320]{1,0:T(8,128)(2,1)} %bitcast.13), channel_id=1, source_target_pairs={{0,8},{1,9},{2,10},{3,11},{4,12},{5,13},{6,14},{7,15},{8,0},{9,1},... | collective-permute-start | bytes 614408 | tf_op jit(solution)/shard_map/lend_1/ppermute | solution.py:32
  8.9 2.0 %collective-permute-start.4 = (bf16[320,320]{1,0:T(8,128)(2,1)}, bf16[320,320]{1,0:T(8,128)(2,1)S(1)}, u32[]{:S(2)}, u32[]{:S(2)}) collective-permute-start(bf16[320,320]{1,0:T(8,128)(2,1)} %bitcast.15), channel_id=1, source_target_pairs={{0,8},{1,9},{2,10},{3,11},{4,12},{5,13},{6,14},{7,15},{8,0},{9,1},... | collective-permute-start | bytes 614408 | tf_op jit(solution)/shard_map/lend_2/ppermute | solution.py:32
  9.4 9.3 %copy-start = (bf16[656,256]{1,0:T(8,128)(2,1)S(1)}, bf16[656,256]{1,0:T(8,128)(2,1)}, u32[]{:S(2)}) copy-start(bf16[656,256]{1,0:T(8,128)(2,1)} %get-tuple-element.25.refs_0_) | copy-start | bytes 1007620
  10.9 0.9 %copy-start.1 = (bf16[1,320,320]{2,1,0:T(8,128)(2,1)S(1)}, bf16[1,320,320]{2,1,0:T(8,128)(2,1)}, u32[]{:S(2)}) copy-start(bf16[1,320,320]{2,1,0:T(8,128)(2,1)} %param.13) | copy-start | bytes 614404
  15.6 9.9 %collective-permute-start.5 = (bf16[656,256]{1,0:T(8,128)(2,1)S(1)}, bf16[656,256]{1,0:T(8,128)(2,1)S(1)}, u32[]{:S(2)}, u32[]{:S(2)}) collective-permute-start(bf16[656,256]{1,0:T(8,128)(2,1)S(1)} %shard_map.93.refs_1_.refs_0_.refs_7_.refs_3_), channel_id=1, source_target_pairs={{0,2},{1,3},{2,0},{3,1},{4,6},{5,7},{6,4},{7,5},{8,10},{9,11},{10,... | collective-permute-start | bytes 1007624 | tf_op jit(solution)/shard_map/gather_0_2/ppermute | solution.py:32
  17.2 10.7 %collective-permute-start.6 = (bf16[656,256]{1,0:T(8,128)(2,1)S(1)}, bf16[656,256]{1,0:T(8,128)(2,1)S(1)}, u32[]{:S(2)}, u32[]{:S(2)}) collective-permute-start(bf16[656,256]{1,0:T(8,128)(2,1)S(1)} %shard_map.93.refs_1_.refs_0_.refs_7_.refs_3_), channel_id=1, source_target_pairs={{0,1},{1,0},{2,3},{3,2},{4,5},{5,4},{6,7},{7,6},{8,9},{9,8},{10,11... | collective-permute-start | bytes 1007624 | tf_op jit(solution)/shard_map/gather_0_1/ppermute | solution.py:32
  18.7 10.9 %copy-start.5 = (bf16[2,256,320]{1,2,0:T(8,128)(2,1)S(1)}, bf16[2,256,320]{1,2,0:T(8,128)(2,1)}, u32[]{:S(2)}) copy-start(bf16[2,256,320]{1,2,0:T(8,128)(2,1)} %param.9) | copy-start | bytes 983044
  18.7 9.1 %collective-permute-start.8 = (bf16[656,256]{1,0:T(8,128)(2,1)S(1)}, bf16[656,256]{1,0:T(8,128)(2,1)S(1)}, u32[]{:S(2)}, u32[]{:S(2)}) collective-permute-start(bf16[656,256]{1,0:T(8,128)(2,1)S(1)} %shard_map.95), channel_id=1, source_target_pairs={{0,0},{1,1},{2,2},{3,3},{4,8},{5,9},{6,10},{7,11},{8,4},{9,5},{10,... | collective-permute-start | bytes 1007624 | tf_op jit(solution)/shard_map/regroup_1/ppermute | solution.py:32
  27.9 8.4 %collective-permute-start.14 = (bf16[656,256]{1,0:T(8,128)(2,1)S(1)}, bf16[656,256]{1,0:T(8,128)(2,1)S(1)}, u32[]{:S(2)}, u32[]{:S(2)}) collective-permute-start(bf16[656,256]{1,0:T(8,128)(2,1)S(1)} %shard_map.99.refs_0_), channel_id=1, source_target_pairs={{0,2},{1,3},{2,0},{3,1},{4,6},{5,7},{6,4},{7,5},{8,10},{9,11},{10,... | collective-permute-start | bytes 1007624 | tf_op jit(solution)/shard_map/gather_1_2/ppermute | solution.py:32
  28.0 11.8 %collective-permute-start.7 = (bf16[656,256]{1,0:T(8,128)(2,1)S(1)}, bf16[656,256]{1,0:T(8,128)(2,1)S(1)}, u32[]{:S(2)}, u32[]{:S(2)}) collective-permute-start(bf16[656,256]{1,0:T(8,128)(2,1)S(1)} %shard_map.94.refs_1_), channel_id=1, source_target_pairs={{0,1},{1,0},{2,3},{3,2},{4,5},{5,4},{6,7},{7,6},{8,9},{9,8},{10,11... | collective-permute-start | bytes 1007624 | tf_op jit(solution)/shard_map/gather_0_3/ppermute | solution.py:32
  29.6 14.5 %collective-permute-start = (bf16[2,320,256]{2,1,0:T(8,128)(2,1)S(1)}, bf16[2,320,256]{2,1,0:T(8,128)(2,1)S(1)}, u32[]{:S(2)}, u32[]{:S(2)}) collective-permute-start(bf16[2,320,256]{2,1,0:T(8,128)(2,1)S(1)} %bitcast.19), channel_id=1, source_target_pairs={{0,0},{1,1},{2,2},{3,3},{4,8},{5,9},{6,10},{7,11},{8,4},{9,5},{10,... | collective-permute-start | bytes 983048 | tf_op jit(solution)/shard_map/regroup_queries/ppermute | solution.py:32
  36.3 12.2 %collective-permute-start.15 = (bf16[656,256]{1,0:T(8,128)(2,1)S(1)}, bf16[656,256]{1,0:T(8,128)(2,1)S(1)}, u32[]{:S(2)}, u32[]{:S(2)}) collective-permute-start(bf16[656,256]{1,0:T(8,128)(2,1)S(1)} %collective-permute-done.14.refs_2_), channel_id=1, source_target_pairs={{0,1},{1,0},{2,3},{3,2},{4,5},{5,4},{6,7},{7,6},{8,9},{9,8},{10,11... | collective-permute-start | bytes 1007624 | tf_op jit(solution)/shard_map/gather_1_3/ppermute | solution.py:32
  40.8 4.5 %collective-permute-start.9 = (bf16[320,384]{1,0:T(8,128)(2,1)S(1)}, bf16[320,384]{1,0:T(8,128)(2,1)S(1)}, u32[]{:S(2)}, u32[]{:S(2)}) collective-permute-start(bf16[320,384]{1,0:T(8,128)(2,1)S(1)} %get-tuple-element.26.refs_0_), channel_id=1, source_target_pairs={{0,8},{1,9},{2,10},{3,11},{4,12},{5,13},{6,14},{7,15},{8,0},{9,1},... | collective-permute-start | bytes 737288 | tf_op jit(solution)/shard_map/swap_0/ppermute | solution.py:32
  43.6 5.0 %collective-permute-start.10 = (bf16[320,384]{1,0:T(8,128)(2,1)S(1)}, bf16[320,384]{1,0:T(8,128)(2,1)S(1)}, u32[]{:S(2)}, u32[]{:S(2)}) collective-permute-start(bf16[320,384]{1,0:T(8,128)(2,1)S(1)} %get-tuple-element.27.refs_1_), channel_id=1, source_target_pairs={{0,8},{1,9},{2,10},{3,11},{4,12},{5,13},{6,14},{7,15},{8,0},{9,1},... | collective-permute-start | bytes 737288 | tf_op jit(solution)/shard_map/swap_0/ppermute | solution.py:32
  43.6 5.0 %collective-permute-start.11 = (bf16[320,384]{1,0:T(8,128)(2,1)S(1)}, bf16[320,384]{1,0:T(8,128)(2,1)S(1)}, u32[]{:S(2)}, u32[]{:S(2)}) collective-permute-start(bf16[320,384]{1,0:T(8,128)(2,1)S(1)} %get-tuple-element.28.refs_2_), channel_id=1, source_target_pairs={{0,8},{1,9},{2,10},{3,11},{4,12},{5,13},{6,14},{7,15},{8,0},{9,1},... | collective-permute-start | bytes 737288 | tf_op jit(solution)/shard_map/swap_0/ppermute | solution.py:32
  44.1 8.7 %collective-permute-start.13 = (bf16[656,256]{1,0:T(8,128)(2,1)S(1)}, bf16[656,256]{1,0:T(8,128)(2,1)S(1)}, u32[]{:S(2)}, u32[]{:S(2)}) collective-permute-start(bf16[656,256]{1,0:T(8,128)(2,1)S(1)} %shard_map.99.refs_0_), channel_id=1, source_target_pairs={{0,1},{1,0},{2,3},{3,2},{4,5},{5,4},{6,7},{7,6},{8,9},{9,8},{10,11... | collective-permute-start | bytes 1007624 | tf_op jit(solution)/shard_map/gather_1_1/ppermute | solution.py:32
  45.3 12.8 %collective-permute-start.12 = (bf16[656,256]{1,0:T(8,128)(2,1)S(1)}, bf16[656,256]{1,0:T(8,128)(2,1)S(1)}, u32[]{:S(2)}, u32[]{:S(2)}) collective-permute-start(bf16[656,256]{1,0:T(8,128)(2,1)S(1)} %collective-permute-done.7.refs_0_.refs_6_), channel_id=1, source_target_pairs={{0,8},{1,9},{2,10},{3,11},{4,12},{5,13},{6,14},{7,15},{8,0},{9,1},... | collective-permute-start | bytes 1007624 | tf_op jit(solution)/shard_map/last_0/ppermute | solution.py:32
  48.5 9.6 %collective-permute-start.16 = (bf16[656,256]{1,0:T(8,128)(2,1)S(1)}, bf16[656,256]{1,0:T(8,128)(2,1)S(1)}, u32[]{:S(2)}, u32[]{:S(2)}) collective-permute-start(bf16[656,256]{1,0:T(8,128)(2,1)S(1)} %collective-permute-done.15.refs_9_.refs_3_), channel_id=1, source_target_pairs={{0,8},{1,9},{2,10},{3,11},{4,12},{5,13},{6,14},{7,15},{8,0},{9,1},... | collective-permute-start | bytes 1007624 | tf_op jit(solution)/shard_map/last_1/ppermute | solution.py:32
  55.6 9.5 %collective-permute-start.21 = (bf16[320,384]{1,0:T(8,128)(2,1)S(1)}, bf16[320,384]{1,0:T(8,128)(2,1)S(1)}, u32[]{:S(2)}, u32[]{:S(2)}) collective-permute-start(bf16[320,384]{1,0:T(8,128)(2,1)S(1)} %get-tuple-element.35.refs_1_), channel_id=1, source_target_pairs={{0,8},{1,9},{2,10},{3,11},{4,12},{5,13},{6,14},{7,15},{8,0},{9,1},... | collective-permute-start | bytes 737288 | tf_op jit(solution)/shard_map/swap_1/ppermute | solution.py:32
  57.6 9.0 %collective-permute-start.22 = (bf16[320,384]{1,0:T(8,128)(2,1)S(1)}, bf16[320,384]{1,0:T(8,128)(2,1)S(1)}, u32[]{:S(2)}, u32[]{:S(2)}) collective-permute-start(bf16[320,384]{1,0:T(8,128)(2,1)S(1)} %get-tuple-element.36.refs_2_), channel_id=1, source_target_pairs={{0,8},{1,9},{2,10},{3,11},{4,12},{5,13},{6,14},{7,15},{8,0},{9,1},... | collective-permute-start | bytes 737288 | tf_op jit(solution)/shard_map/swap_1/ppermute | solution.py:32
  57.7 8.9 %collective-permute-start.23 = (bf16[320,384]{1,0:T(8,128)(2,1)S(1)}, bf16[320,384]{1,0:T(8,128)(2,1)S(1)}, u32[]{:S(2)}, u32[]{:S(2)}) collective-permute-start(bf16[320,384]{1,0:T(8,128)(2,1)S(1)} %get-tuple-element.37.refs_3_), channel_id=1, source_target_pairs={{0,8},{1,9},{2,10},{3,11},{4,12},{5,13},{6,14},{7,15},{8,0},{9,1},... | collective-permute-start | bytes 737288 | tf_op jit(solution)/shard_map/swap_1/ppermute | solution.py:32
  60.6 11.9 %collective-permute-start.17 = (bf16[3,64,320]{2,1,0:T(8,128)(2,1)S(1)}, bf16[3,64,320]{2,1,0:T(8,128)(2,1)S(1)}, u32[]{:S(2)}, u32[]{:S(2)}) collective-permute-start(bf16[3,64,320]{2,1,0:T(8,128)(2,1)S(1)} %get-tuple-element.29), channel_id=1, source_target_pairs={{0,0},{1,1},{2,2},{3,3},{4,8},{5,9},{6,10},{7,11},{8,4},{9,5},{10,... | collective-permute-start | bytes 368648 | tf_op jit(solution)/shard_map/spread_early_0/ppermute | solution.py:32
  61.2 15.8 %collective-permute-start.18 = (bf16[3,64,320]{2,1,0:T(8,128)(2,1)S(1)}, bf16[3,64,320]{2,1,0:T(8,128)(2,1)S(1)}, u32[]{:S(2)}, u32[]{:S(2)}) collective-permute-start(bf16[3,64,320]{2,1,0:T(8,128)(2,1)S(1)} %get-tuple-element.30), channel_id=1, source_target_pairs={{0,8},{1,9},{2,10},{3,11},{4,16},{5,17},{6,18},{7,19},{8,12},{9,13... | collective-permute-start | bytes 368648 | tf_op jit(solution)/shard_map/spread_early_1/ppermute | solution.py:32
  65.1 12.5 %collective-permute-start.19 = (bf16[3,64,320]{2,1,0:T(8,128)(2,1)S(1)}, bf16[3,64,320]{2,1,0:T(8,128)(2,1)S(1)}, u32[]{:S(2)}, u32[]{:S(2)}) collective-permute-start(bf16[3,64,320]{2,1,0:T(8,128)(2,1)S(1)} %get-tuple-element.31), channel_id=1, source_target_pairs={{0,16},{1,17},{2,18},{3,19},{4,24},{5,25},{6,26},{7,27},{8,20},{9,... | collective-permute-start | bytes 368648 | tf_op jit(solution)/shard_map/spread_early_2/ppermute | solution.py:32
  66.6 12.7 %collective-permute-start.20 = (bf16[3,64,320]{2,1,0:T(8,128)(2,1)S(1)}, bf16[3,64,320]{2,1,0:T(8,128)(2,1)S(1)}, u32[]{:S(2)}, u32[]{:S(2)}) collective-permute-start(bf16[3,64,320]{2,1,0:T(8,128)(2,1)S(1)} %get-tuple-element.32), channel_id=1, source_target_pairs={{0,24},{1,25},{2,26},{3,27},{4,0},{5,1},{6,2},{7,3},{8,28},{9,29},... | collective-permute-start | bytes 368648 | tf_op jit(solution)/shard_map/spread_early_3/ppermute | solution.py:32
  66.6 12.7 %copy-start.4 = (f32[2,1280]{1,0:T(2,128)S(1)}, f32[2,1280]{1,0:T(2,128)}, u32[]{:S(2)}) copy-start(f32[2,1280]{1,0:T(2,128)} %refs_1_.3) | copy-start | bytes 30724
  71.8 8.6 %collective-permute-start.24 = (bf16[64,320]{1,0:T(8,128)(2,1)S(1)}, bf16[64,320]{1,0:T(8,128)(2,1)S(1)}, u32[]{:S(2)}, u32[]{:S(2)}) collective-permute-start(bf16[64,320]{1,0:T(8,128)(2,1)S(1)} %get-tuple-element.39), channel_id=1, source_target_pairs={{0,0},{1,1},{2,2},{3,3},{4,8},{5,9},{6,10},{7,11},{8,4},{9,5},{10,... | collective-permute-start | bytes 122888 | tf_op jit(solution)/shard_map/spread_late_0/ppermute | solution.py:32
  72.4 9.9 %collective-permute-start.25 = (bf16[64,320]{1,0:T(8,128)(2,1)S(1)}, bf16[64,320]{1,0:T(8,128)(2,1)S(1)}, u32[]{:S(2)}, u32[]{:S(2)}) collective-permute-start(bf16[64,320]{1,0:T(8,128)(2,1)S(1)} %get-tuple-element.40), channel_id=1, source_target_pairs={{0,8},{1,9},{2,10},{3,11},{4,16},{5,17},{6,18},{7,19},{8,12},{9,13... | collective-permute-start | bytes 122888 | tf_op jit(solution)/shard_map/spread_late_1/ppermute | solution.py:32
  77.0 5.4 %collective-permute-start.26 = (bf16[64,320]{1,0:T(8,128)(2,1)S(1)}, bf16[64,320]{1,0:T(8,128)(2,1)S(1)}, u32[]{:S(2)}, u32[]{:S(2)}) collective-permute-start(bf16[64,320]{1,0:T(8,128)(2,1)S(1)} %get-tuple-element.41), channel_id=1, source_target_pairs={{0,16},{1,17},{2,18},{3,19},{4,24},{5,25},{6,26},{7,27},{8,20},{9,... | collective-permute-start | bytes 122888 | tf_op jit(solution)/shard_map/spread_late_2/ppermute | solution.py:32
  77.5 5.1 %collective-permute-start.27 = (bf16[64,320]{1,0:T(8,128)(2,1)S(1)}, bf16[64,320]{1,0:T(8,128)(2,1)S(1)}, u32[]{:S(2)}, u32[]{:S(2)}) collective-permute-start(bf16[64,320]{1,0:T(8,128)(2,1)S(1)} %get-tuple-element.42), channel_id=1, source_target_pairs={{0,24},{1,25},{2,26},{3,27},{4,0},{5,1},{6,2},{7,3},{8,28},{9,29},... | collective-permute-start | bytes 122888 | tf_op jit(solution)/shard_map/spread_late_3/ppermute | solution.py:32
  (2 other events, 1.9 us)

commit v5 on v4

--- a/solution.py
+++ b/solution.py
@@ -180,10 +180,10 @@
     main = size - size % 256
     if main in (0, size):
         return product(slice(0, size), slice(0, size)).astype(BF16)
-    left = product(slice(0, size), slice(0, main))
+    left = product(slice(0, size), slice(0, main)).astype(BF16)
     corner = product(slice(main, size), slice(main, size)).astype(BF16)
-    right = jnp.concatenate([left[main:].T.astype(BF16), corner], 0)
-    return jnp.concatenate([left.astype(BF16), right], 1)
+    right = jnp.concatenate([left[main:].T, corner], 0)
+    return jnp.concatenate([left, right], 1)
 
 
 def square_of(x):
@@ -442,23 +442,22 @@
         own.append(send(tied(blocks[s], own[-1]), regroup, f"regroup_{s}"))
     queries = send(turned(query_rows), regroup, "regroup_queries")
 
-    here = []
-    for s in range(segments):
-        got = {0: tied(own[s], gate) if s else own[s]}
+    def gathered(s, block, others):
+        got = {0: block}
         step = half // 2
         while step:
             for mask in sorted(got):
-                block = got[mask]
-                if s == 0 and mask and step == 1:
-                    block = gate = tied(block, got[1])
+                one = got[mask]
+                if mask and step == 1:
+                    one = gates[s] = tied(one, *(others or [got[1]]))
                 got[mask | step] = send(
-                    block,
-                    lambda h, t, step=step: (h, t ^ step),
-                    f"gather_{s}_{mask | step}",
+                    one, lambda h, t, step=step: (h, t ^ step), f"gather_{s}_{mask | step}"
                 )
             step //= 2
-        here.append([got[mask] for mask in range(half)])
-
+        return [got[mask] for mask in range(half)]
+
+    gates = {}
+    here = [gathered(0, own[0], [])]
     grad_shapes = (jax.ShapeDtypeStruct((width, padded), BF16),) * 3
     total = pltpu.VMEM((3 * width, width), F32)
     grad_flops = 2 * 6 * half * rows * width * width
@@ -471,6 +470,8 @@
         waits=own[1:],
         flops=grad_flops,
     )
+    for s in range(1, segments):
+        here.append(gathered(s, tied(own[s], gates[0]), [before]))
     mine = call(second_kernel, grad_shapes, (here[0][-1], weights, before), (total,))
     all_weights = []
     for s in range(1, segments):

time: 84.1 us -> 84.1 us (level)
  starting transfers between devices: 37.1 us -> 39.3 us
  waiting for transfers between devices: 19 us -> 16.9 us
    ppermute x28, starting transfers between devices: 37.1 us -> 39.3 us  [moved(): return lax.ppermute(array, BOTH, pairs)]
    ppermute x28, waiting for transfers between devices: 19 us -> 16.9 us  [moved(): return lax.ppermute(array, BOTH, pairs)]
    pallas_call x14 -> x15, Pallas kernels: 23.8 us -> 23.7 us  [call(): pl.pallas_call(body, out_shape=shapes, in_specs=specs, out_specs=tuple((p...]
where the time goes in v5:
time: 84.1 us; the launch traced here: 83.8 us
  starting transfers between devices  39.3 us (47%)
  Pallas kernels  23.7 us (28%)
  waiting for transfers between devices  16.9 us (20%)
  local copies, waits for them, and re-layouts  2.85 us (3%)
  between operations  1.01 us (1%)
    ppermute x28, starting transfers between devices, moved(): return lax.ppermute(array, BOTH, pairs)  39.3 us
    pallas_call x15, Pallas kernels, call(): pl.pallas_call(body, out_shape=shapes, in_specs=specs, out_specs=tuple((p...  23.7 us
    ppermute x28, waiting for transfers between devices, moved(): return lax.ppermute(array, BOTH, pairs)  16.9 us
    unnamed x12, local copies, waits for them, and re-layouts  2.85 us
  transfers between devices with their start and end apart: 28, of which 10 were waited for; matrix products, arithmetic and copies ran while one was open for 0% of the time, Pallas kernels for 25%

profile of v5, /device:TPU:0, one launch (start us, length us, event | category | flops | bytes accessed | tf_op | source)
XLA Modules:
  0.0 83.8 jit_solution(2082480664218381636)
XLA Ops:
  0.7 2.1 %shard_map.91 = (bf16[656,256]{1,0:T(8,128)(2,1)}, bf16[656,256]{1,0:T(8,128)(2,1)}) custom-call(bf16[2,320,256]{2,1,0:T(8,128)(2,1)} %bitcast.17, bf16[2,320,256]{2,1,0:T(8,128)(2,1)} %bitcast.18, f32[2,1,256]{2,1,0:T(1,128)} %refs_2_.1, f32[1]{0:T(128)S(6)} %copy.12.refs_3_), custom_call_target="tpu_custom_call" | custom-call | bytes 1048576 | tf_op jit(solution)/shard_map/pallas_call | solution.py:81
  2.7 1.6 %collective-permute-start.1 = (bf16[656,256]{1,0:T(8,128)(2,1)}, bf16[656,256]{1,0:T(8,128)(2,1)S(1)}, u32[]{:S(2)}, u32[]{:S(2)}) collective-permute-start(bf16[656,256]{1,0:T(8,128)(2,1)} %get-tuple-element.24), channel_id=1, source_target_pairs={{0,0},{1,1},{2,2},{3,3},{4,8},{5,9},{6,10},{7,11},{8,4},{9,5},{10,... | collective-permute-start | bytes 1007624 | tf_op jit(solution)/shard_map/regroup_0/ppermute | solution.py:32
  4.4 4.5 %collective-permute-start.2 = (bf16[320,320]{1,0:T(8,128)(2,1)}, bf16[320,320]{1,0:T(8,128)(2,1)S(1)}, u32[]{:S(2)}, u32[]{:S(2)}) collective-permute-start(bf16[320,320]{1,0:T(8,128)(2,1)} %bitcast.11), channel_id=1, source_target_pairs={{0,8},{1,9},{2,10},{3,11},{4,12},{5,13},{6,14},{7,15},{8,0},{9,1},... | collective-permute-start | bytes 614408 | tf_op jit(solution)/shard_map/lend_0/ppermute | solution.py:32
  9.4 0.8 collective-permute-done.2.refs_4_
  10.9 0.9 %copy-done.1 = bf16[1,320,320]{2,1,0:T(8,128)(2,1)S(1)} copy-done((bf16[1,320,320]{2,1,0:T(8,128)(2,1)S(1)}, bf16[1,320,320]{2,1,0:T(8,128)(2,1)}, u32[]{:S(2)}) %copy-start.1) | copy-done | bytes 204824
  11.9 0.9 %copy-done.2 = bf16[1,320,320]{2,1,0:T(8,128)(2,1)S(1)} copy-done((bf16[1,320,320]{2,1,0:T(8,128)(2,1)S(1)}, bf16[1,320,320]{2,1,0:T(8,128)(2,1)}, u32[]{:S(2)}) %copy-start.2) | copy-done | bytes 204824
  12.8 0.9 %copy-done.3 = bf16[1,320,320]{2,1,0:T(8,128)(2,1)S(1)} copy-done((bf16[1,320,320]{2,1,0:T(8,128)(2,1)S(1)}, bf16[1,320,320]{2,1,0:T(8,128)(2,1)}, u32[]{:S(2)}) %copy-start.3) | copy-done | bytes 204824
  13.8 1.7 %shard_map.92.refs_1_.refs_3_.refs_6_ = bf16[960,320]{1,0:T(8,128)(2,1)S(1)} custom-call(s32[4]{0:T(128)S(1)} %pad_add_fusion.refs_0_, bf16[320,320]{1,0:T(8,128)(2,1)S(1)} %bitcast.12, bf16[320,320]{1,0:T(8,128)(2,1)S(1)} %bitcast.14, bf16[320,320]{1,0:T(8,128)(2,1)S(1)} %bitcast.16, bf16[320,320]{1,0:T(8,128)(2,1)S(1)} %collective-permute-done.2.refs_4_, ...), custom_call_target="tpu_custom_call" | custom-call | bytes 1048576 | tf_op jit(solution)/shard_map/pallas_call | solution.py:81
  15.6 1.6 %collective-permute-start.5 = (bf16[656,256]{1,0:T(8,128)(2,1)S(1)}, bf16[656,256]{1,0:T(8,128)(2,1)S(1)}, u32[]{:S(2)}, u32[]{:S(2)}) collective-permute-start(bf16[656,256]{1,0:T(8,128)(2,1)S(1)} %shard_map.93.refs_1_.refs_0_.refs_7_.refs_3_), channel_id=1, source_target_pairs={{0,2},{1,3},{2,0},{3,1},{4,6},{5,7},{6,4},{7,5},{8,10},{9,11},{10,... | collective-permute-start | bytes 1007624 | tf_op jit(solution)/shard_map/gather_0_2/ppermute | solution.py:32
  17.2 1.5 %collective-permute-start.6 = (bf16[656,256]{1,0:T(8,128)(2,1)S(1)}, bf16[656,256]{1,0:T(8,128)(2,1)S(1)}, u32[]{:S(2)}, u32[]{:S(2)}) collective-permute-start(bf16[656,256]{1,0:T(8,128)(2,1)S(1)} %shard_map.93.refs_1_.refs_0_.refs_7_.refs_3_), channel_id=1, source_target_pairs={{0,1},{1,0},{2,3},{3,2},{4,5},{5,4},{6,7},{7,6},{8,9},{9,8},{10,11... | collective-permute-start | bytes 1007624 | tf_op jit(solution)/shard_map/gather_0_1/ppermute | solution.py:32
  18.7 0.8 collective-permute-start.8
  19.6 5.9 %collective-permute-done.5.refs_0_.refs_2_ = bf16[656,256]{1,0:T(8,128)(2,1)S(1)} collective-permute-done((bf16[656,256]{1,0:T(8,128)(2,1)S(1)}, bf16[656,256]{1,0:T(8,128)(2,1)S(1)}, u32[]{:S(2)}, u32[]{:S(2)}) %collective-permute-start.5) | collective-permute-done | bytes 335904 | tf_op jit(solution)/shard_map/gather_0_2/ppermute | solution.py:32
  25.5 2.4 %collective-permute-done.6.refs_1_.refs_5_ = bf16[656,256]{1,0:T(8,128)(2,1)S(1)} collective-permute-done((bf16[656,256]{1,0:T(8,128)(2,1)S(1)}, bf16[656,256]{1,0:T(8,128)(2,1)S(1)}, u32[]{:S(2)}, u32[]{:S(2)}) %collective-permute-start.6) | collective-permute-done | bytes 335904 | tf_op jit(solution)/shard_map/gather_0_1/ppermute | solution.py:32
  28.0 1.6 %collective-permute-start.7 = (bf16[656,256]{1,0:T(8,128)(2,1)S(1)}, bf16[656,256]{1,0:T(8,128)(2,1)S(1)}, u32[]{:S(2)}, u32[]{:S(2)}) collective-permute-start(bf16[656,256]{1,0:T(8,128)(2,1)S(1)} %shard_map.94.refs_1_), channel_id=1, source_target_pairs={{0,1},{1,0},{2,3},{3,2},{4,5},{5,4},{6,7},{7,6},{8,9},{9,8},{10,11... | collective-permute-start | bytes 1007624 | tf_op jit(solution)/shard_map/gather_0_3/ppermute | solution.py:32
  30.3 2.1 %shard_map.96.refs_2_.refs_1_ = f32[960,320]{1,0:T(8,128)S(1)} custom-call(bf16[656,256]{1,0:T(8,128)(2,1)S(1)} %shard_map.93.refs_1_.refs_0_.refs_7_.refs_3_, bf16[656,256]{1,0:T(8,128)(2,1)S(1)} %collective-permute-done.6.refs_1_.refs_5_, bf16[656,256]{1,0:T(8,128)(2,1)S(1)} %collective-permute-done.5.refs_0_.refs_2_, ...), custom_call_target="tpu_custom_call" | custom-call | flops 1258291200 | bytes 1048576 | tf_op jit(solution)/shard_map/pallas_call | solution.py:81
  32.4 4.0 %collective-permute-done.14.refs_0_.refs_2_ = bf16[656,256]{1,0:T(8,128)(2,1)S(1)} collective-permute-done((bf16[656,256]{1,0:T(8,128)(2,1)S(1)}, bf16[656,256]{1,0:T(8,128)(2,1)S(1)}, u32[]{:S(2)}, u32[]{:S(2)}) %collective-permute-start.14) | collective-permute-done | bytes 335904 | tf_op jit(solution)/shard_map/gather_1_2/ppermute | solution.py:32
  36.4 1.3 %collective-permute-start.15 = (bf16[656,256]{1,0:T(8,128)(2,1)S(1)}, bf16[656,256]{1,0:T(8,128)(2,1)S(1)}, u32[]{:S(2)}, u32[]{:S(2)}) collective-permute-start(bf16[656,256]{1,0:T(8,128)(2,1)S(1)} %shard_map.100), channel_id=1, source_target_pairs={{0,1},{1,0},{2,3},{3,2},{4,5},{5,4},{6,7},{7,6},{8,9},{9,8},{10,11... | collective-permute-start | bytes 1007624 | tf_op jit(solution)/shard_map/gather_1_3/ppermute | solution.py:32
  37.7 1.0 %shard_map.97 = (bf16[320,384]{1,0:T(8,128)(2,1)S(1)}, bf16[320,384]{1,0:T(8,128)(2,1)S(1)}, bf16[320,384]{1,0:T(8,128)(2,1)S(1)}) custom-call(bf16[656,256]{1,0:T(8,128)(2,1)S(1)} %collective-permute-done.7.refs_0_.refs_6_, bf16[960,320]{1,0:T(8,128)(2,1)S(1)} %shard_map.92.refs_1_.refs_3_.refs_6_, f32[960,320]{1,0:T(8,128)S(1)} %shard_map.96.refs_2_.refs_1_), custom_call_target="tpu_custom_call" | custom-call | bytes 1048576 | tf_op jit(solution)/shard_map/pallas_call | solution.py:81
  38.7 4.8 %collective-permute-start.10 = (bf16[320,384]{1,0:T(8,128)(2,1)S(1)}, bf16[320,384]{1,0:T(8,128)(2,1)S(1)}, u32[]{:S(2)}, u32[]{:S(2)}) collective-permute-start(bf16[320,384]{1,0:T(8,128)(2,1)S(1)} %get-tuple-element.27.refs_1_), channel_id=1, source_target_pairs={{0,8},{1,9},{2,10},{3,11},{4,12},{5,13},{6,14},{7,15},{8,0},{9,1},... | collective-permute-start | bytes 737288 | tf_op jit(solution)/shard_map/swap_0/ppermute | solution.py:32
  44.7 3.8 %collective-permute-start.12 = (bf16[656,256]{1,0:T(8,128)(2,1)S(1)}, bf16[656,256]{1,0:T(8,128)(2,1)S(1)}, u32[]{:S(2)}, u32[]{:S(2)}) collective-permute-start(bf16[656,256]{1,0:T(8,128)(2,1)S(1)} %collective-permute-done.7.refs_0_.refs_6_), channel_id=1, source_target_pairs={{0,8},{1,9},{2,10},{3,11},{4,12},{5,13},{6,14},{7,15},{8,0},{9,1},... | collective-permute-start | bytes 1007624 | tf_op jit(solution)/shard_map/last_0/ppermute | solution.py:32
  48.6 4.1 %shard_map.98.refs_2_.refs_4_.refs_7_ = bf16[960,320]{1,0:T(8,128)(2,1)S(1)} custom-call(bf16[320,384]{1,0:T(8,128)(2,1)S(1)} %get-tuple-element.26.refs_0_, bf16[320,384]{1,0:T(8,128)(2,1)S(1)} %get-tuple-element.27.refs_1_, bf16[320,384]{1,0:T(8,128)(2,1)S(1)} %get-tuple-element.28.refs_2_, bf16[320,384]{1,0:T(8,128)(2,1)S(1)} %collective-permute-done.9.refs_3_, ...), custom_call_target="tpu_custom_call" | custom-call | flops 1769472000 | bytes 1048576 | tf_op jit(solution)/shard_map/pallas_call | solution.py:81
  52.7 2.8 %shard_map.103 = (bf16[320,384]{1,0:T(8,128)(2,1)S(1)}, bf16[320,384]{1,0:T(8,128)(2,1)S(1)}, bf16[320,384]{1,0:T(8,128)(2,1)S(1)}) custom-call(bf16[656,256]{1,0:T(8,128)(2,1)S(1)} %shard_map.99.refs_0_, bf16[656,256]{1,0:T(8,128)(2,1)S(1)} %collective-permute-done.13.refs_8_.refs_1_, bf16[656,256]{1,0:T(8,128)(2,1)S(1)} %collective-permute-done.14.refs_0_.refs_2_, ...), custom_call_target="tpu_custom_call" | custom-call | flops 1258291200 | bytes 1048576 | tf_op jit(solution)/shard_map/pallas_call | solution.py:81
  55.5 2.0 %collective-permute-start.21 = (bf16[320,384]{1,0:T(8,128)(2,1)S(1)}, bf16[320,384]{1,0:T(8,128)(2,1)S(1)}, u32[]{:S(2)}, u32[]{:S(2)}) collective-permute-start(bf16[320,384]{1,0:T(8,128)(2,1)S(1)} %get-tuple-element.35.refs_1_), channel_id=1, source_target_pairs={{0,8},{1,9},{2,10},{3,11},{4,12},{5,13},{6,14},{7,15},{8,0},{9,1},... | collective-permute-start | bytes 737288 | tf_op jit(solution)/shard_map/swap_1/ppermute | solution.py:32
  58.1 2.4 %shard_map.101 = (bf16[3,64,320]{2,1,0:T(8,128)(2,1)S(1)}, bf16[3,64,320]{2,1,0:T(8,128)(2,1)S(1)}, bf16[3,64,320]{2,1,0:T(8,128)(2,1)S(1)}, bf16[3,64,320]{2,1,0:T(8,128)(2,1)S(1)}, bf16[256,320]{1,0:T(8,128)(2,1)S(1)}) custom-call(s32[4]{0:T(128)S(1)} %pad_add_fusion.refs_0_, bf16[2,320,256]{2,1,0:T(8,128)(2,1)S(1)} %collective-permute-done.refs_8_.refs_1_, ...), custom_call_target="tpu_custom_call" | custom-call | flops 335544320 | bytes 1048576 | tf_op jit(solution)/shard_map/pallas_call | solution.py:81
  61.2 3.9 %collective-permute-start.18 = (bf16[3,64,320]{2,1,0:T(8,128)(2,1)S(1)}, bf16[3,64,320]{2,1,0:T(8,128)(2,1)S(1)}, u32[]{:S(2)}, u32[]{:S(2)}) collective-permute-start(bf16[3,64,320]{2,1,0:T(8,128)(2,1)S(1)} %get-tuple-element.30), channel_id=1, source_target_pairs={{0,8},{1,9},{2,10},{3,11},{4,16},{5,17},{6,18},{7,19},{8,12},{9,13... | collective-permute-start | bytes 368648 | tf_op jit(solution)/shard_map/spread_early_1/ppermute | solution.py:32
  65.1 1.5 %collective-permute-start.19 = (bf16[3,64,320]{2,1,0:T(8,128)(2,1)S(1)}, bf16[3,64,320]{2,1,0:T(8,128)(2,1)S(1)}, u32[]{:S(2)}, u32[]{:S(2)}) collective-permute-start(bf16[3,64,320]{2,1,0:T(8,128)(2,1)S(1)} %get-tuple-element.31), channel_id=1, source_target_pairs={{0,16},{1,17},{2,18},{3,19},{4,24},{5,25},{6,26},{7,27},{8,20},{9,... | collective-permute-start | bytes 368648 | tf_op jit(solution)/shard_map/spread_early_2/ppermute | solution.py:32
  66.7 5.1 %shard_map.104 = (bf16[64,320]{1,0:T(8,128)(2,1)S(1)}, bf16[64,320]{1,0:T(8,128)(2,1)S(1)}, bf16[64,320]{1,0:T(8,128)(2,1)S(1)}, bf16[64,320]{1,0:T(8,128)(2,1)S(1)}) custom-call(s32[4]{0:T(128)S(1)} %pad_add_fusion.refs_0_, bf16[320,384]{1,0:T(8,128)(2,1)S(1)} %get-tuple-element.35.refs_1_, bf16[320,384]{1,0:T(8,128)(2,1)S(1)} %get-tuple-element.36.refs_2_, ...), custom_call_target="tpu_custom_call" | custom-call | flops 1769472000 | bytes 1048576 | tf_op jit(solution)/shard_map/pallas_call | solution.py:81
  72.5 4.3 %collective-permute-start.25 = (bf16[64,320]{1,0:T(8,128)(2,1)S(1)}, bf16[64,320]{1,0:T(8,128)(2,1)S(1)}, u32[]{:S(2)}, u32[]{:S(2)}) collective-permute-start(bf16[64,320]{1,0:T(8,128)(2,1)S(1)} %get-tuple-element.40), channel_id=1, source_target_pairs={{0,8},{1,9},{2,10},{3,11},{4,16},{5,17},{6,18},{7,19},{8,12},{9,13... | collective-permute-start | bytes 122888 | tf_op jit(solution)/shard_map/spread_late_1/ppermute | solution.py:32
  77.5 1.1 %collective-permute-start.27 = (bf16[64,320]{1,0:T(8,128)(2,1)S(1)}, bf16[64,320]{1,0:T(8,128)(2,1)S(1)}, u32[]{:S(2)}, u32[]{:S(2)}) collective-permute-start(bf16[64,320]{1,0:T(8,128)(2,1)S(1)} %get-tuple-element.42), channel_id=1, source_target_pairs={{0,24},{1,25},{2,26},{3,27},{4,0},{5,1},{6,2},{7,3},{8,28},{9,29},... | collective-permute-start | bytes 122888 | tf_op jit(solution)/shard_map/spread_late_3/ppermute | solution.py:32
  79.2 1.1 %shard_map.102 = (f32[2,1,64,1280]{3,2,1,0:T(8,128)}, f32[64,1280]{1,0:T(8,128)S(1)}) custom-call(s32[1]{0:T(128)} %bitcast.refs_0_, f32[2,1280]{1,0:T(2,128)S(1)} %copy-done.4, bf16[3,64,320]{2,1,0:T(8,128)(2,1)S(1)} %collective-permute-done.17.refs_2_, bf16[3,64,320]{2,1,0:T(8,128)(2,1)S(1)} %collective-permute-done.18.refs_3_, ...), custom_call_target="tpu_custom_call" | custom-call | bytes 1048576 | tf_op jit(solution)/shard_map/pallas_call | solution.py:81
  80.3 2.0 %collective-permute-done.25.refs_5_ = bf16[64,320]{1,0:T(8,128)(2,1)S(1)} collective-permute-done((bf16[64,320]{1,0:T(8,128)(2,1)S(1)}, bf16[64,320]{1,0:T(8,128)(2,1)S(1)}, u32[]{:S(2)}, u32[]{:S(2)}) %collective-permute-start.25) | collective-permute-done | bytes 40992 | tf_op jit(solution)/shard_map/spread_late_1/ppermute | solution.py:32
  82.6 1.0 %shard_map.105 = f32[2,1,64,1280]{3,2,1,0:T(8,128)} custom-call(s32[1]{0:T(128)} %bitcast.refs_0_, f32[2,1280]{1,0:T(2,128)S(1)} %copy-done.4, f32[2,1,64,1280]{3,2,1,0:T(8,128)} %get-tuple-element.33.refs_2_, f32[64,1280]{1,0:T(8,128)S(1)} %get-tuple-element.34.refs_3_, ...), custom_call_target="tpu_custom_call", output_to_operand_aliasing={{}: (2, {})} | custom-call | bytes 1048576 | tf_op jit(solution)/shard_map/pallas_call | solution.py:81
  (52 shorter events, 6.9 us)
Async XLA Ops:
  2.7 12.8 %collective-permute-start.1 = (bf16[656,256]{1,0:T(8,128)(2,1)}, bf16[656,256]{1,0:T(8,128)(2,1)S(1)}, u32[]{:S(2)}, u32[]{:S(2)}) collective-permute-start(bf16[656,256]{1,0:T(8,128)(2,1)} %get-tuple-element.24), channel_id=1, source_target_pairs={{0,0},{1,1},{2,2},{3,3},{4,8},{5,9},{6,10},{7,11},{8,4},{9,5},{10,... | collective-permute-start | bytes 1007624 | tf_op jit(solution)/shard_map/regroup_0/ppermute | solution.py:32
  4.4 5.8 %collective-permute-start.2 = (bf16[320,320]{1,0:T(8,128)(2,1)}, bf16[320,320]{1,0:T(8,128)(2,1)S(1)}, u32[]{:S(2)}, u32[]{:S(2)}) collective-permute-start(bf16[320,320]{1,0:T(8,128)(2,1)} %bitcast.11), channel_id=1, source_target_pairs={{0,8},{1,9},{2,10},{3,11},{4,12},{5,13},{6,14},{7,15},{8,0},{9,1},... | collective-permute-start | bytes 614408 | tf_op jit(solution)/shard_map/lend_0/ppermute | solution.py:32
  8.9 1.7 %collective-permute-start.3 = (bf16[320,320]{1,0:T(8,128)(2,1)}, bf16[320,320]{1,0:T(8,128)(2,1)S(1)}, u32[]{:S(2)}, u32[]{:S(2)}) collective-permute-start(bf16[320,320]{1,0:T(8,128)(2,1)} %bitcast.13), channel_id=1, source_target_pairs={{0,8},{1,9},{2,10},{3,11},{4,12},{5,13},{6,14},{7,15},{8,0},{9,1},... | collective-permute-start | bytes 614408 | tf_op jit(solution)/shard_map/lend_1/ppermute | solution.py:32
  8.9 2.0 %collective-permute-start.4 = (bf16[320,320]{1,0:T(8,128)(2,1)}, bf16[320,320]{1,0:T(8,128)(2,1)S(1)}, u32[]{:S(2)}, u32[]{:S(2)}) collective-permute-start(bf16[320,320]{1,0:T(8,128)(2,1)} %bitcast.15), channel_id=1, source_target_pairs={{0,8},{1,9},{2,10},{3,11},{4,12},{5,13},{6,14},{7,15},{8,0},{9,1},... | collective-permute-start | bytes 614408 | tf_op jit(solution)/shard_map/lend_2/ppermute | solution.py:32
  9.4 9.3 %copy-start = (bf16[656,256]{1,0:T(8,128)(2,1)S(1)}, bf16[656,256]{1,0:T(8,128)(2,1)}, u32[]{:S(2)}) copy-start(bf16[656,256]{1,0:T(8,128)(2,1)} %get-tuple-element.25.refs_0_) | copy-start | bytes 1007620
  10.9 0.9 %copy-start.1 = (bf16[1,320,320]{2,1,0:T(8,128)(2,1)S(1)}, bf16[1,320,320]{2,1,0:T(8,128)(2,1)}, u32[]{:S(2)}) copy-start(bf16[1,320,320]{2,1,0:T(8,128)(2,1)} %param.13) | copy-start | bytes 614404
  15.6 9.9 %collective-permute-start.5 = (bf16[656,256]{1,0:T(8,128)(2,1)S(1)}, bf16[656,256]{1,0:T(8,128)(2,1)S(1)}, u32[]{:S(2)}, u32[]{:S(2)}) collective-permute-start(bf16[656,256]{1,0:T(8,128)(2,1)S(1)} %shard_map.93.refs_1_.refs_0_.refs_7_.refs_3_), channel_id=1, source_target_pairs={{0,2},{1,3},{2,0},{3,1},{4,6},{5,7},{6,4},{7,5},{8,10},{9,11},{10,... | collective-permute-start | bytes 1007624 | tf_op jit(solution)/shard_map/gather_0_2/ppermute | solution.py:32
  17.2 10.7 %collective-permute-start.6 = (bf16[656,256]{1,0:T(8,128)(2,1)S(1)}, bf16[656,256]{1,0:T(8,128)(2,1)S(1)}, u32[]{:S(2)}, u32[]{:S(2)}) collective-permute-start(bf16[656,256]{1,0:T(8,128)(2,1)S(1)} %shard_map.93.refs_1_.refs_0_.refs_7_.refs_3_), channel_id=1, source_target_pairs={{0,1},{1,0},{2,3},{3,2},{4,5},{5,4},{6,7},{7,6},{8,9},{9,8},{10,11... | collective-permute-start | bytes 1007624 | tf_op jit(solution)/shard_map/gather_0_1/ppermute | solution.py:32
  18.7 10.9 %copy-start.5 = (bf16[2,256,320]{1,2,0:T(8,128)(2,1)S(1)}, bf16[2,256,320]{1,2,0:T(8,128)(2,1)}, u32[]{:S(2)}) copy-start(bf16[2,256,320]{1,2,0:T(8,128)(2,1)} %param.9) | copy-start | bytes 983044
  18.7 9.1 %collective-permute-start.8 = (bf16[656,256]{1,0:T(8,128)(2,1)S(1)}, bf16[656,256]{1,0:T(8,128)(2,1)S(1)}, u32[]{:S(2)}, u32[]{:S(2)}) collective-permute-start(bf16[656,256]{1,0:T(8,128)(2,1)S(1)} %shard_map.95), channel_id=1, source_target_pairs={{0,0},{1,1},{2,2},{3,3},{4,8},{5,9},{6,10},{7,11},{8,4},{9,5},{10,... | collective-permute-start | bytes 1007624 | tf_op jit(solution)/shard_map/regroup_1/ppermute | solution.py:32
  27.9 8.4 %collective-permute-start.14 = (bf16[656,256]{1,0:T(8,128)(2,1)S(1)}, bf16[656,256]{1,0:T(8,128)(2,1)S(1)}, u32[]{:S(2)}, u32[]{:S(2)}) collective-permute-start(bf16[656,256]{1,0:T(8,128)(2,1)S(1)} %shard_map.99.refs_0_), channel_id=1, source_target_pairs={{0,2},{1,3},{2,0},{3,1},{4,6},{5,7},{6,4},{7,5},{8,10},{9,11},{10,... | collective-permute-start | bytes 1007624 | tf_op jit(solution)/shard_map/gather_1_2/ppermute | solution.py:32
  28.0 9.7 %collective-permute-start.7 = (bf16[656,256]{1,0:T(8,128)(2,1)S(1)}, bf16[656,256]{1,0:T(8,128)(2,1)S(1)}, u32[]{:S(2)}, u32[]{:S(2)}) collective-permute-start(bf16[656,256]{1,0:T(8,128)(2,1)S(1)} %shard_map.94.refs_1_), channel_id=1, source_target_pairs={{0,1},{1,0},{2,3},{3,2},{4,5},{5,4},{6,7},{7,6},{8,9},{9,8},{10,11... | collective-permute-start | bytes 1007624 | tf_op jit(solution)/shard_map/gather_0_3/ppermute | solution.py:32
  29.6 14.5 %collective-permute-start = (bf16[2,320,256]{2,1,0:T(8,128)(2,1)S(1)}, bf16[2,320,256]{2,1,0:T(8,128)(2,1)S(1)}, u32[]{:S(2)}, u32[]{:S(2)}) collective-permute-start(bf16[2,320,256]{2,1,0:T(8,128)(2,1)S(1)} %bitcast.19), channel_id=1, source_target_pairs={{0,0},{1,1},{2,2},{3,3},{4,8},{5,9},{6,10},{7,11},{8,4},{9,5},{10,... | collective-permute-start | bytes 983048 | tf_op jit(solution)/shard_map/regroup_queries/ppermute | solution.py:32
  36.4 12.2 %collective-permute-start.15 = (bf16[656,256]{1,0:T(8,128)(2,1)S(1)}, bf16[656,256]{1,0:T(8,128)(2,1)S(1)}, u32[]{:S(2)}, u32[]{:S(2)}) collective-permute-start(bf16[656,256]{1,0:T(8,128)(2,1)S(1)} %shard_map.100), channel_id=1, source_target_pairs={{0,1},{1,0},{2,3},{3,2},{4,5},{5,4},{6,7},{7,6},{8,9},{9,8},{10,11... | collective-permute-start | bytes 1007624 | tf_op jit(solution)/shard_map/gather_1_3/ppermute | solution.py:32
  38.7 6.0 %collective-permute-start.10 = (bf16[320,384]{1,0:T(8,128)(2,1)S(1)}, bf16[320,384]{1,0:T(8,128)(2,1)S(1)}, u32[]{:S(2)}, u32[]{:S(2)}) collective-permute-start(bf16[320,384]{1,0:T(8,128)(2,1)S(1)} %get-tuple-element.27.refs_1_), channel_id=1, source_target_pairs={{0,8},{1,9},{2,10},{3,11},{4,12},{5,13},{6,14},{7,15},{8,0},{9,1},... | collective-permute-start | bytes 737288 | tf_op jit(solution)/shard_map/swap_0/ppermute | solution.py:32
  43.6 5.0 %collective-permute-start.11 = (bf16[320,384]{1,0:T(8,128)(2,1)S(1)}, bf16[320,384]{1,0:T(8,128)(2,1)S(1)}, u32[]{:S(2)}, u32[]{:S(2)}) collective-permute-start(bf16[320,384]{1,0:T(8,128)(2,1)S(1)} %get-tuple-element.28.refs_2_), channel_id=1, source_target_pairs={{0,8},{1,9},{2,10},{3,11},{4,12},{5,13},{6,14},{7,15},{8,0},{9,1},... | collective-permute-start | bytes 737288 | tf_op jit(solution)/shard_map/swap_0/ppermute | solution.py:32
  43.6 5.0 %collective-permute-start.9 = (bf16[320,384]{1,0:T(8,128)(2,1)S(1)}, bf16[320,384]{1,0:T(8,128)(2,1)S(1)}, u32[]{:S(2)}, u32[]{:S(2)}) collective-permute-start(bf16[320,384]{1,0:T(8,128)(2,1)S(1)} %get-tuple-element.26.refs_0_), channel_id=1, source_target_pairs={{0,8},{1,9},{2,10},{3,11},{4,12},{5,13},{6,14},{7,15},{8,0},{9,1},... | collective-permute-start | bytes 737288 | tf_op jit(solution)/shard_map/swap_0/ppermute | solution.py:32
  44.1 8.6 %collective-permute-start.13 = (bf16[656,256]{1,0:T(8,128)(2,1)S(1)}, bf16[656,256]{1,0:T(8,128)(2,1)S(1)}, u32[]{:S(2)}, u32[]{:S(2)}) collective-permute-start(bf16[656,256]{1,0:T(8,128)(2,1)S(1)} %shard_map.99.refs_0_), channel_id=1, source_target_pairs={{0,1},{1,0},{2,3},{3,2},{4,5},{5,4},{6,7},{7,6},{8,9},{9,8},{10,11... | collective-permute-start | bytes 1007624 | tf_op jit(solution)/shard_map/gather_1_1/ppermute | solution.py:32
  44.7 13.4 %collective-permute-start.12 = (bf16[656,256]{1,0:T(8,128)(2,1)S(1)}, bf16[656,256]{1,0:T(8,128)(2,1)S(1)}, u32[]{:S(2)}, u32[]{:S(2)}) collective-permute-start(bf16[656,256]{1,0:T(8,128)(2,1)S(1)} %collective-permute-done.7.refs_0_.refs_6_), channel_id=1, source_target_pairs={{0,8},{1,9},{2,10},{3,11},{4,12},{5,13},{6,14},{7,15},{8,0},{9,1},... | collective-permute-start | bytes 1007624 | tf_op jit(solution)/shard_map/last_0/ppermute | solution.py:32
  48.5 9.6 %collective-permute-start.16 = (bf16[656,256]{1,0:T(8,128)(2,1)S(1)}, bf16[656,256]{1,0:T(8,128)(2,1)S(1)}, u32[]{:S(2)}, u32[]{:S(2)}) collective-permute-start(bf16[656,256]{1,0:T(8,128)(2,1)S(1)} %collective-permute-done.15.refs_9_.refs_3_), channel_id=1, source_target_pairs={{0,8},{1,9},{2,10},{3,11},{4,12},{5,13},{6,14},{7,15},{8,0},{9,1},... | collective-permute-start | bytes 1007624 | tf_op jit(solution)/shard_map/last_1/ppermute | solution.py:32
  55.5 9.6 %collective-permute-start.21 = (bf16[320,384]{1,0:T(8,128)(2,1)S(1)}, bf16[320,384]{1,0:T(8,128)(2,1)S(1)}, u32[]{:S(2)}, u32[]{:S(2)}) collective-permute-start(bf16[320,384]{1,0:T(8,128)(2,1)S(1)} %get-tuple-element.35.refs_1_), channel_id=1, source_target_pairs={{0,8},{1,9},{2,10},{3,11},{4,12},{5,13},{6,14},{7,15},{8,0},{9,1},... | collective-permute-start | bytes 737288 | tf_op jit(solution)/shard_map/swap_1/ppermute | solution.py:32
  57.6 9.1 %collective-permute-start.22 = (bf16[320,384]{1,0:T(8,128)(2,1)S(1)}, bf16[320,384]{1,0:T(8,128)(2,1)S(1)}, u32[]{:S(2)}, u32[]{:S(2)}) collective-permute-start(bf16[320,384]{1,0:T(8,128)(2,1)S(1)} %get-tuple-element.36.refs_2_), channel_id=1, source_target_pairs={{0,8},{1,9},{2,10},{3,11},{4,12},{5,13},{6,14},{7,15},{8,0},{9,1},... | collective-permute-start | bytes 737288 | tf_op jit(solution)/shard_map/swap_1/ppermute | solution.py:32
  57.6 9.0 %collective-permute-start.23 = (bf16[320,384]{1,0:T(8,128)(2,1)S(1)}, bf16[320,384]{1,0:T(8,128)(2,1)S(1)}, u32[]{:S(2)}, u32[]{:S(2)}) collective-permute-start(bf16[320,384]{1,0:T(8,128)(2,1)S(1)} %get-tuple-element.37.refs_3_), channel_id=1, source_target_pairs={{0,8},{1,9},{2,10},{3,11},{4,12},{5,13},{6,14},{7,15},{8,0},{9,1},... | collective-permute-start | bytes 737288 | tf_op jit(solution)/shard_map/swap_1/ppermute | solution.py:32
  60.5 11.9 %collective-permute-start.17 = (bf16[3,64,320]{2,1,0:T(8,128)(2,1)S(1)}, bf16[3,64,320]{2,1,0:T(8,128)(2,1)S(1)}, u32[]{:S(2)}, u32[]{:S(2)}) collective-permute-start(bf16[3,64,320]{2,1,0:T(8,128)(2,1)S(1)} %get-tuple-element.29), channel_id=1, source_target_pairs={{0,0},{1,1},{2,2},{3,3},{4,8},{5,9},{6,10},{7,11},{8,4},{9,5},{10,... | collective-permute-start | bytes 368648 | tf_op jit(solution)/shard_map/spread_early_0/ppermute | solution.py:32
  61.2 15.8 %collective-permute-start.18 = (bf16[3,64,320]{2,1,0:T(8,128)(2,1)S(1)}, bf16[3,64,320]{2,1,0:T(8,128)(2,1)S(1)}, u32[]{:S(2)}, u32[]{:S(2)}) collective-permute-start(bf16[3,64,320]{2,1,0:T(8,128)(2,1)S(1)} %get-tuple-element.30), channel_id=1, source_target_pairs={{0,8},{1,9},{2,10},{3,11},{4,16},{5,17},{6,18},{7,19},{8,12},{9,13... | collective-permute-start | bytes 368648 | tf_op jit(solution)/shard_map/spread_early_1/ppermute | solution.py:32
  65.1 12.4 %collective-permute-start.19 = (bf16[3,64,320]{2,1,0:T(8,128)(2,1)S(1)}, bf16[3,64,320]{2,1,0:T(8,128)(2,1)S(1)}, u32[]{:S(2)}, u32[]{:S(2)}) collective-permute-start(bf16[3,64,320]{2,1,0:T(8,128)(2,1)S(1)} %get-tuple-element.31), channel_id=1, source_target_pairs={{0,16},{1,17},{2,18},{3,19},{4,24},{5,25},{6,26},{7,27},{8,20},{9,... | collective-permute-start | bytes 368648 | tf_op jit(solution)/shard_map/spread_early_2/ppermute | solution.py:32
  66.6 12.6 %collective-permute-start.20 = (bf16[3,64,320]{2,1,0:T(8,128)(2,1)S(1)}, bf16[3,64,320]{2,1,0:T(8,128)(2,1)S(1)}, u32[]{:S(2)}, u32[]{:S(2)}) collective-permute-start(bf16[3,64,320]{2,1,0:T(8,128)(2,1)S(1)} %get-tuple-element.32), channel_id=1, source_target_pairs={{0,24},{1,25},{2,26},{3,27},{4,0},{5,1},{6,2},{7,3},{8,28},{9,29},... | collective-permute-start | bytes 368648 | tf_op jit(solution)/shard_map/spread_early_3/ppermute | solution.py:32
  66.6 12.6 %copy-start.4 = (f32[2,1280]{1,0:T(2,128)S(1)}, f32[2,1280]{1,0:T(2,128)}, u32[]{:S(2)}) copy-start(f32[2,1280]{1,0:T(2,128)} %refs_1_.3) | copy-start | bytes 30724
  71.8 8.5 %collective-permute-start.24 = (bf16[64,320]{1,0:T(8,128)(2,1)S(1)}, bf16[64,320]{1,0:T(8,128)(2,1)S(1)}, u32[]{:S(2)}, u32[]{:S(2)}) collective-permute-start(bf16[64,320]{1,0:T(8,128)(2,1)S(1)} %get-tuple-element.39), channel_id=1, source_target_pairs={{0,0},{1,1},{2,2},{3,3},{4,8},{5,9},{6,10},{7,11},{8,4},{9,5},{10,... | collective-permute-start | bytes 122888 | tf_op jit(solution)/shard_map/spread_late_0/ppermute | solution.py:32
  72.5 9.9 %collective-permute-start.25 = (bf16[64,320]{1,0:T(8,128)(2,1)S(1)}, bf16[64,320]{1,0:T(8,128)(2,1)S(1)}, u32[]{:S(2)}, u32[]{:S(2)}) collective-permute-start(bf16[64,320]{1,0:T(8,128)(2,1)S(1)} %get-tuple-element.40), channel_id=1, source_target_pairs={{0,8},{1,9},{2,10},{3,11},{4,16},{5,17},{6,18},{7,19},{8,12},{9,13... | collective-permute-start | bytes 122888 | tf_op jit(solution)/shard_map/spread_late_1/ppermute | solution.py:32
  77.0 5.4 %collective-permute-start.26 = (bf16[64,320]{1,0:T(8,128)(2,1)S(1)}, bf16[64,320]{1,0:T(8,128)(2,1)S(1)}, u32[]{:S(2)}, u32[]{:S(2)}) collective-permute-start(bf16[64,320]{1,0:T(8,128)(2,1)S(1)} %get-tuple-element.41), channel_id=1, source_target_pairs={{0,16},{1,17},{2,18},{3,19},{4,24},{5,25},{6,26},{7,27},{8,20},{9,... | collective-permute-start | bytes 122888 | tf_op jit(solution)/shard_map/spread_late_2/ppermute | solution.py:32
  77.5 5.1 %collective-permute-start.27 = (bf16[64,320]{1,0:T(8,128)(2,1)S(1)}, bf16[64,320]{1,0:T(8,128)(2,1)S(1)}, u32[]{:S(2)}, u32[]{:S(2)}) collective-permute-start(bf16[64,320]{1,0:T(8,128)(2,1)S(1)} %get-tuple-element.42), channel_id=1, source_target_pairs={{0,24},{1,25},{2,26},{3,27},{4,0},{5,1},{6,2},{7,3},{8,28},{9,29},... | collective-permute-start | bytes 122888 | tf_op jit(solution)/shard_map/spread_late_3/ppermute | solution.py:32
  (2 other events, 1.9 us)
